TPU v7x, 32 devices: a whole 2x2x4 slice. The times are simulated.
32 devices in a mesh: ctx: 4 (over z), fsdp: 8 (over y, x, core).
Axes of the slice: x: 2, y: 2, z: 4, core: 2. Of those that a mesh axis runs over, the one named last changes fastest.
Arguments:
- activations: bfloat16 [8, 2, 1024, 2560], P('fsdp', None, 'ctx'), may hold values from -6 to 6
- cotangent: bfloat16 [8, 2, 1024, 2560], P('fsdp', None, 'ctx'), may hold values from -6 to 6
- seq_length: int32 [8, 2], P('fsdp'), may hold values from 513 to 1024
- block_order: int32 [8], replicated, may hold values from 0 to 7, each once
- attn_norm: bfloat16 [2560], P('fsdp'), may hold values from 0.5 to 1.5
- query_down: bfloat16 [2560, 768], P('fsdp'), may hold values from -0.125 to 0.125
- query_norm: bfloat16 [768], P('fsdp'), may hold values from 0.5 to 1.5
- query_up: bfloat16 [768, 3840], P('fsdp'), may hold values from -0.21875 to 0.21875
- latent_down: bfloat16 [2560, 288], P('fsdp'), may hold values from -0.125 to 0.125
- latent_norm: bfloat16 [256], P('fsdp'), may hold values from 0.5 to 1.5
- latent_up: bfloat16 [256, 5120], P('fsdp'), may hold values from -0.375 to 0.375
- attn_out: bfloat16 [2560, 2560], P('fsdp'), may hold values from -4 to 4
- mlp_norm: bfloat16 [2560], P('fsdp'), may hold values from 0.5 to 1.5
- gate_weight: bfloat16 [6400, 2560], P('fsdp'), may hold values from -0.125 to 0.125
- up_weight: bfloat16 [6400, 2560], P('fsdp'), may hold values from -0.125 to 0.125
- down_weight: bfloat16 [6400, 2560], P('fsdp'), may hold values from -0.875 to 0.875
Outputs:
- output: bfloat16 [8, 2, 1024, 2560], P('fsdp', None, 'ctx')
- input_grad: bfloat16 [8, 2, 1024, 2560], P('fsdp', None, 'ctx')
- attn_norm_grad: float32 [2560], P('fsdp')
- query_down_grad: float32 [2560, 768], P('fsdp')
- query_norm_grad: float32 [768], P('fsdp')
- query_up_grad: float32 [768, 3840], P('fsdp')
- latent_down_grad: float32 [2560, 288], P('fsdp')
- latent_norm_grad: float32 [256], P('fsdp')
- latent_up_grad: float32 [256, 5120], P('fsdp')
- attn_out_grad: float32 [2560, 2560], P('fsdp')
- mlp_norm_grad: float32 [2560], P('fsdp')
- gate_weight_grad: float32 [6400, 2560], P('fsdp')
- up_weight_grad: float32 [6400, 2560], P('fsdp')
- down_weight_grad: float32 [6400, 2560], P('fsdp')
All inputs are finite; a program needn't handle non-finite values.
Results may differ from a plain program's by a relative error of at most 0.024.
Values may be sent and summed in bfloat16 or wider, within the bound.
No kernel may reach another device: no remote copies, remote signals or barrier semaphores. Data moves between devices by JAX's collectives and lax.ppermute only.
A program may use at most 576 MiB of HBM per device.

v0:
```python
import math

import jax
import jax.numpy as jnp
from jax import lax
from jax.sharding import PartitionSpec as P

H = 40
DN = 64
DR = 32
DV = 64
KVR = 256


branch_scale = 1.4 / math.sqrt(62.0)
norm_eps = 1e-05
rope_base = 10000.0
lowest_score = -1e30


def rms_scale(values, gain):
    inverse = lax.rsqrt(jnp.mean(values * values, axis=-1, keepdims=True) + norm_eps)
    plain = values * inverse
    return (plain * gain, plain, inverse)


def rms_back(grad_out, plain, inverse, gain):
    gain_grad = jnp.sum(grad_out * plain, axis=0)
    scaled = grad_out * gain
    values_grad = inverse * (scaled - plain * jnp.mean(scaled * plain, axis=-1, keepdims=True))
    return (values_grad, gain_grad)


def rope_tables(positions, width):
    half = width // 2
    freq = rope_base ** (-(jnp.arange(half, dtype=jnp.float32) * 2.0 / width))
    angle = positions.astype(jnp.float32)[:, None] * freq[None, :]
    return (
        jnp.concatenate([jnp.cos(angle), jnp.cos(angle)], axis=-1),
        jnp.concatenate([jnp.sin(angle), jnp.sin(angle)], axis=-1),
    )


def turn_half(values):
    half = values.shape[-1] // 2
    return jnp.concatenate([-values[..., half:], values[..., :half]], axis=-1)


def turn_back(values):
    half = values.shape[-1] // 2
    return jnp.concatenate([values[..., half:], -values[..., :half]], axis=-1)


def rope_apply(values, cosine, sine):
    return values * cosine + turn_half(values) * sine


def rope_back(grads, cosine, sine):
    return grads * cosine + turn_back(grads * sine)


def matmul_plain(left, right):
    return jnp.dot(left, right, preferred_element_type=jnp.float32)


def matmul_left(left, right):
    return lax.dot_general(
        left, right, (((0,), (0,)), ((), ())), preferred_element_type=jnp.float32
    )


def matmul_right(left, right):
    return lax.dot_general(
        left, right, (((1,), (1,)), ((), ())), preferred_element_type=jnp.float32
    )


def split_pair(values):
    grad_high = values.astype(jnp.bfloat16)
    grad_rest = (values - grad_high.astype(jnp.float32)).astype(jnp.bfloat16)
    return (grad_high, grad_rest)


def latent_products(latent_rows, expanded_grad, up_weights):
    grad_high, grad_rest = split_pair(expanded_grad)
    up_part = matmul_left(latent_rows, grad_high) + matmul_left(latent_rows, grad_rest)
    latent_grad = matmul_right(grad_high, up_weights) + matmul_right(grad_rest, up_weights)
    return (up_part, latent_grad)


def feed_forward(rows_in, grad_in, gate_piece, up_piece, down_piece):
    gate_value = matmul_right(rows_in, gate_piece)
    up_value = matmul_right(rows_in, up_piece)
    sigmoid_gate = jax.nn.sigmoid(gate_value)
    silu_gate = gate_value * sigmoid_gate
    hidden_low = (silu_gate * up_value).astype(jnp.bfloat16)
    branch_part = matmul_plain(hidden_low, down_piece)
    hidden_grad = matmul_right(grad_in, down_piece)
    gate_grad = (
        hidden_grad * up_value * sigmoid_gate * (1.0 + gate_value * (1.0 - sigmoid_gate))
    ).astype(jnp.bfloat16)
    up_grad = (hidden_grad * silu_gate).astype(jnp.bfloat16)
    rows_grad = matmul_plain(gate_grad, gate_piece) + matmul_plain(up_grad, up_piece)
    return (branch_part, rows_grad, gate_grad, up_grad, hidden_low)


def body(
    activations,
    cotangent,
    seq_length,
    block_order,
    attn_norm,
    query_down,
    query_norm,
    query_up,
    latent_down,
    latent_norm,
    latent_up,
    attn_out,
    mlp_norm,
    gate_weight,
    up_weight,
    down_weight,
):
    ctx_count = lax.axis_size("ctx")
    ctx_place = lax.axis_index("ctx")
    batches = activations.shape[1]
    local_rows = activations.shape[2]
    seq_rows = local_rows * ctx_count
    blocks = block_order.shape[0]
    block_size = seq_rows // blocks
    score_scale = (DN + DR) ** (-0.5)
    every_row = jnp.arange(seq_rows, dtype=jnp.int32)
    block_of = every_row // block_size
    placed = jnp.sum(
        jnp.where(
            block_of[:, None] == jnp.arange(blocks, dtype=jnp.int32)[None, :],
            block_order[None, :],
            0,
        ),
        axis=1,
    )
    key_pos = placed * block_size + every_row % block_size
    query_pos = lax.dynamic_slice_in_dim(key_pos, ctx_place * local_rows, local_rows)
    local_cos, local_sin = rope_tables(query_pos, DR)
    head_cos = local_cos[:, None, :]
    head_sin = local_sin[:, None, :]
    sums = [
        jnp.zeros(weight.shape, jnp.float32)
        for weight in (
            attn_norm,
            query_down,
            query_norm,
            query_up,
            latent_down,
            latent_norm,
            latent_up,
            attn_out,
            mlp_norm,
            gate_weight,
            up_weight,
            down_weight,
        )
    ]
    attn_sums = None
    outputs = []
    input_grads = []
    for batch in range(batches):
        (
            full_attn_norm,
            full_query_down,
            full_query_norm,
            full_query_up,
            full_latent_down,
            full_latent_norm,
            full_latent_up,
            full_attn_out,
            full_mlp_norm,
        ) = (
            lax.all_gather(attn_norm, "fsdp", axis=0, tiled=True),
            lax.all_gather(query_down, "fsdp", axis=0, tiled=True),
            lax.all_gather(query_norm, "fsdp", axis=0, tiled=True),
            lax.all_gather(query_up, "fsdp", axis=0, tiled=True),
            lax.all_gather(latent_down, "fsdp", axis=0, tiled=True),
            lax.all_gather(latent_norm, "fsdp", axis=0, tiled=True),
            lax.all_gather(latent_up, "fsdp", axis=0, tiled=True),
            lax.all_gather(attn_out, "fsdp", axis=0, tiled=True),
            lax.all_gather(mlp_norm, "fsdp", axis=0, tiled=True),
        )
        attn_gain = full_attn_norm.astype(jnp.float32)
        query_gain = full_query_norm.astype(jnp.float32)
        latent_gain = full_latent_norm.astype(jnp.float32)
        mlp_gain = full_mlp_norm.astype(jnp.float32)
        inputs = activations[0, batch].astype(jnp.float32)
        length = seq_length[0, batch]
        live = (query_pos < length).astype(jnp.float32)[:, None]
        out_grad = cotangent[0, batch].astype(jnp.float32) * live
        first_normed, first_plain, first_inverse = rms_scale(inputs, attn_gain)
        first_low = first_normed.astype(jnp.bfloat16)
        query_latent = matmul_plain(first_low, full_query_down)
        query_mixed, query_plain, query_inverse = rms_scale(query_latent, query_gain)
        query_low = query_mixed.astype(jnp.bfloat16)
        query_raw = matmul_plain(query_low, full_query_up).reshape(local_rows, H, DN + DR)
        query_turned = jnp.concatenate(
            [query_raw[..., :DN], rope_apply(query_raw[..., DN:], head_cos, head_sin)], axis=-1
        ).astype(jnp.bfloat16)
        query_nope = query_turned[..., :DN]
        query_rope = query_turned[..., DN:]
        latent_raw = matmul_plain(first_low, full_latent_down)
        latent_mixed, latent_plain, latent_inverse = rms_scale(latent_raw[:, :KVR], latent_gain)
        latent_low = latent_mixed.astype(jnp.bfloat16)
        key_rope_low = rope_apply(latent_raw[:, KVR:], local_cos, local_sin).astype(jnp.bfloat16)
        latent_all, key_rope_all = (
            lax.all_gather(latent_low, "ctx", axis=0, tiled=True),
            lax.all_gather(key_rope_low, "ctx", axis=0, tiled=True),
        )
        expanded = matmul_plain(latent_all, full_latent_up).astype(jnp.bfloat16)
        expanded = expanded.reshape(seq_rows, H, DN + DV)
        key_nope = expanded[..., :DN]
        value_rows = expanded[..., DN:]
        allowed = (key_pos[None, :] <= query_pos[:, None]) & (key_pos[None, :] < length)
        raw_scores = (
            jnp.einsum("ihd,jhd->hij", query_nope, key_nope, preferred_element_type=jnp.float32)
            + jnp.einsum(
                "ihd,jd->hij", query_rope, key_rope_all, preferred_element_type=jnp.float32
            )
        ) * score_scale
        masked = jnp.where(allowed[None], raw_scores, lowest_score)
        row_top = jnp.max(masked, axis=-1, keepdims=True)
        expo = jnp.exp(masked - row_top)
        row_total = jnp.sum(expo, axis=-1, keepdims=True)
        log_total = row_top + jnp.log(row_total)
        probs_low = (expo / row_total).astype(jnp.bfloat16)
        mixed = (
            jnp.einsum("hij,jhd->ihd", probs_low, value_rows, preferred_element_type=jnp.float32)
            .reshape(local_rows, H * DV)
            .astype(jnp.bfloat16)
        )
        attn_branch = matmul_plain(mixed, full_attn_out)
        resid = inputs + branch_scale * attn_branch
        second_normed, second_plain, second_inverse = rms_scale(resid, mlp_gain)
        second_low = second_normed.astype(jnp.bfloat16)
        branch_grad = (branch_scale * out_grad).astype(jnp.bfloat16)
        rows_all, grads_all = (
            lax.all_gather(second_low, "fsdp", axis=0, tiled=True),
            lax.all_gather(branch_grad, "fsdp", axis=0, tiled=True),
        )
        parts = feed_forward(rows_all, grads_all, gate_weight, up_weight, down_weight)
        ffn_out, second_grad = (
            lax.psum_scatter(parts[0], "fsdp", scatter_dimension=0, tiled=True),
            lax.psum_scatter(parts[1], "fsdp", scatter_dimension=0, tiled=True),
        )
        sums[9] = sums[9] + matmul_left(parts[2], rows_all)
        sums[10] = sums[10] + matmul_left(parts[3], rows_all)
        sums[11] = sums[11] + matmul_left(parts[4], grads_all)
        outputs.append((resid + branch_scale * ffn_out).astype(jnp.bfloat16))
        second_back, mlp_gain_grad = rms_back(second_grad, second_plain, second_inverse, mlp_gain)
        resid_grad = out_grad + second_back
        attn_grad = (branch_scale * resid_grad).astype(jnp.bfloat16)
        attn_out_part = matmul_left(mixed, attn_grad)
        mixed_grad = (
            matmul_right(attn_grad, full_attn_out).astype(jnp.bfloat16).reshape(local_rows, H, DV)
        )
        probs = jnp.exp(masked - log_total)
        prob_grad = jnp.einsum(
            "ihd,jhd->hij", mixed_grad, value_rows, preferred_element_type=jnp.float32
        )
        row_dot = jnp.sum(probs * prob_grad, axis=-1, keepdims=True)
        score_grad = (probs * (prob_grad - row_dot)).astype(jnp.bfloat16)
        query_nope_grad = (
            jnp.einsum("hij,jhd->ihd", score_grad, key_nope, preferred_element_type=jnp.float32)
            * score_scale
        )
        query_rope_grad = (
            jnp.einsum("hij,jd->ihd", score_grad, key_rope_all, preferred_element_type=jnp.float32)
            * score_scale
        )
        key_nope_grad = (
            jnp.einsum("hij,ihd->jhd", score_grad, query_nope, preferred_element_type=jnp.float32)
            * score_scale
        )
        key_rope_grad = (
            jnp.einsum("hij,ihd->jd", score_grad, query_rope, preferred_element_type=jnp.float32)
            * score_scale
        )
        value_grad = jnp.einsum(
            "hij,ihd->jhd", probs_low, mixed_grad, preferred_element_type=jnp.float32
        )
        expanded_grad = jnp.concatenate([key_nope_grad, value_grad], axis=-1).reshape(
            seq_rows, H * (DN + DV)
        )
        latent_up_part, latent_grad_all = latent_products(latent_all, expanded_grad, full_latent_up)
        latent_grad, key_rope_own = (
            lax.psum_scatter(
                latent_grad_all.astype(jnp.bfloat16), "ctx", scatter_dimension=0, tiled=True
            ).astype(jnp.float32),
            lax.psum_scatter(
                key_rope_grad.astype(jnp.bfloat16), "ctx", scatter_dimension=0, tiled=True
            ).astype(jnp.float32),
        )
        latent_back, latent_gain_grad = rms_back(
            latent_grad, latent_plain, latent_inverse, latent_gain
        )
        latent_raw_grad = jnp.concatenate(
            [latent_back, rope_back(key_rope_own, local_cos, local_sin)], axis=-1
        ).astype(jnp.bfloat16)
        query_raw_grad = (
            jnp.concatenate(
                [query_nope_grad, rope_back(query_rope_grad, head_cos, head_sin)], axis=-1
            )
            .reshape(local_rows, H * (DN + DR))
            .astype(jnp.bfloat16)
        )
        query_up_part = matmul_left(query_low, query_raw_grad)
        query_mixed_grad = matmul_right(query_raw_grad, full_query_up)
        query_back, query_gain_grad = rms_back(
            query_mixed_grad, query_plain, query_inverse, query_gain
        )
        query_latent_grad = query_back.astype(jnp.bfloat16)
        query_down_part = matmul_left(first_low, query_latent_grad)
        latent_down_part = matmul_left(first_low, latent_raw_grad)
        first_grad = matmul_right(query_latent_grad, full_query_down) + matmul_right(
            latent_raw_grad, full_latent_down
        )
        first_back, attn_gain_grad = rms_back(first_grad, first_plain, first_inverse, attn_gain)
        input_grads.append((resid_grad + first_back).astype(jnp.bfloat16))
        batch_parts = [
            attn_gain_grad,
            query_down_part,
            query_gain_grad,
            query_up_part,
            latent_down_part,
            latent_gain_grad,
            latent_up_part,
            attn_out_part,
            mlp_gain_grad,
        ]
        if attn_sums is None:
            attn_sums = batch_parts
        else:
            attn_sums = [held + fresh for held, fresh in zip(attn_sums, batch_parts)]
    shares = (
        lax.psum_scatter(
            attn_sums[0].astype(jnp.bfloat16), "fsdp", scatter_dimension=0, tiled=True
        ).astype(jnp.float32),
        lax.psum_scatter(
            attn_sums[1].astype(jnp.bfloat16), "fsdp", scatter_dimension=0, tiled=True
        ).astype(jnp.float32),
        lax.psum_scatter(
            attn_sums[2].astype(jnp.bfloat16), "fsdp", scatter_dimension=0, tiled=True
        ).astype(jnp.float32),
        lax.psum_scatter(
            attn_sums[3].astype(jnp.bfloat16), "fsdp", scatter_dimension=0, tiled=True
        ).astype(jnp.float32),
        lax.psum_scatter(
            attn_sums[4].astype(jnp.bfloat16), "fsdp", scatter_dimension=0, tiled=True
        ).astype(jnp.float32),
        lax.psum_scatter(
            attn_sums[5].astype(jnp.bfloat16), "fsdp", scatter_dimension=0, tiled=True
        ).astype(jnp.float32),
        lax.psum_scatter(
            attn_sums[6].astype(jnp.bfloat16), "fsdp", scatter_dimension=0, tiled=True
        ).astype(jnp.float32),
        lax.psum_scatter(
            attn_sums[7].astype(jnp.bfloat16), "fsdp", scatter_dimension=0, tiled=True
        ).astype(jnp.float32),
        lax.psum_scatter(
            attn_sums[8].astype(jnp.bfloat16), "fsdp", scatter_dimension=0, tiled=True
        ).astype(jnp.float32),
    )
    for place in range(9):
        sums[place] = shares[place]
    totals = (
        lax.psum(sums[0].astype(jnp.bfloat16), "ctx").astype(jnp.float32),
        lax.psum(sums[1].astype(jnp.bfloat16), "ctx").astype(jnp.float32),
        lax.psum(sums[2].astype(jnp.bfloat16), "ctx").astype(jnp.float32),
        lax.psum(sums[3].astype(jnp.bfloat16), "ctx").astype(jnp.float32),
        lax.psum(sums[4].astype(jnp.bfloat16), "ctx").astype(jnp.float32),
        lax.psum(sums[5].astype(jnp.bfloat16), "ctx").astype(jnp.float32),
        lax.psum(sums[6].astype(jnp.bfloat16), "ctx").astype(jnp.float32),
        lax.psum(sums[7].astype(jnp.bfloat16), "ctx").astype(jnp.float32),
        lax.psum(sums[8].astype(jnp.bfloat16), "ctx").astype(jnp.float32),
        lax.psum(sums[9].astype(jnp.bfloat16), "ctx").astype(jnp.float32),
        lax.psum(sums[10].astype(jnp.bfloat16), "ctx").astype(jnp.float32),
        lax.psum(sums[11].astype(jnp.bfloat16), "ctx").astype(jnp.float32),
    )
    return (
        jnp.stack(outputs)[None],
        jnp.stack(input_grads)[None],
        totals[0],
        totals[1],
        totals[2],
        totals[3],
        totals[4],
        totals[5],
        totals[6],
        totals[7],
        totals[8],
        totals[9],
        totals[10],
        totals[11],
    )


def solution(mesh):
    placed = (
        P("fsdp", None, "ctx", None),
        P("fsdp", None, "ctx", None),
        P("fsdp", None),
        P(),
        P("fsdp"),
        P("fsdp", None),
        P("fsdp"),
        P("fsdp", None),
        P("fsdp", None),
        P("fsdp"),
        P("fsdp", None),
        P("fsdp", None),
        P("fsdp"),
        P("fsdp", None),
        P("fsdp", None),
        P("fsdp", None),
    )
    return jax.shard_map(
        body,
        mesh=mesh,
        in_specs=placed,
        out_specs=(
            P("fsdp", None, "ctx", None),
            P("fsdp", None, "ctx", None),
            P("fsdp"),
            P("fsdp", None),
            P("fsdp"),
            P("fsdp", None),
            P("fsdp", None),
            P("fsdp"),
            P("fsdp", None),
            P("fsdp", None),
            P("fsdp"),
            P("fsdp", None),
            P("fsdp", None),
            P("fsdp", None),
        ),
        check_vma=False,
    )
```

profile of v0, /device:TPU:0, one launch (start us, length us, event | category | flops | bytes accessed | tf_op | source)
XLA Modules:
  0.0 2488.6 jit_solution(1350618064368545653)
XLA Ops:
  18.2 25.8 %all-reduce.9 = (bf16[2560]{0:T(1024)(128)(2,1)S(1)}, bf16[256]{0:T(256)(128)(2,1)S(1)}, bf16[768]{0:T(1024)(128)(2,1)S(1)}, bf16[2560]{0:T(1024)(128)(2,1)S(1)}) all-reduce(bf16[2560]{0:T(1024)(128)(2,1)S(1)} %dynamic-update-slice, bf16[256]{0:T(256)(128)(2,1)S(1)} %dynamic-update-slice.1, ...), channel_id=1, replica_groups=mesh['ctx'=4,'fsdp'=8] {'fsdp'}, use_global_device_ids=true, to_apply=%add | all-reduce | flops 6144 | bytes 24576
  56.2 14.1 all_gather.68
  71.2 15.8 all_gather.63
  94.5 14.5 copy.107
  114.8 39.8 %all-gather.15.cloned.1.call-done = bf16[768,3840]{1,0:T(8,128)(2,1)} async-done(((bf16[96,3840]{1,0:T(8,128)(2,1)}), bf16[768,3840]{1,0:T(8,128)(2,1)}) %all-gather.15.cloned.1.call-update) | async-done | bytes 5898256 | tf_op jit(solution)/shard_map/all_gather | solution.py:183
  165.3 19.9 fusion.22
  185.3 28.2 %fusion.157 = (f32[40,256]{1,0:T(8,128)S(1)}, f32[40,256,1024]{2,1,0:T(8,128)}) fusion(f32[40,256,1024]{2,1,0:T(8,128)} %fusion.22, bf16[256,40,32]{0,2,1:T(8,128)(2,1)S(1)} %get-tuple-element.86, bf16[1024,32]{0,1:T(8,128)(2,1)} %all_gather.68, pred[256,1024]{1,0:T(8,128)(4,1)S(1)} %copy-done.51), kind=kOutput, calls=%fused_computation.305 | convolution fusion | flops 713021440 | bytes 84910080 | tf_op jit(solution)/shard_map/ihd,jd->hij/dot_general | solution.py:224
  213.5 18.0 fusion.4
  232.1 23.6 divide_convert_fusion.1
  255.7 13.0 fusion.61
  281.9 60.3 %all-gather.19.cloned.1.call-done = bf16[2048,2560]{1,0:T(8,128)(2,1)} async-done(((bf16[256,2560]{1,0:T(8,128)(2,1)}), bf16[2048,2560]{1,0:T(8,128)(2,1)}) %all-gather.19.cloned.1.call-update) | async-done | bytes 10485776 | tf_op jit(solution)/shard_map/all_gather | solution.py:245
  342.2 14.8 fusion.160
  367.6 40.4 %all-gather.23.cloned.1.call-done = bf16[2048,2560]{1,0:T(8,128)(2,1)} async-done(((bf16[256,2560]{1,0:T(8,128)(2,1)}), bf16[2048,2560]{1,0:T(8,128)(2,1)}) %all-gather.23.cloned.1.call-update) | async-done | bytes 10485776 | tf_op jit(solution)/shard_map/all_gather | solution.py:246
  407.9 20.0 multiply_convert_fusion.4
  427.9 17.1 fusion.165
  445.0 20.3 convolution_add_fusion.1
  466.0 13.4 all_gather.73
  479.4 15.9 all_gather.72
  501.8 13.6 copy.108
  515.4 20.7 fusion.14
  536.1 28.8 %fusion.158 = (f32[40,256]{1,0:T(8,128)S(1)}, f32[40,256,1024]{2,1,0:T(8,128)}) fusion(f32[40,256,1024]{2,1,0:T(8,128)} %fusion.14, bf16[256,40,32]{0,2,1:T(8,128)(2,1)S(1)} %copy-done.16, bf16[1024,32]{0,1:T(8,128)(2,1)S(1)} %all_gather.73, pred[256,1024]{1,0:T(8,128)(4,1)S(1)} %copy-done.50), kind=kOutput, calls=%fused_computation.306 | convolution fusion | flops 713021440 | bytes 84910080 | tf_op jit(solution)/shard_map/ihd,jd->hij/dot_general | solution.py:224
  564.9 18.6 fusion.5
  584.2 23.7 divide_convert_fusion
  607.9 13.5 fusion.64
  638.4 62.6 %all-gather.21.cloned.1.call-done = bf16[2048,2560]{1,0:T(8,128)(2,1)} async-done(((bf16[256,2560]{1,0:T(8,128)(2,1)}), bf16[2048,2560]{1,0:T(8,128)(2,1)}) %all-gather.21.cloned.1.call-update) | async-done | bytes 10485776 | tf_op jit(solution)/shard_map/all_gather | solution.py:245
  701.0 14.4 fusion.163
  726.0 40.0 %all-gather.25.cloned.1.call-done = bf16[2048,2560]{1,0:T(8,128)(2,1)} async-done(((bf16[256,2560]{1,0:T(8,128)(2,1)}), bf16[2048,2560]{1,0:T(8,128)(2,1)}) %all-gather.25.cloned.1.call-update) | async-done | bytes 10485776 | tf_op jit(solution)/shard_map/all_gather | solution.py:246
  766.0 19.9 multiply_convert_fusion.2
  786.0 16.9 fusion.167
  802.9 20.3 convolution_add_fusion
  823.3 20.7 fusion.161
  844.0 19.4 fusion.164
  865.0 94.4 %reduce-scatter.26.cloned.1.call-done = f32[256,2560]{1,0:T(8,128)} async-done(((f32[2048,2560]{1,0:T(8,128)}), f32[256,2560]{1,0:T(8,128)}) %reduce-scatter.26.cloned.1.call-update) | async-done | bytes 2621456 | tf_op jit(solution)/shard_map/reduce_scatter | solution.py:251
  963.2 135.6 %reduce-scatter.16.cloned.1.call-done = f32[256,2560]{1,0:T(8,128)} async-done(((f32[2048,2560]{1,0:T(8,128)}), f32[256,2560]{1,0:T(8,128)}) %reduce-scatter.16.cloned.1.call-update) | async-done | bytes 2621456 | tf_op jit(solution)/shard_map/reduce_scatter | solution.py:250
  1098.8 139.6 %reduce-scatter.18.cloned.1.call-done = f32[256,2560]{1,0:T(8,128)} async-done(((f32[2048,2560]{1,0:T(8,128)}), f32[256,2560]{1,0:T(8,128)}) %reduce-scatter.18.cloned.1.call-update) | async-done | bytes 2621456 | tf_op jit(solution)/shard_map/reduce_scatter | solution.py:250
  1257.5 14.5 convolution_bitcast_fusion.1
  1272.0 29.2 %multiply_reduce_fusion.1 = (f32[40,256]{1,0:T(8,128)S(1)}, f32[40,256,1024]{2,1,0:T(8,128)}) fusion(f32[40,256,1024]{2,1,0:T(8,128)} %get-tuple-element.126, f32[40,256]{1,0:T(8,128)S(1)} %log_add_fusion.1, bf16[256,40,64]{0,2,1:T(8,128)(2,1)S(1)} %bitcast.269, bf16[1024,40,128]{0,2,1:T(8,128)(2,1)} %bitcast.250), kind=kOutput, calls=%fused_computation.10 | convolution fusion | flops 1373624320 | bytes 90521600 | tf_op jit(solution)/shard_map/ihd,jhd->hij/dot_general | solution.py:265
  1301.2 34.1 %multiply_convert_fusion.1 = bf16[40,256,1024]{2,1,0:T(8,128)(2,1)} fusion(f32[40,256,1024]{2,1,0:T(8,128)} %get-tuple-element.134, f32[40,256,1024]{2,1,0:T(8,128)} %get-tuple-element.126, f32[40,256]{1,0:T(8,128)S(1)} %get-tuple-element.133, f32[40,256]{1,0:T(8,128)S(1)} %log_add_fusion.1), kind=kLoop, calls=%fused_computation.9 | loop fusion | flops 41943040 | bytes 104939520 | tf_op jit(solution)/shard_map/convert_element_type | solution.py:269
  1335.3 13.2 fusion.71
  1358.0 15.7 multiply_bitcast_fusion.1
  1382.9 14.5 convolution_bitcast_fusion
  1397.5 29.2 %multiply_reduce_fusion = (f32[40,256]{1,0:T(8,128)S(1)}, f32[40,256,1024]{2,1,0:T(8,128)}) fusion(f32[40,256,1024]{2,1,0:T(8,128)} %get-tuple-element.130, f32[40,256]{1,0:T(8,128)S(1)} %copy-done.59, bf16[256,40,64]{0,2,1:T(8,128)(2,1)S(1)} %bitcast.271, bf16[1024,40,128]{0,2,1:T(8,128)(2,1)} %bitcast.246), kind=kOutput, calls=%fused_computation.7 | convolution fusion | flops 1373624320 | bytes 90521600 | tf_op jit(solution)/shard_map/ihd,jhd->hij/dot_general | solution.py:265
  1426.7 34.1 %multiply_convert_fusion = bf16[40,256,1024]{2,1,0:T(8,128)(2,1)} fusion(f32[40,256,1024]{2,1,0:T(8,128)} %get-tuple-element.136, f32[40,256,1024]{2,1,0:T(8,128)} %get-tuple-element.130, f32[40,256]{1,0:T(8,128)S(1)} %get-tuple-element.135, f32[40,256]{1,0:T(8,128)S(1)} %copy-done.59), kind=kLoop, calls=%fused_computation.6 | loop fusion | flops 41943040 | bytes 104939520 | tf_op jit(solution)/shard_map/convert_element_type | solution.py:269
  1470.3 15.4 multiply_bitcast_fusion
  1485.8 10.7 pad_maximum_fusion
  1551.6 10.9 convolution_add_fusion.2
  1562.5 13.9 fusion.11
  1593.4 18.4 reduce-scatter.28.cloned.1.call-done
  1620.5 11.7 convolution_bitcast_fusion.2
  1632.2 13.4 fusion.74
  1645.7 11.0 broadcast_multiply_fusion.1
  1684.1 12.7 fusion.93
  1696.8 16.2 add_convert_fusion
  1713.2 14.7 fusion.173
  1728.0 13.4 fusion.172
  1741.5 12.3 fusion.171
  1753.9 13.8 add_convert_fusion.2
  1767.6 14.0 add_convert_fusion.4
  1781.6 11.8 add_convert_fusion.3
  1795.2 28.7 %reduce-scatter.34.cloned.1.call-done = bf16[96,3840]{1,0:T(8,128)(2,1)} async-done(((bf16[768,3840]{1,0:T(8,128)(2,1)}), bf16[96,3840]{1,0:T(8,128)(2,1)}) %reduce-scatter.34.cloned.1.call-update) | async-done | bytes 737296 | tf_op jit(solution)/shard_map/reduce_scatter | solution.py:352
  1823.9 98.8 %reduce-scatter.38.cloned.1.call-done = bf16[320,2560]{1,0:T(8,128)(2,1)} async-done(((bf16[2560,2560]{1,0:T(8,128)(2,1)}), bf16[320,2560]{1,0:T(8,128)(2,1)}) %reduce-scatter.38.cloned.1.call-update) | async-done | bytes 1638416 | tf_op jit(solution)/shard_map/reduce_scatter | solution.py:364
  1936.1 24.7 all-reduce.8
  1961.1 12.0 all-reduce.10
  1981.8 477.5 %all-reduce.14.cloned.1.call-done = (bf16[320,768]{1,0:T(8,128)(2,1)}, bf16[96,3840]{1,0:T(8,128)(2,1)}, bf16[320,288]{0,1:T(8,128)(2,1)}, bf16[32,5120]{1,0:T(8...) async-done(((bf16[320,768]{1,0:T(8,128)(2,1)}, bf16[96,3840]{1,0:T(8,128)(2,1)}, ...) | async-done | bytes 15667216 | tf_op jit(solution)/shard_map/psum | solution.py:375
  (503 shorter events, 310.1 us)
Async XLA Ops:
  7.3 38.1 %all-gather.27.cloned.1.call-start = ((), (), s32[]{:S(2)}) async-start(), calls=%async_computation.33 | async-start | bytes 1990656 | tf_op jit(solution)/shard_map/all_gather | solution.py:184
  8.0 79.0 %all-gather.11.cloned.1.call-start = ((), (), s32[]{:S(2)}) async-start(), calls=%async_computation.13 | async-start | bytes 2949120 | tf_op jit(solution)/shard_map/all_gather | solution.py:186
  8.7 100.2 %all-gather.13.cloned.1.call-start = ((), (), s32[]{:S(2)}) async-start(), calls=%async_computation.14 | async-start | bytes 4423680 | tf_op jit(solution)/shard_map/all_gather | solution.py:181
  9.5 145.1 %all-gather.15.cloned.1.call-start = ((), (), s32[]{:S(2)}) async-start(), calls=%async_computation.15 | async-start | bytes 6635520 | tf_op jit(solution)/shard_map/all_gather | solution.py:183
  10.1 258.6 %all-gather.17.cloned.1.call-start = ((), (), s32[]{:S(2)}) async-start(), calls=%async_computation.16 | async-start | bytes 14745600 | tf_op jit(solution)/shard_map/all_gather | solution.py:187
  10.6 331.5 %all-gather.19.cloned.1.call-start = ((), (), s32[]{:S(2)}) async-start(), calls=%async_computation.17 | async-start | bytes 11796480 | tf_op jit(solution)/shard_map/all_gather | solution.py:245
  17.2 35.5 %copy-start.108 = (s32[256]{0:T(256)}, s32[256]{0:T(256)S(1)}, u32[]{:S(2)}) copy-start(s32[256]{0:T(256)S(1)} %get-tuple-element.57) | copy-start | bytes 3076
  44.0 26.4 %copy-start.96 = (f32[256]{0:T(256)}, f32[256]{0:T(256)S(1)}, u32[]{:S(2)}) copy-start(f32[256]{0:T(256)S(1)} %convert_element_type.317) | copy-start | bytes 3076
  44.0 116.4 %copy-start.78 = (f32[768]{0:T(1024)}, f32[768]{0:T(1024)S(1)}, u32[]{:S(2)}) copy-start(f32[768]{0:T(1024)S(1)} %convert_element_type.320) | copy-start | bytes 9220
  44.0 68.6 %copy-start.64 = (f32[2560]{0:T(1024)}, f32[2560]{0:T(1024)S(1)}, u32[]{:S(2)}) copy-start(f32[2560]{0:T(1024)S(1)} %convert_element_type.315) | copy-start | bytes 30724
  44.0 232.1 %copy-start.80 = (f32[2560]{0:T(1024)}, f32[2560]{0:T(1024)S(1)}, u32[]{:S(2)}) copy-start(f32[2560]{0:T(1024)S(1)} %convert_element_type.328) | copy-start | bytes 30724
  44.1 68.5 %copy-start.93 = (f32[256]{0:T(256)}, f32[256]{0:T(256)S(1)}, u32[]{:S(2)}) copy-start(f32[256]{0:T(256)S(1)} %get-tuple-element.142) | copy-start | bytes 3076
  70.4 24.1 copy-start.102
  70.4 24.0 copy-start.104
  112.6 47.8 %copy-start.32 = (f32[256,768]{1,0:T(8,128)}, f32[256,768]{1,0:T(8,128)S(1)}, u32[]{:S(2)}) copy-start(f32[256,768]{1,0:T(8,128)S(1)} %get-tuple-element.124) | copy-start | bytes 2359300
  112.6 47.8 %copy-start.98 = (f32[256]{0:T(256)}, f32[256]{0:T(256)S(1)}, u32[]{:S(2)}) copy-start(f32[256]{0:T(256)S(1)} %add_rsqrt_fusion.1) | copy-start | bytes 3076
  114.8 45.5 %copy-start.100 = (f32[256]{0:T(256)}, f32[256]{0:T(256)S(1)}, u32[]{:S(2)}) copy-start(f32[256]{0:T(256)S(1)} %add_rsqrt_fusion.5) | copy-start | bytes 3076
  165.3 19.9 copy-start.18
  165.3 19.9 copy-start.51
  213.5 18.0 copy-start.60
  278.9 129.0 %all-gather.23.cloned.1.call-start = ((), (), s32[]{:S(2)}) async-start(), calls=%async_computation.21 | async-start | bytes 11796480 | tf_op jit(solution)/shard_map/all_gather | solution.py:246
  281.8 350.0 %reduce-scatter.20.cloned.1.call-start = ((), (), s32[]{:S(2)}) async-start(), calls=%async_computation.22 | async-start | bytes 23592960 | tf_op jit(solution)/shard_map/reduce_scatter | solution.py:251
  407.9 20.0 copy-start.130
  427.9 17.1 copy-start.133
  465.3 30.8 %copy-start.23 = (bf16[256,5120]{1,0:T(8,128)(2,1)S(1)}, bf16[256,5120]{1,0:T(8,128)(2,1)}, u32[]{:S(2)}) copy-start(bf16[256,5120]{1,0:T(8,128)(2,1)} %all-gather.11.cloned.1.call-done) | copy-start | bytes 7864324
  465.3 235.6 %all-gather.21.cloned.1.call-start = ((), (), s32[]{:S(2)}) async-start(), calls=%async_computation.19 | async-start | bytes 11796480 | tf_op jit(solution)/shard_map/all_gather | solution.py:245
  479.4 56.7 %copy-start.68 = (bf16[1024,32]{0,1:T(8,128)(2,1)}, bf16[1024,32]{0,1:T(8,128)(2,1)S(1)}, u32[]{:S(2)}) copy-start(bf16[1024,32]{0,1:T(8,128)(2,1)S(1)} %all_gather.73) | copy-start | bytes 196612
  515.4 20.7 copy-start.16
  515.4 20.7 copy-start.50
  564.9 18.6 copy-start.62
  637.8 128.2 %all-gather.25.cloned.1.call-start = ((), (), s32[]{:S(2)}) async-start(), calls=%async_computation.25 | async-start | bytes 11796480 | tf_op jit(solution)/shard_map/all_gather | solution.py:246
  638.4 321.0 %reduce-scatter.26.cloned.1.call-start = ((), (), s32[]{:S(2)}) async-start(), calls=%async_computation.26 | async-start | bytes 23592960 | tf_op jit(solution)/shard_map/reduce_scatter | solution.py:251
  766.0 20.0 copy-start.132
  823.2 275.6 %reduce-scatter.16.cloned.1.call-start = ((), (), s32[]{:S(2)}) async-start(), calls=%async_computation.18 | async-start | bytes 23592960 | tf_op jit(solution)/shard_map/reduce_scatter | solution.py:250
  844.0 394.4 %reduce-scatter.18.cloned.1.call-start = ((), (), s32[]{:S(2)}) async-start(), calls=%async_computation.20 | async-start | bytes 23592960 | tf_op jit(solution)/shard_map/reduce_scatter | solution.py:250
  863.5 374.9 %copy-start.7 = (f32[256,2560]{1,0:T(8,128)S(1)}, f32[256,2560]{1,0:T(8,128)}, u32[]{:S(2)}) copy-start(f32[256,2560]{1,0:T(8,128)} %copy-done.6) | copy-start | bytes 7864324
  863.5 374.9 %copy-start.115 = (f32[256]{0:T(256)S(1)}, f32[256]{0:T(256)}, u32[]{:S(2)}) copy-start(f32[256]{0:T(256)} %copy-done.114) | copy-start | bytes 3076
  863.6 374.9 %copy-start.117 = (f32[256]{0:T(256)S(1)}, f32[256]{0:T(256)}, u32[]{:S(2)}) copy-start(f32[256]{0:T(256)} %get-tuple-element.56) | copy-start | bytes 3076
  863.6 726.5 %reduce-scatter.24.cloned.1.call-start = ((), (), s32[]{:S(2)}) async-start(), calls=%async_computation.24 | async-start | bytes 81920 | tf_op jit(solution)/shard_map/reduce_scatter | solution.py:297
  1426.7 34.1 %copy-start.17 = (bf16[256,40,32]{0,2,1:T(8,128)(2,1)S(1)}, bf16[256,40,32]{0,2,1:T(8,128)(2,1)}, u32[]{:S(2)}) copy-start(bf16[256,40,32]{0,2,1:T(8,128)(2,1)} %get-tuple-element.87) | copy-start | bytes 1966084
  1485.8 104.4 %reduce-scatter.30.cloned.1.call-start = ((), (), s32[]{:S(2)}) async-start(), calls=%async_computation.28 | async-start | bytes 81920 | tf_op jit(solution)/shard_map/reduce_scatter | solution.py:297
  1485.8 20.4 slice-start
  1485.8 20.4 slice-start.1
  1528.6 63.2 %reduce-scatter.22.cloned.1.call-start = ((), (), s32[]{:S(2)}) async-start(), calls=%async_computation.23 | async-start | bytes 655360 | tf_op jit(solution)/shard_map/reduce_scatter | solution.py:294
  1551.4 60.4 %reduce-scatter.28.cloned.1.call-start = ((), (), s32[]{:S(2)}) async-start(), calls=%async_computation.27 | async-start | bytes 655360 | tf_op jit(solution)/shard_map/reduce_scatter | solution.py:294
  1582.2 29.6 %copy-start.43 = (f32[256,288]{0,1:T(8,128)S(1)}, f32[256,288]{0,1:T(8,128)}, u32[]{:S(2)}) copy-start(f32[256,288]{0,1:T(8,128)} %copy-done.42) | copy-start | bytes 884740
  1582.2 29.6 %copy-start.103 = (f32[256]{0:T(256)S(1)}, f32[256]{0:T(256)}, u32[]{:S(2)}) copy-start(f32[256]{0:T(256)} %copy-done.102) | copy-start | bytes 3076
  1582.2 31.3 %copy-start.2 = (bf16[1,2,256,2560]{3,2,1,0:T(8,128)(2,1)S(1)}, bf16[1,2,256,2560]{3,2,1,0:T(8,128)(2,1)}, u32[]{:S(2)}) copy-start(bf16[1,2,256,2560]{3,2,1,0:T(8,128)(2,1)} %param.16) | copy-start | bytes 7864324
  1582.2 31.3 %copy-start.65 = (f32[2560]{0:T(1024)S(1)}, f32[2560]{0:T(1024)}, u32[]{:S(2)}) copy-start(f32[2560]{0:T(1024)} %copy-done.64) | copy-start | bytes 30724
  1582.2 31.3 %copy-start.94 = (f32[256]{0:T(256)S(1)}, f32[256]{0:T(256)}, u32[]{:S(2)}) copy-start(f32[256]{0:T(256)} %copy-done.93) | copy-start | bytes 3076
  1590.0 203.4 %reduce-scatter.40.cloned.1.call-start = ((), (), s32[]{:S(2)}) async-start(), calls=%async_computation.34 | async-start | bytes 2211840
  1591.7 22.5 copy-start.88
  1591.7 22.9 copy-start.82
  1620.2 175.0 %reduce-scatter.36.cloned.1.call-start = ((), (), s32[]{:S(2)}) async-start(), calls=%async_computation.31 | async-start | bytes 2949120 | tf_op jit(solution)/shard_map/reduce_scatter | solution.py:361
  1645.7 149.6 %reduce-scatter.32.cloned.1.call-start = ((), (), s32[]{:S(2)}) async-start(), calls=%async_computation.29 | async-start | bytes 4423680 | tf_op jit(solution)/shard_map/reduce_scatter | solution.py:346
  1673.4 150.5 %reduce-scatter.34.cloned.1.call-start = ((), (), s32[]{:S(2)}) async-start(), calls=%async_computation.30 | async-start | bytes 6635520 | tf_op jit(solution)/shard_map/reduce_scatter | solution.py:352
  1682.8 239.9 %reduce-scatter.38.cloned.1.call-start = ((), (), s32[]{:S(2)}) async-start(), calls=%async_computation.32 | async-start | bytes 14745600 | tf_op jit(solution)/shard_map/reduce_scatter | solution.py:364
  1713.0 746.3 %all-reduce.14.cloned.1.call-start = ((), (), s32[]{:S(2)}) async-start(), calls=%async_computation.35 | async-start | bytes 31408128 | tf_op jit(solution)/shard_map/psum | solution.py:375
  1713.2 28.2 %slice-start.5 = ((s8[10485760]{0:T(1024)(128)(4,1)}), s8[4194304]{0:T(1024)(128)(4,1)S(1)}, s32[]{:S(2)}) async-start(s8[10485760]{0:T(1024)(128)(4,1)} %bitcast.277), calls=%async_computation.41 | async-start | bytes 8388608
  1713.2 28.2 %slice-start.6 = ((s8[10485760]{0:T(1024)(128)(4,1)}), s8[4194304]{0:T(1024)(128)(4,1)S(1)}, s32[]{:S(2)}) async-start(s8[10485760]{0:T(1024)(128)(4,1)} %bitcast.277), calls=%async_computation.42 | async-start | bytes 8388608
  1728.0 25.8 %slice-start.11 = ((s8[10485760]{0:T(1024)(128)(4,1)}), s8[4194304]{0:T(1024)(128)(4,1)S(1)}, s32[]{:S(2)}) async-start(s8[10485760]{0:T(1024)(128)(4,1)} %bitcast.281), calls=%async_computation.47 | async-start | bytes 8388608
  1728.0 25.8 %slice-start.12 = ((s8[10485760]{0:T(1024)(128)(4,1)}), s8[4194304]{0:T(1024)(128)(4,1)S(1)}, s32[]{:S(2)}) async-start(s8[10485760]{0:T(1024)(128)(4,1)} %bitcast.281), calls=%async_computation.48 | async-start | bytes 8388608
  1741.5 26.2 %slice-start.8 = ((s8[10485760]{0:T(1024)(128)(4,1)}), s8[2097152]{0:T(1024)(128)(4,1)S(1)}, s32[]{:S(2)}) async-start(s8[10485760]{0:T(1024)(128)(4,1)} %bitcast.279), calls=%async_computation.44 | async-start | bytes 4194304
  1741.5 26.2 %slice-start.9 = ((s8[10485760]{0:T(1024)(128)(4,1)}), s8[4194304]{0:T(1024)(128)(4,1)S(1)}, s32[]{:S(2)}) async-start(s8[10485760]{0:T(1024)(128)(4,1)} %bitcast.279), calls=%async_computation.45 | async-start | bytes 8388608
  (112 other events, 677.3 us)
Sparse Core Ops, SparseCore 0:
  10.0 29.3 all-gather.26
  41.3 30.1 all-gather.10
  73.3 35.6 all-gather.12
  110.7 43.8 all-gather.14
  156.4 74.3 all-gather.16
  279.0 63.1 all-gather.18
  344.6 63.2 all-gather.22
  465.5 135.9 reduce-scatter.19
  637.9 63.0 all-gather.20
  702.7 63.2 all-gather.24
  823.3 135.9 reduce-scatter.25
  962.8 135.9 reduce-scatter.15
  1102.4 135.9 reduce-scatter.17
  1485.9 19.0 reduce-scatter.23
  1528.7 18.9 reduce-scatter.29
  1551.5 21.6 reduce-scatter.21
  1590.1 21.5 reduce-scatter.27
  1620.4 38.5 reduce-scatter.39
  1663.3 43.6 reduce-scatter.35
  1710.7 50.0 reduce-scatter.31
  1764.3 59.6 reduce-scatter.33
  1827.5 95.1 reduce-scatter.37
  1927.3 531.9 all-reduce.13
where the time goes:
time: 2500 us; the launch traced here: 2490 us
  waiting for transfers between devices  1240 us (50%)
  matrix products  782 us (31%)
  other arithmetic  261 us (10%)
  blocking collectives  122 us (5%)
  local copies, waits for them, and re-layouts  61.5 us (2%)
    psum x1, waiting for transfers between devices, body(): lax.psum(sums[1].astype(jnp.bfloat16), 'ctx').astype(jnp.float32)  477 us
    reduce_scatter x2, waiting for transfers between devices, body(): lax.psum_scatter(parts[0], 'fsdp', scatter_dimension=0, tiled=True)  275 us
    dot_general x18, matrix products, matmul_left(): lax.dot_general(left, right, (((0,), (0,)), ((), ())), preferred_element_...  163 us
    dot_general x16, matrix products, matmul_plain(): return jnp.dot(left, right, preferred_element_type=jnp.float32)  162 us
    dot_general x18, matrix products, matmul_right(): lax.dot_general(left, right, (((1,), (1,)), ((), ())), preferred_element_...  146 us
    all_gather x2, waiting for transfers between devices, body(): lax.all_gather(second_low, 'fsdp', axis=0, tiled=True)  123 us
    reduce_scatter x1, waiting for transfers between devices, body(): lax.psum_scatter(attn_sums[7].astype(jnp.bfloat16), 'fsdp', scatter_dimen...  98.8 us
    reduce_scatter x2, waiting for transfers between devices, body(): lax.psum_scatter(parts[1], 'fsdp', scatter_dimension=0, tiled=True)  94.4 us
  transfers between devices with their start and end apart: 23, of which 12 were waited for; matrix products, arithmetic and copies ran while one was open for 27% of the time, Pallas kernels for 0%

commit v1 on v0

v1 whole, which is shorter than its diff:
```python
import functools
import math

import jax
import jax.numpy as jnp
from jax import lax
from jax.experimental import pallas as pl
from jax.experimental.pallas import tpu as pltpu
from jax.sharding import PartitionSpec as P

H = 40
DN = 64
DR = 32
DV = 64
KVR = 256
QUAD = 4


branch_scale = 1.4 / math.sqrt(62.0)
norm_eps = 1e-05
rope_base = 10000.0
lowest_score = -1e30
score_scale = (DN + DR) ** -0.5
exp_scale = math.log2(math.e) * score_scale


def rms_scale(values, gain):
    inverse = lax.rsqrt(jnp.mean(values * values, axis=-1, keepdims=True) + norm_eps)
    plain = values * inverse
    return (plain * gain, plain, inverse)


def rms_back(grad_out, plain, inverse, gain):
    gain_grad = jnp.sum(grad_out * plain, axis=0)
    scaled = grad_out * gain
    values_grad = inverse * (scaled - plain * jnp.mean(scaled * plain, axis=-1, keepdims=True))
    return (values_grad, gain_grad)


def rope_tables(positions, width):
    half = width // 2
    freq = rope_base ** (-(jnp.arange(half, dtype=jnp.float32) * 2.0 / width))
    angle = positions.astype(jnp.float32)[:, None] * freq[None, :]
    return (
        jnp.concatenate([jnp.cos(angle), jnp.cos(angle)], axis=-1),
        jnp.concatenate([jnp.sin(angle), jnp.sin(angle)], axis=-1),
    )


def turn_half(values):
    half = values.shape[-1] // 2
    return jnp.concatenate([-values[..., half:], values[..., :half]], axis=-1)


def turn_back(values):
    half = values.shape[-1] // 2
    return jnp.concatenate([values[..., half:], -values[..., :half]], axis=-1)


def rope_apply(values, cosine, sine):
    return values * cosine + turn_half(values) * sine


def rope_back(grads, cosine, sine):
    return grads * cosine + turn_back(grads * sine)


def matmul_plain(left, right):
    return jnp.dot(left, right, preferred_element_type=jnp.float32)


def matmul_left(left, right):
    return lax.dot_general(
        left, right, (((0,), (0,)), ((), ())), preferred_element_type=jnp.float32
    )


def matmul_right(left, right):
    return lax.dot_general(
        left, right, (((1,), (1,)), ((), ())), preferred_element_type=jnp.float32
    )


def flip(values, bit):
    count = lax.axis_size("fsdp")
    return lax.ppermute(values, "fsdp", [(i, i ^ bit) for i in range(count)])


def chip_bits():
    return [1 << k for k in range(1, lax.axis_size("fsdp").bit_length() - 1)]


def low(values):
    return values.astype(jnp.bfloat16)


def add_up(left, right):
    return left.astype(jnp.float32) + right.astype(jnp.float32)


def place_kernel(plan, me_ref, *refs):
    sources, outs, sems = refs[: len(plan)], refs[len(plan) : -1], refs[-1]
    me = me_ref[0]
    copies = []
    for source, (out, rows, places, stride, offset) in zip(sources, plan):
        for k, place in enumerate(places):
            start = pl.multiple_of((me ^ place) * stride + offset, 16)
            copies.append(
                pltpu.make_async_copy(
                    source.at[pl.ds(k * rows, rows)],
                    outs[out].at[pl.ds(start, rows)],
                    sems.at[len(copies)],
                )
            )
    for copy in copies:
        copy.start()
    for copy in copies:
        copy.wait()


def place_shards(groups):
    count = lax.axis_size("fsdp")
    me = lax.axis_index("fsdp").astype(jnp.int32).reshape(1)
    plan, sources, shapes = [], [], []
    for out, parts in enumerate(groups):
        heights = [held.shape[0] * 2 // count for held, _, _ in parts]
        offset = 0
        for (held, other, order), rows in zip(parts, heights):
            places = [0]
            for bit in order:
                places = places + [place ^ bit for place in places]
            plan.append((out, rows, tuple(places), sum(heights), offset))
            plan.append((out, rows, tuple(place ^ 1 for place in places), sum(heights), offset))
            sources += [held, other]
            offset += rows
        shapes.append(jax.ShapeDtypeStruct((count * sum(heights), parts[0][0].shape[1]), jnp.bfloat16))
    anywhere = pl.BlockSpec(memory_space=pl.ANY)
    return pl.pallas_call(
        functools.partial(place_kernel, tuple(plan)),
        in_specs=[pl.BlockSpec(memory_space=pltpu.SMEM)] + [anywhere] * len(sources),
        out_specs=[pl.BlockSpec(memory_space=pltpu.VMEM)] * len(shapes),
        out_shape=shapes,
        scratch_shapes=[pltpu.SemaphoreType.DMA((len(plan) * count // 2,))],
        compiler_params=pltpu.CompilerParams(vmem_limit_bytes=32 * 2**20),
        name="place_shards",
    )(me, *sources)


class ScatterWhole:
    def __init__(self, held, order):
        self.held = held
        self.order = list(order)
        self.left = [1 << k for k in range(held.shape[0].bit_length() - 2, -1, -1)]
        self.me = lax.axis_index("fsdp")

    def send(self):
        rows, width = self.held.shape[1:]
        place = self.left.index(self.order[0])
        below = 1 << (len(self.left) - place - 1)
        held = self.held.reshape(-1, 2, below, rows, width)
        mine = (self.me // self.order[0]) % 2
        self.kept = lax.dynamic_index_in_dim(held, mine, 1, keepdims=False)
        return lax.dynamic_index_in_dim(held, 1 - mine, 1, keepdims=False)

    def move(self, value):
        return flip(value, self.order[0])

    def absorb(self, value):
        self.held = low(add_up(self.kept, value)).reshape((-1,) + self.held.shape[1:])
        self.left.remove(self.order.pop(0))


def lane_part(values, width, place):
    lane = lax.broadcasted_iota(jnp.int32, values.shape, 1)
    return jnp.where(lane // width == place, values, 0.0)


def pair_rows(nope, rope, pair):
    both = nope[:, pair * 2 * DN : (pair + 1) * 2 * DN]
    return low(
        jnp.concatenate(
            [
                jnp.concatenate(
                    [lane_part(both, DN, head), lane_part(rope, DR, 2 * pair + head)], axis=1
                )
                for head in range(2)
            ],
            axis=0,
        )
    )


def forward_kernel(
    low_ref, latent_ref, rope_ref, bias_ref, cos_ref, ahead_ref, behind_ref,
    query_w, key_w, value_w, query_ref, mixed_ref, total_ref,
):
    rows = low_ref.shape[1]
    raw = matmul_plain(low_ref[0], query_w[...])
    nope = raw[:, : QUAD * DN]
    rope = raw[:, QUAD * DN :]
    lanes = QUAD * DR
    rope = (
        rope * cos_ref[...]
        + pltpu.roll(rope, lanes - DR // 2, 1) * ahead_ref[...]
        + pltpu.roll(rope, DR // 2, 1) * behind_ref[...]
    )
    query_ref[0] = low(jnp.concatenate([nope, rope], axis=1))
    latent = latent_ref[0]
    keys = low(matmul_plain(latent, key_w[...]))
    values = low(matmul_plain(latent, value_w[...])).T
    mixed = []
    for pair in range(2):
        key_cat = jnp.concatenate(
            [keys[:, pair * 2 * DN : (pair + 1) * 2 * DN], rope_ref[0]], axis=1
        )
        scores = matmul_right(key_cat, pair_rows(nope, rope, pair))
        for head in range(2):
            place = 2 * pair + head
            own = scores[:, head * rows : (head + 1) * rows] * exp_scale + bias_ref[0]
            top = jnp.max(own, axis=0, keepdims=True)
            expo = jnp.exp2(own - top)
            total = jnp.sum(expo, axis=0, keepdims=True)
            out = matmul_plain(values[place * DV : (place + 1) * DV], low(expo))
            mixed.append(out / total)
            total_ref[0, 0, place : place + 1, :] = top + jnp.log2(total)
    mixed_ref[0] = low(jnp.concatenate(mixed, axis=0).T)


def attend_forward(query_low, latent, rope_keys, bias, cosine, ahead, behind, query_w, key_w, value_w, quads):
    batches, rows, rank = query_low.shape
    keys, width = latent.shape[1:]
    qw, kw, rw = QUAD * (DN + DR), QUAD * DN, QUAD * DR
    fixed = lambda b, j: (0, 0)
    whole = lambda b, j: (b, 0, 0)
    flops = batches * quads * (2 * keys * width * 2 * kw + 2 * rows * rank * qw + 4 * 4 * keys * rows * 256)
    return pl.pallas_call(
        forward_kernel,
        grid=(batches, quads),
        in_specs=[
            pl.BlockSpec((1, rows, rank), whole),
            pl.BlockSpec((1, keys, width), whole),
            pl.BlockSpec((1, keys, rw), whole),
            pl.BlockSpec((1, keys, rows), whole),
            pl.BlockSpec((rows, rw), fixed),
            pl.BlockSpec((rows, rw), fixed),
            pl.BlockSpec((rows, rw), fixed),
            pl.BlockSpec((rank, qw), lambda b, j: (0, j)),
            pl.BlockSpec((width, kw), lambda b, j: (0, j)),
            pl.BlockSpec((width, kw), lambda b, j: (0, j)),
        ],
        out_specs=[
            pl.BlockSpec((1, rows, qw), lambda b, j: (b, 0, j)),
            pl.BlockSpec((1, rows, kw), lambda b, j: (b, 0, j)),
            pl.BlockSpec((1, 1, QUAD, rows), lambda b, j: (b, j, 0, 0)),
        ],
        out_shape=[
            jax.ShapeDtypeStruct((batches, rows, quads * qw), jnp.bfloat16),
            jax.ShapeDtypeStruct((batches, rows, quads * kw), jnp.bfloat16),
            jax.ShapeDtypeStruct((batches, quads, QUAD, rows), jnp.float32),
        ],
        compiler_params=pltpu.CompilerParams(
            dimension_semantics=("arbitrary", "arbitrary"), vmem_limit_bytes=48 * 2**20
        ),
        cost_estimate=pl.CostEstimate(
            flops=int(flops), bytes_accessed=40 * 2**20, transcendentals=batches * quads * 4 * keys * rows
        ),
        name="attend_forward",
    )(query_low, latent, rope_keys, bias, cosine, ahead, behind, query_w, key_w, value_w)


def backward_kernel(
    query_ref, grad_ref, latent_ref, flat_ref, rope_ref, turned_ref, bias_ref, total_ref,
    cos_ref, sin_ref, key_w, value_w,
    query_out, key_up_out, value_up_out, latent_out, rope_out,
):
    rows = query_ref.shape[0]
    half = DR // 2

    @pl.when(pl.program_id(0) == 0)
    def _():
        latent_out[...] = jnp.zeros_like(latent_out)
        rope_out[...] = jnp.zeros_like(rope_out)

    latent = latent_ref[...]
    keys = low(matmul_plain(latent, key_w[...]))
    values = low(matmul_plain(latent, value_w[...]))
    turned_keys = keys.T
    query = query_ref[...].astype(jnp.float32)
    nope = query[:, : QUAD * DN]
    rope = query[:, QUAD * DN :]
    grad = grad_ref[...].astype(jnp.float32)
    key_grads, value_grads, nope_grads, rope_grads = [], [], [], []
    for pair in range(2):
        lanes = slice(pair * 2 * DN, (pair + 1) * 2 * DN)
        key_cat = jnp.concatenate([keys[:, lanes], rope_ref[...]], axis=1)
        query_cat = pair_rows(nope, rope, pair)
        grad_cat = low(
            jnp.concatenate([lane_part(grad[:, lanes], DV, head) for head in range(2)], axis=0)
        )
        scores = matmul_right(key_cat, query_cat)
        prob_grads = matmul_right(values[:, lanes], grad_cat)
        probs_low, score_low = [], []
        for head in range(2):
            place = 2 * pair + head
            cut = slice(head * rows, (head + 1) * rows)
            probs = jnp.exp2(
                scores[:, cut] * exp_scale + bias_ref[...] - total_ref[0, place : place + 1, :]
            )
            mixed = probs * prob_grads[:, cut]
            dots = jnp.sum(mixed, axis=0, keepdims=True)
            score_grad = low(mixed - probs * dots)
            probs_low.append(low(probs))
            score_low.append(score_grad)
            left = jnp.concatenate(
                [turned_keys[place * DN : (place + 1) * DN], turned_ref[...]], axis=0
            )
            turned = matmul_plain(left, score_grad) * score_scale
            nope_grads.append(turned[:DN])
            upper, lower = turned[DN : DN + half], turned[DN + half :]
            rope_grads.append(upper * cos_ref[...] + lower * sin_ref[...])
            rope_grads.append(lower * cos_ref[...] - upper * sin_ref[...])
        value_grads.append(matmul_plain(jnp.concatenate(probs_low, axis=1), grad_cat))
        key_cat_grad = matmul_plain(jnp.concatenate(score_low, axis=1), query_cat)
        key_grads.append(key_cat_grad[:, : 2 * DN])
        rope_out[...] += key_cat_grad[:, 2 * DN :] * score_scale
    query_out[...] = low(jnp.concatenate(nope_grads + rope_grads, axis=0).T)
    key_grad = low(jnp.concatenate(key_grads, axis=1) * score_scale)
    value_grad = low(jnp.concatenate(value_grads, axis=1))
    key_up_out[...] = matmul_plain(flat_ref[...], key_grad)
    value_up_out[...] = matmul_plain(flat_ref[...], value_grad)
    latent_out[...] += matmul_right(key_grad, key_w[...]) + matmul_right(value_grad, value_w[...])


def attend_backward(query, grad, latent, latent_flat, rope_keys, rope_flat, bias, totals, cos_flat, sin_flat, key_w, value_w, quads):
    rows = query.shape[0]
    keys, width = latent.shape
    qw, kw, rw = QUAD * (DN + DR), QUAD * DN, QUAD * DR
    fixed = lambda j: (0, 0)
    step = lambda j: (0, j)
    flops = quads * (2 * keys * width * 6 * kw + 5 * 4 * 2 * keys * rows * 256)
    return pl.pallas_call(
        backward_kernel,
        grid=(quads,),
        in_specs=[
            pl.BlockSpec((rows, qw), step),
            pl.BlockSpec((rows, kw), step),
            pl.BlockSpec((keys, width), fixed),
            pl.BlockSpec((width, keys), fixed),
            pl.BlockSpec((keys, rw), fixed),
            pl.BlockSpec((DR, keys), fixed),
            pl.BlockSpec((keys, rows), fixed),
            pl.BlockSpec((1, QUAD, rows), lambda j: (j, 0, 0)),
            pl.BlockSpec((DR // 2, rows), fixed),
            pl.BlockSpec((DR // 2, rows), fixed),
            pl.BlockSpec((width, kw), step),
            pl.BlockSpec((width, kw), step),
        ],
        out_specs=[
            pl.BlockSpec((rows, qw), step),
            pl.BlockSpec((width, kw), step),
            pl.BlockSpec((width, kw), step),
            pl.BlockSpec((keys, width), fixed),
            pl.BlockSpec((keys, rw), fixed),
        ],
        out_shape=[
            jax.ShapeDtypeStruct((rows, quads * qw), jnp.bfloat16),
            jax.ShapeDtypeStruct((width, quads * kw), jnp.float32),
            jax.ShapeDtypeStruct((width, quads * kw), jnp.float32),
            jax.ShapeDtypeStruct((keys, width), jnp.float32),
            jax.ShapeDtypeStruct((keys, rw), jnp.float32),
        ],
        compiler_params=pltpu.CompilerParams(
            dimension_semantics=("arbitrary",), vmem_limit_bytes=48 * 2**20
        ),
        cost_estimate=pl.CostEstimate(
            flops=int(flops), bytes_accessed=25 * 2**20, transcendentals=quads * 4 * keys * rows
        ),
        name="attend_backward",
    )(query, grad, latent, latent_flat, rope_keys, rope_flat, bias, totals, cos_flat, sin_flat, key_w, value_w)


class LineSum:
    def __init__(self):
        self.count = lax.axis_size("ctx")
        self.me = lax.axis_index("ctx")
        self.hops = self.count // 2 - 1
        self.held = []
        self.stage = []
        self.queue = []

    def add(self, *pieces):
        for piece in pieces:
            self.queue.append(len(self.held))
            self.held.append(piece)
            self.stage.append(None)

    def busy(self):
        return bool(self.queue) or any(s is not None and s >= 0 for s in self.stage)

    def outer(self, hop):
        return (self.me == hop) | (self.me == self.count - 1 - hop)

    def sends(self):
        if self.queue:
            self.stage[self.queue.pop(0)] = 0
        self.plan, values = [], []
        at = {stage: item for item, stage in enumerate(self.stage) if stage is not None}
        last = self.count - 1
        for hop in range(self.hops):
            entering, leaving = at.get(hop), at.get(2 * self.hops - hop)
            inward = [(hop, hop + 1), (last - hop, last - hop - 1)]
            outward = [(to, source) for source, to in inward]
            both = entering is not None and leaving is not None
            if both and self.held[entering].shape == self.held[leaving].shape:
                self.plan.append((hop, entering, leaving, inward + outward))
                values.append(
                    jnp.where(self.outer(hop), self.held[entering], self.held[leaving])
                )
                continue
            if entering is not None:
                self.plan.append((hop, entering, None, inward))
                values.append(self.held[entering])
            if leaving is not None:
                self.plan.append((hop, None, leaving, outward))
                values.append(self.held[leaving])
        crossing = at.get(self.hops)
        if crossing is not None:
            self.plan.append(
                (None, crossing, None, [(self.hops, self.hops + 1), (self.hops + 1, self.hops)])
            )
            values.append(self.held[crossing])
        return values

    def move(self, values):
        return [lax.ppermute(value, "ctx", pairs) for value, (_, _, _, pairs) in zip(values, self.plan)]

    def absorb(self, values):
        for value, (hop, entering, leaving, _) in zip(values, self.plan):
            if entering is not None:
                self.held[entering] = low(add_up(self.held[entering], value))
            if leaving is not None:
                self.held[leaving] = jnp.where(self.outer(hop), value, self.held[leaving])
        for item, stage in enumerate(self.stage):
            if stage is not None:
                self.stage[item] = stage + 1 if stage < 2 * self.hops else None


def weight_kernel(fresh, *refs):
    first, second, first_rows, second_rows = refs[:4]
    half = first.shape[0] // 2
    total = matmul_plain(first[...], first_rows[...]) + matmul_plain(second[...], second_rows[...])
    if fresh:
        upper, lower = refs[4:]
        upper[...] = low(total[:half])
        lower[...] = low(total[half:])
    else:
        upper_in, lower_in, upper, lower = refs[4:]
        upper[...] = low(total[:half] + upper_in[...].astype(jnp.float32))
        lower[...] = low(total[half:] + lower_in[...].astype(jnp.float32))


def weight_sums(lefts, rights, place, held):
    rows = lefts[0].shape[0] // 2
    depth, width = rights[0].shape
    tile = 512 if width % 512 == 0 else width
    part = jax.ShapeDtypeStruct((rows // 2, width), jnp.bfloat16)
    part_spec = pl.BlockSpec((rows // 2, tile), lambda j: (0, j))
    return pl.pallas_call(
        functools.partial(weight_kernel, held is None),
        grid=(width // tile,),
        in_specs=[pl.BlockSpec((rows, depth), lambda j: (place, 0))] * 2
        + [pl.BlockSpec((depth, tile), lambda j: (0, j))] * 2
        + ([] if held is None else [part_spec] * 2),
        out_specs=[part_spec] * 2,
        out_shape=[part] * 2,
        compiler_params=pltpu.CompilerParams(
            dimension_semantics=("arbitrary",), vmem_limit_bytes=40 * 2**20
        ),
        cost_estimate=pl.CostEstimate(
            flops=4 * rows * depth * width,
            bytes_accessed=4 * (rows * depth + depth * width + rows * width),
            transcendentals=0,
        ),
        name="weight_sums",
    )(*lefts, *rights, *(held or ()))


def spread_line(rows):
    count = lax.axis_size("ctx")
    return [rows] + [
        lax.ppermute(rows, "ctx", [(i, (i + k) % count) for i in range(count)])
        for k in range(1, count)
    ]


def collect_line(parts):
    count = lax.axis_size("ctx")
    rows = parts.shape[0] // count
    total = parts[:rows].astype(jnp.float32)
    for k in range(1, count):
        got = lax.ppermute(
            low(parts[k * rows : (k + 1) * rows]), "ctx", [(i, (i - k) % count) for i in range(count)]
        )
        total = total + got.astype(jnp.float32)
    return total


def pad_columns(values, width):
    return jnp.pad(values, ((0, 0), (0, width - values.shape[1])))


def up_to(width):
    return (width + 127) // 128 * 128


def body(
    activations,
    cotangent,
    seq_length,
    block_order,
    attn_norm,
    query_down,
    query_norm,
    query_up,
    latent_down,
    latent_norm,
    latent_up,
    attn_out,
    mlp_norm,
    gate_weight,
    up_weight,
    down_weight,
):
    ctx_count = lax.axis_size("ctx")
    ctx_place = lax.axis_index("ctx")
    batches = activations.shape[1]
    local_rows = activations.shape[2]
    width = activations.shape[3]
    seq_rows = local_rows * ctx_count
    blocks = block_order.shape[0]
    block_size = seq_rows // blocks
    quads = query_up.shape[1] // (QUAD * (DN + DR))
    query_rank = query_down.shape[1]
    down_width = query_rank + KVR + DR
    bits = chip_bits()

    every_row = jnp.arange(seq_rows, dtype=jnp.int32)
    block_of = every_row // block_size
    placed = jnp.sum(
        jnp.where(
            block_of[:, None] == jnp.arange(blocks, dtype=jnp.int32)[None, :],
            block_order[None, :],
            0,
        ),
        axis=1,
    )
    stored_pos = placed * block_size + every_row % block_size
    near_pos = [
        lax.dynamic_slice_in_dim(
            stored_pos, (ctx_place - k) % ctx_count * local_rows, local_rows
        )
        for k in range(ctx_count)
    ]
    query_pos = near_pos[0]
    key_pos = jnp.concatenate(near_pos)
    local_cos, local_sin = rope_tables(query_pos, DR)
    half = DR // 2
    nothing = jnp.zeros_like(local_sin[:, :half])
    quad_cos = jnp.tile(local_cos, (1, QUAD))
    quad_ahead = jnp.tile(jnp.concatenate([-local_sin[:, :half], nothing], axis=1), (1, QUAD))
    quad_behind = jnp.tile(jnp.concatenate([nothing, local_sin[:, :half]], axis=1), (1, QUAD))
    lengths = seq_length[0]
    allowed = (key_pos[None, :, None] <= query_pos[None, None, :]) & (
        key_pos[None, :, None] < lengths[:, None, None]
    )
    bias = jnp.where(allowed, 0.0, lowest_score).astype(jnp.float32)

    shard_rows = query_down.shape[0]
    column = lambda gain: jnp.pad(gain[:, None], ((0, shard_rows - gain.shape[0]), (0, 0)))
    down_shard = pad_columns(
        jnp.concatenate(
            [query_down, latent_down]
            + [column(gain) for gain in (attn_norm, mlp_norm, query_norm, latent_norm)],
            axis=1,
        ),
        up_to(down_width + 4),
    )
    by_quad = query_up.reshape(-1, quads, QUAD, DN + DR)
    query_shard = jnp.concatenate(
        [
            by_quad[..., :DN].reshape(-1, quads, QUAD * DN),
            by_quad[..., DN:].reshape(-1, quads, QUAD * DR),
        ],
        axis=2,
    ).reshape(query_up.shape)
    by_head = latent_up.reshape(-1, H, DN + DV)
    latent_shard = jnp.concatenate(
        [by_head[..., :DN].reshape(-1, H * DN), by_head[..., DN:].reshape(-1, H * DV)], axis=1
    )
    out_half = attn_out.shape[0] // 2
    one_way = tuple(bits)
    other_way = tuple(bits[::-1])
    hold = lax.optimization_barrier
    rows = batches * local_rows
    lengths_live = query_pos[None, :] < lengths[:, None]
    live = lengths_live.astype(jnp.float32)[..., None]
    out_grad = cotangent[0].astype(jnp.float32) * live
    key_shard, value_shard = latent_shard[:, : H * DN], latent_shard[:, H * DN :]
    upper_out, lower_out = attn_out[:out_half], attn_out[out_half:]
    half_rows = local_rows // 2

    wave = (down_shard, key_shard, query_shard, value_shard)
    ways = (one_way, one_way, other_way, other_way)
    partner_weights = [flip(weight, 1) for weight in (gate_weight, up_weight, down_weight)]
    for place in range(len(bits)):
        moved = [flip(held, way[place]) for held, way in zip(wave, ways)]
        if place == 0:
            branch_grad = low(branch_scale * out_grad)
            moved, branch_grad, upper_out, lower_out = hold((moved, branch_grad, upper_out, lower_out))
        else:
            moved = hold(moved)
        wave = [jnp.concatenate([held, got]) for held, got in zip(wave, moved)]
        wave, branch_grad, upper_out, lower_out = hold((wave, branch_grad, upper_out, lower_out))
    crossed = [flip(held, 1) for held in wave]
    out_wave = (upper_out, lower_out)
    out_ways = (one_way, other_way)
    out_moved = [flip(held, way[0]) for held, way in zip(out_wave, out_ways)]
    crossed, wave = hold((crossed, wave))
    full_down, full_key, full_query, full_value = place_shards(
        [[(held, other, way)] for held, other, way in zip(wave, crossed, ways)]
    )
    gains = full_down[:, down_width : down_width + 4].astype(jnp.float32).T
    devices = lax.axis_size("fsdp")
    spread_gain = lambda gain, size: gain.reshape(devices, -1)[:, : size // devices].reshape(-1)
    attn_gain = gains[0]
    mlp_gain = gains[1]
    query_gain = spread_gain(gains[2], query_rank)
    latent_gain = spread_gain(gains[3], KVR)

    flat_inputs = activations[0].astype(jnp.float32).reshape(rows, width)
    first_normed, first_plain, first_inverse = rms_scale(flat_inputs, attn_gain)
    first_low = low(first_normed)
    down_raw = matmul_plain(first_low, full_down)
    query_mixed, query_plain, query_inverse = rms_scale(down_raw[:, :query_rank], query_gain)
    query_low = low(query_mixed)
    latent_raw = down_raw[:, query_rank:down_width]
    latent_mixed, latent_plain, latent_inverse = rms_scale(latent_raw[:, :KVR], latent_gain)
    both_cos = jnp.tile(local_cos, (batches, 1))
    both_sin = jnp.tile(local_sin, (batches, 1))
    key_rope_low = low(rope_apply(latent_raw[:, KVR:], both_cos, both_sin))
    near_own = jnp.concatenate([low(latent_mixed), key_rope_low], axis=1).reshape(
        batches, local_rows, KVR + DR
    )
    near_own, query_low, out_moved = hold((near_own, query_low, out_moved))
    near = spread_line(near_own)
    out_wave = [jnp.concatenate([held, got]) for held, got in zip(out_wave, out_moved)]
    near, out_wave, branch_grad = hold((near, out_wave, branch_grad))
    for place in range(1, len(bits) - 1):
        out_moved = [flip(held, way[place]) for held, way in zip(out_wave, out_ways)]
        out_wave = [jnp.concatenate([held, got]) for held, got in zip(out_wave, out_moved)]
    out_moved = [flip(held, way[-1]) for held, way in zip(out_wave, out_ways)]
    grad_wave = [branch_grad[None, :, :half_rows], branch_grad[None, :, half_rows:]]
    grad_moved = [flip(held, way[0]) for held, way in zip(grad_wave, out_ways)]
    near = jnp.stack(near, axis=1).reshape(batches, seq_rows, KVR + DR)
    latent_all = near[..., :KVR]
    key_rope_all = near[..., KVR:]
    quad_rope = jnp.tile(key_rope_all, (1, 1, QUAD))
    query_turned, mixed, log_total = attend_forward(
        query_low.reshape(batches, local_rows, query_rank),
        latent_all,
        quad_rope,
        bias,
        quad_cos,
        quad_ahead,
        quad_behind,
        full_query,
        full_key,
        full_value,
        quads,
    )
    out_moved, mixed, grad_wave, grad_moved = hold((out_moved, mixed, grad_wave, grad_moved))
    out_wave = [jnp.concatenate([held, got]) for held, got in zip(out_wave, out_moved)]
    out_crossed = [flip(held, 1) for held in out_wave]
    for place in range(1, len(bits)):
        grad_wave = [jnp.concatenate([held, got]) for held, got in zip(grad_wave, grad_moved)]
        grad_moved = [flip(held, way[place]) for held, way in zip(grad_wave, out_ways)]
    gate_all, up_all, down_all = (
        jnp.concatenate([weight, other])
        for weight, other in zip((gate_weight, up_weight, down_weight), partner_weights)
    )
    out_wave, out_crossed, gate_all, up_all, down_all = hold(
        (out_wave, out_crossed, gate_all, up_all, down_all)
    )
    (full_out,) = place_shards(
        [[(held, other, way) for held, other, way in zip(out_wave, out_crossed, out_ways)]]
    )
    mixed_flat = mixed.reshape(rows, H * DV)
    resid = flat_inputs + branch_scale * matmul_plain(mixed_flat, full_out)
    second_normed, second_plain, second_inverse = rms_scale(resid, mlp_gain)
    second_low = low(second_normed).reshape(batches, local_rows, width)
    of_batch = lambda values, batch: values[batch * local_rows : (batch + 1) * local_rows]
    second_low, grad_wave, grad_moved = hold((second_low, grad_wave, grad_moved))

    def start_rows(batch):
        return [second_low[batch, :half_rows], second_low[batch, half_rows:]]

    def spread_rows(wave, place):
        return [flip(held, way[place]) for held, way in zip(wave, out_ways)]

    def join_rows(wave, moved):
        return [jnp.concatenate([held, got]) for held, got in zip(wave, moved)]

    rows_wave = [start_rows(batch) for batch in range(batches)]
    rows_moved = spread_rows(rows_wave[0], 0)
    grad_wave = join_rows(grad_wave, grad_moved)
    grads_all = [
        jnp.concatenate(
            [held[:, batch].reshape(-1, width) for held in grad_wave]
        )
        for batch in range(batches)
    ]
    hidden_grads = [matmul_right(down_all, grads_all[0])]
    rows_moved, grads_all, hidden_grads = hold((rows_moved, grads_all, hidden_grads))
    rows_wave[0] = join_rows(rows_wave[0], rows_moved)
    for place in range(1, len(bits) - 1):
        rows_wave[0] = join_rows(rows_wave[0], spread_rows(rows_wave[0], place))
    rows_moved = spread_rows(rows_wave[0], -1)
    hidden_grads.append(matmul_right(down_all, grads_all[1]))
    rows_moved, hidden_grads, rows_wave = hold((rows_moved, hidden_grads, rows_wave))
    rows_all = [jnp.concatenate(join_rows(rows_wave[0], rows_moved))]

    def ffn_gate(batch):
        return matmul_right(gate_all, rows_all[batch])

    def ffn_up(batch, gate_value):
        up_value = matmul_right(up_all, rows_all[batch])
        sigmoid_gate = jax.nn.sigmoid(gate_value)
        silu_gate = gate_value * sigmoid_gate
        hidden_low = low(silu_gate * up_value)
        gate_grad = low(
            hidden_grads[batch]
            * up_value
            * sigmoid_gate
            * (1.0 + gate_value * (1.0 - sigmoid_gate))
        )
        up_grad = low(hidden_grads[batch] * silu_gate)
        return hidden_low, gate_grad, up_grad

    def scatter_first(parts):
        quarter = parts.shape[0] // 4
        first, second = parts[: 2 * quarter], parts[2 * quarter :]
        return (
            [first[:quarter], second[:quarter]],
            [flip(first[quarter:], bits[-1]), flip(second[quarter:], bits[0])],
        )

    def scatter_next(kept, got, place):
        joined = [low(add_up(held, value)) for held, value in zip(kept, got)]
        half = joined[0].shape[0] // 2
        moved = [
            flip(joined[0][half:], bits[-1 - place]),
            flip(joined[1][half:], bits[place]),
        ]
        return [held[:half] for held in joined], moved

    def scatter_mid(kept, got):
        for place in range(1, len(bits) - 1):
            kept, got = scatter_next(kept, got, place)
        return scatter_next(kept, got, len(bits) - 1)

    def scatter_end(kept, got):
        return jnp.concatenate([add_up(held, value) for held, value in zip(kept, got)])

    rows_moved = spread_rows(rows_wave[1], 0)
    gate_value = ffn_gate(0)
    rows_moved, gate_value, rows_all = hold((rows_moved, gate_value, rows_all))
    rows_wave[1] = join_rows(rows_wave[1], rows_moved)
    for place in range(1, len(bits) - 1):
        rows_wave[1] = join_rows(rows_wave[1], spread_rows(rows_wave[1], place))
    rows_moved = spread_rows(rows_wave[1], -1)
    ffn_parts = [ffn_up(0, gate_value)]
    branch_part = low(matmul_left(ffn_parts[0][0], down_all))
    rows_moved, ffn_parts, branch_part, rows_wave[1] = hold(
        (rows_moved, ffn_parts, branch_part, rows_wave[1])
    )
    rows_all.append(jnp.concatenate(join_rows(rows_wave[1], rows_moved)))
    first_out = scatter_first(branch_part)
    gate_value = ffn_gate(1)
    first_out, gate_value, rows_all = hold((first_out, gate_value, rows_all))
    first_out = scatter_mid(*first_out)
    ffn_parts.append(ffn_up(1, gate_value))
    first_out, ffn_parts = hold((first_out, ffn_parts))

    def rows_grad_of(batch):
        return low(
            matmul_left(ffn_parts[batch][1], gate_all) + matmul_left(ffn_parts[batch][2], up_all)
        )

    outputs = [low(of_batch(resid, 0) + branch_scale * scatter_end(*first_out))]
    rows_grad = rows_grad_of(0)
    outputs, rows_grad, ffn_parts = hold((outputs, rows_grad, ffn_parts))
    first_grad_way = scatter_first(rows_grad)
    gate_grads = [parts[1] for parts in ffn_parts]
    up_grads = [parts[2] for parts in ffn_parts]
    hiddens = [parts[0] for parts in ffn_parts]
    jobs = [(hiddens, grads_all), (gate_grads, rows_all), (up_grads, rows_all)]
    away = [weight_sums(lefts, rights, 1, None) for lefts, rights in jobs]
    first_grad_way, away, ffn_parts = hold((first_grad_way, away, ffn_parts))
    first_grad_way = scatter_mid(*first_grad_way)
    back = [[flip(part, 1) for part in parts] for parts in away]
    branch_part = low(matmul_left(ffn_parts[1][0], down_all))
    first_grad_way, back, branch_part = hold((first_grad_way, back, branch_part))
    second_out = scatter_first(branch_part)
    own = [weight_sums(*jobs[i], 0, back[i]) for i in range(1)]
    line = LineSum()
    line.add(*own[0])
    sends, second_out, first_grad_way, ffn_parts = hold(
        (line.sends(), second_out, first_grad_way, ffn_parts)
    )

    got = line.move(sends)
    second_out = scatter_mid(*second_out)
    own += [weight_sums(*jobs[i], 0, back[i]) for i in range(1, 3)]
    rows_grad = rows_grad_of(1)
    got, own, rows_grad, second_out = hold((got, own, rows_grad, second_out))
    line.absorb(got)
    line.add(*own[1], *own[2])

    def grads_begin(batch, second_grad):
        second_back, mlp_gain_grad = rms_back(
            second_grad, of_batch(second_plain, batch), of_batch(second_inverse, batch), mlp_gain
        )
        resid_grad = out_grad[batch] + second_back
        attn_grad = low(branch_scale * resid_grad)
        mixed_grad = low(matmul_right(attn_grad, full_out))
        return resid_grad, attn_grad, mixed_grad, mlp_gain_grad

    def grads_attend(batch, mixed_grad):
        query_raw_grad, key_up_part, value_up_part, latent_grad_all, rope_grad_all = attend_backward(
            query_turned[batch],
            mixed_grad,
            latent_all[batch],
            latent_all[batch].T,
            quad_rope[batch],
            key_rope_all[batch].T,
            bias[batch],
            log_total[batch],
            local_cos[:, :half].T,
            local_sin[:, :half].T,
            full_key,
            full_value,
            quads,
        )
        key_rope_grad = rope_grad_all.reshape(seq_rows, QUAD, DR).sum(axis=1)
        latent_part = low(jnp.concatenate([latent_grad_all, key_rope_grad], axis=1))
        return query_raw_grad, key_up_part, value_up_part, latent_part

    def grads_end(batch, query_raw_grad, collected, resid_grad):
        latent_back, latent_gain_grad = rms_back(
            collected[:, :KVR], of_batch(latent_plain, batch), of_batch(latent_inverse, batch), latent_gain
        )
        latent_raw_grad = low(
            jnp.concatenate(
                [latent_back, rope_back(collected[:, KVR:], local_cos, local_sin)], axis=-1
            )
        )
        query_mixed_grad = matmul_right(query_raw_grad, full_query)
        query_back, query_gain_grad = rms_back(
            query_mixed_grad, of_batch(query_plain, batch), of_batch(query_inverse, batch), query_gain
        )
        down_grad = pad_columns(
            jnp.concatenate([low(query_back), latent_raw_grad], axis=1), full_down.shape[1]
        )
        first_grad = matmul_right(down_grad, full_down)
        first_back, attn_gain_grad = rms_back(
            first_grad, of_batch(first_plain, batch), of_batch(first_inverse, batch), attn_gain
        )
        return low(resid_grad + first_back), down_grad, attn_gain_grad, query_gain_grad, latent_gain_grad

    sends, rows_grad, first_grad_way, second_out = hold(
        (line.sends(), rows_grad, first_grad_way, second_out)
    )
    got = line.move(sends)
    second_grad_way = scatter_first(rows_grad)
    begun = [grads_begin(0, scatter_end(*first_grad_way))]
    outputs.append(low(of_batch(resid, 1) + branch_scale * scatter_end(*second_out)))
    got, begun, second_grad_way, outputs = hold((got, begun, second_grad_way, outputs))
    line.absorb(got)

    sends, second_grad_way, begun = hold((line.sends(), second_grad_way, begun))
    got = line.move(sends)
    second_grad_way = scatter_mid(*second_grad_way)
    attended = [grads_attend(0, begun[0][2])]
    got, attended, second_grad_way, begun = hold((got, attended, second_grad_way, begun))
    line.absorb(got)

    sends, second_grad_way, attended = hold((line.sends(), second_grad_way, attended))
    got = line.move(sends)
    begun.append(grads_begin(1, scatter_end(*second_grad_way)))
    collected = [collect_line(attended[0][3])]
    out_sum = low(matmul_left(mixed_flat, jnp.concatenate([begun[0][1], begun[1][1]])))
    got, begun, collected, out_sum = hold((got, begun, collected, out_sum))
    line.absorb(got)
    in_shards = lambda values: values.reshape(devices, -1, values.shape[-1])
    back_way = [1] + bits[::-1]
    back_other = [1] + bits
    out_sum = in_shards(out_sum)
    out_steps = [
        ScatterWhole(out_sum[:, :out_half], back_way),
        ScatterWhole(out_sum[:, out_half:], back_other),
    ]

    sends, begun, out_sends, attended = hold(
        (line.sends(), begun, [job.send() for job in out_steps], attended)
    )
    got = line.move(sends)
    out_got = [job.move(value) for job, value in zip(out_steps, out_sends)]
    attended.append(grads_attend(1, begun[1][2]))
    got, attended, out_got = hold((got, attended, out_got))
    line.absorb(got)
    for job, value in zip(out_steps, out_got):
        job.absorb(value)

    sends, attended, out_sends = hold(
        (line.sends(), attended, [job.send() for job in out_steps])
    )
    got = line.move(sends)
    out_got = [job.move(value) for job, value in zip(out_steps, out_sends)]
    collected.append(collect_line(attended[1][3]))
    latent_up_sum = low(
        jnp.concatenate([attended[0][1] + attended[1][1], attended[0][2] + attended[1][2]], axis=1)
    )
    query_sum = low(matmul_left(query_low, jnp.concatenate([attended[0][0], attended[1][0]])))
    ended = [
        grads_end(batch, attended[batch][0], collected[batch], begun[batch][0])
        for batch in range(batches)
    ]
    input_grads = [ended[batch][0] for batch in range(batches)]
    gain_sums = [
        ended[0][2] + ended[1][2],
        begun[0][3] + begun[1][3],
        ended[0][3] + ended[1][3],
        ended[0][4] + ended[1][4],
    ]
    places = lax.broadcasted_iota(jnp.int32, full_down.shape, 1) - down_width
    down_sum = matmul_left(first_low, jnp.concatenate([ended[0][1], ended[1][1]]))
    gathered_gain = lambda gain: jnp.pad(
        gain.reshape(devices, -1), ((0, 0), (0, shard_rows - gain.shape[0] // devices))
    ).reshape(-1)
    gain_columns = gain_sums[:2] + [gathered_gain(gain) for gain in gain_sums[2:]]
    for place, gain in enumerate(gain_columns):
        down_sum = jnp.where(places == place, gain[:, None], down_sum)
    down_sum = low(down_sum)
    got, out_got, latent_up_sum, query_sum, down_sum = hold(
        (got, out_got, latent_up_sum, query_sum, down_sum)
    )
    line.absorb(got)
    for job, value in zip(out_steps, out_got):
        job.absorb(value)

    steps = [
        ScatterWhole(in_shards(down_sum), back_way),
        ScatterWhole(in_shards(query_sum), back_other),
        ScatterWhole(in_shards(latent_up_sum), back_way),
    ]
    while line.busy() or steps:
        jobs = [job for job in out_steps + steps if job.order]
        sends, values = hold((line.sends(), [job.send() for job in jobs]))
        got = line.move(sends)
        values = [job.move(value) for job, value in zip(jobs, values)]
        got, values = hold((got, values))
        line.absorb(got)
        for job, value in zip(jobs, values):
            job.absorb(value)
        if out_steps and not any(job.order for job in out_steps):
            line.add(jnp.concatenate([job.held[0] for job in out_steps]))
            out_steps = []
        if steps and not any(job.order for job in steps):
            line.add(*[job.held[0] for job in steps])
            steps = []
    totals = [total.astype(jnp.float32) for total in line.held]
    ffn_totals = [jnp.concatenate(totals[2 * i : 2 * i + 2]) for i in (1, 2, 0)]
    out_total, down_total, query_total, latent_total = totals[6:]
    by_quad = query_total.reshape(-1, quads, QUAD * (DN + DR))
    query_up_total = jnp.concatenate(
        [
            by_quad[..., : QUAD * DN].reshape(-1, quads, QUAD, DN),
            by_quad[..., QUAD * DN :].reshape(-1, quads, QUAD, DR),
        ],
        axis=-1,
    ).reshape(query_up.shape)
    latent_up_total = jnp.concatenate(
        [
            latent_total[:, : H * DN].reshape(-1, H, DN),
            latent_total[:, H * DN :].reshape(-1, H, DV),
        ],
        axis=-1,
    ).reshape(latent_up.shape)
    return (
        jnp.stack(outputs)[None],
        jnp.stack(input_grads)[None],
        down_total[:, down_width],
        down_total[:, :query_rank],
        down_total[: query_norm.shape[0], down_width + 2],
        query_up_total,
        down_total[:, query_rank:down_width],
        down_total[: latent_norm.shape[0], down_width + 3],
        latent_up_total,
        out_total,
        down_total[:, down_width + 1],
        ffn_totals[0],
        ffn_totals[1],
        ffn_totals[2],
    )


def solution(mesh):
    placed = (
        P("fsdp", None, "ctx", None),
        P("fsdp", None, "ctx", None),
        P("fsdp", None),
        P(),
        P("fsdp"),
        P("fsdp", None),
        P("fsdp"),
        P("fsdp", None),
        P("fsdp", None),
        P("fsdp"),
        P("fsdp", None),
        P("fsdp", None),
        P("fsdp"),
        P("fsdp", None),
        P("fsdp", None),
        P("fsdp", None),
    )
    return jax.shard_map(
        body,
        mesh=mesh,
        in_specs=placed,
        out_specs=(
            P("fsdp", None, "ctx", None),
            P("fsdp", None, "ctx", None),
            P("fsdp"),
            P("fsdp", None),
            P("fsdp"),
            P("fsdp", None),
            P("fsdp", None),
            P("fsdp"),
            P("fsdp", None),
            P("fsdp", None),
            P("fsdp"),
            P("fsdp", None),
            P("fsdp", None),
            P("fsdp", None),
        ),
        check_vma=False,
    )
```

time: 2500 us -> 1380 us (0.55)
  waiting for transfers between devices: 1240 us -> 341 us
  matrix products: 782 us -> 239 us
  Pallas kernels: 0 us -> 236 us
  starting transfers between devices: 2.3 us -> 143 us
  blocking collectives: 122 us -> 0 us
  local copies, waits for them, and re-layouts: 61.5 us -> 152 us
    reduce_scatter x12 -> x0, waiting for transfers between devices: 515 us -> none  [the longest x2 275 us: body(): lax.psum_scatter(parts[0], 'fsdp', scatter_dimension=0, tiled=True)]
    psum x1 -> x0, waiting for transfers between devices: 477 us -> none  [body(): lax.psum(sums[1].astype(jnp.bfloat16), 'ctx').astype(jnp.float32)]
    ppermute x0 -> x105, waiting for transfers between devices: none -> 341 us  [the longest x70 223 us: flip(): return lax.ppermute(values, 'fsdp', [(i, i ^ bit) for i in range(count)])]
    dot_general x18 -> x0, matrix products: 311 us -> none  [the longest x2 58.4 us: body(): jnp.einsum('ihd,jhd->hij', mixed_grad, value_rows, preferred_element_type...]
    all_gather x9 -> x0, waiting for transfers between devices: 243 us -> none  [the longest x2 123 us: body(): lax.all_gather(second_low, 'fsdp', axis=0, tiled=True)]
    pallas_call x0 -> x11, Pallas kernels: none -> 236 us  [the longest x2 93 us: attend_backward(): pl.pallas_call(backward_kernel, grid=(quads,), in_specs=[pl.BlockSpec((ro...]
    dot_general x16 -> x2, matrix products: 162 us -> 16.3 us  [matmul_plain(): return jnp.dot(left, right, preferred_element_type=jnp.float32)]
    ppermute x0 -> x105, starting transfers between devices: none -> 143 us  [the longest x26 67.3 us: move(): lax.ppermute(value, 'ctx', pairs)]
  transfers between devices with their start and end apart: 23 -> 105, of which waited for: 12 -> 34; matrix products, arithmetic and copies ran while one was open for 27% -> 33% of each run, Pallas kernels for 0% -> 17%
where the time goes in v1:
time: 1380 us; the launch traced here: 1360 us
  waiting for transfers between devices  341 us (25%)
  other arithmetic  248 us (18%)
  matrix products  239 us (17%)
  Pallas kernels  236 us (17%)
  local copies, waits for them, and re-layouts  152 us (11%)
  starting transfers between devices  143 us (10%)
    ppermute x70, waiting for transfers between devices, flip(): return lax.ppermute(values, 'fsdp', [(i, i ^ bit) for i in range(count)])  223 us
    dot_general x9, matrix products, matmul_left(): lax.dot_general(left, right, (((0,), (0,)), ((), ())), preferred_element_...  114 us
    dot_general x12, matrix products, matmul_right(): lax.dot_general(left, right, (((1,), (1,)), ((), ())), preferred_element_...  109 us
    convert_element_type x45, other arithmetic, low(): return values.astype(jnp.bfloat16)  98.4 us
    pallas_call x2, Pallas kernels, attend_backward(): pl.pallas_call(backward_kernel, grid=(quads,), in_specs=[pl.BlockSpec((ro...  93 us
    ppermute x26, waiting for transfers between devices, move(): lax.ppermute(value, 'ctx', pairs)  79.5 us
    pallas_call x6, Pallas kernels, weight_sums(): pl.pallas_call(functools.partial(weight_kernel, held is None), grid=(widt...  74 us
    ppermute x26, starting transfers between devices, move(): lax.ppermute(value, 'ctx', pairs)  67.3 us
  transfers between devices with their start and end apart: 105, of which 34 were waited for; matrix products, arithmetic and copies ran while one was open for 33% of the time, Pallas kernels for 17%

profile of v1, /device:TPU:0, one launch (start us, length us, event | category | flops | bytes accessed | tf_op | source)
XLA Modules:
  0.0 1363.4 jit_solution(11407666368958310467)
XLA Ops:
  25.1 5.7 convert_multiply_fusion
  32.9 5.8 collective-permute-done.3
  49.6 35.1 %collective-permute-done.5 = bf16[64,2560]{1,0:T(8,128)(2,1)S(1)} collective-permute-done((bf16[64,2560]{1,0:T(8,128)(2,1)S(1)}, bf16[64,2560]{1,0:T(8,128)(2,1)S(1)}, u32[]{:S(2)}, u32[]{:S(2)}) %collective-permute-start.5) | collective-permute-done | bytes 327712 | tf_op jit(solution)/shard_map/ppermute | solution.py:86
  103.0 7.3 pad_maximum_fusion
  110.3 7.3 pad_maximum_fusion.1
  118.7 7.3 pad_maximum_fusion.2
  128.6 7.0 place_shards.2
  139.6 5.9 fusion.38
  164.8 11.7 collective-permute-done.15
  187.2 52.3 %attend_forward.1 = (bf16[2,256,3840]{2,1,0:T(8,128)(2,1)}, bf16[2,256,2560]{2,1,0:T(8,128)(2,1)}, f32[2,10,4,256]{3,2,1,0:T(4,128)S(1)}) custom-call(bf16[2,256,768]{2,1,0:T(8,128)(2,1)S(1)} %bitcast.235, bf16[2,1024,256]{2,1,0:T(8,128)(2,1)S(1)} %copy.256.latent_ref, bf16[2,1024,128]{2,1,0:T(8,128)(2,1)S(1)} %copy.257.rope_ref, ...), custom_call_target="tpu_custom_call" | custom-call | flops 29863444480 | bytes 41943040 | tf_op jit(solution)/shard_map/attend_forward/pallas_call | solution.py:236
  264.1 9.6 place_shards.3
  273.6 10.4 multiply_reduce_fusion
  288.0 32.4 %collective-permute-done.26 = bf16[2,2,128,2560]{3,2,1,0:T(8,128)(2,1)S(1)} collective-permute-done((bf16[2,2,128,2560]{3,2,1,0:T(8,128)(2,1)S(1)}, bf16[2,2,128,2560]{3,2,1,0:T(8,128)(2,1)S(1)}, u32[]{:S(2)}, u32[]{:S(2)}) %collective-permute-start.26) | collective-permute-done | bytes 2621472 | tf_op jit(solution)/shard_map/ppermute | solution.py:86
  329.6 11.8 fusion.73
  351.1 12.9 fusion.105
  364.0 13.0 collective-permute-done.30
  386.3 12.8 fusion.106
  400.7 12.4 fusion.107
  413.1 8.9 multiply_convert_fusion.3
  422.0 15.3 %convolution_convert_fusion.3 = bf16[1024,2560]{1,0:T(8,128)(2,1)S(1)} fusion(bf16[1600,1024]{1,0:T(8,128)(2,1)S(1)} %get-tuple-element.465.refs_0_, bf16[1600,2560]{1,0:T(8,128)(2,1)} %pad_maximum_fusion.2), kind=kOutput, calls=%fused_computation.31 | convolution fusion | flops 8391229440 | bytes 16711680 | tf_op jit(solution)/shard_map/dot_general | solution.py:73
  448.7 12.4 fusion.108
  461.1 6.0 collective-permute-done.36
  474.4 14.4 %fusion.109 = f32[1600,1024]{1,0:T(8,128)} fusion(bf16[1600,2560]{1,0:T(8,128)(2,1)} %pad_maximum_fusion.1, bf16[1024,2560]{1,0:T(8,128)(2,1)} %constant_dynamic-update-slice_fusion.20.refs_3_), kind=kOutput, calls=%fused_computation.380 | convolution fusion | flops 8388608000 | bytes 19988480 | tf_op jit(solution)/shard_map/dot_general | solution.py:79
  488.7 9.1 multiply_convert_fusion
  497.9 18.7 %fusion.110 = f32[1024,2560]{1,0:T(8,128)} fusion(bf16[1600,1024]{1,0:T(8,128)(2,1)S(1)} %get-tuple-element.476.refs_0_, bf16[1600,2560]{1,0:T(8,128)(2,1)} %pad_maximum_fusion.1), kind=kOutput, calls=%fused_computation.381 | convolution fusion | flops 8388608000 | bytes 21954560 | tf_op jit(solution)/shard_map/dot_general | solution.py:73
  520.8 15.6 %add_convert_fusion.1 = bf16[1024,2560]{1,0:T(8,128)(2,1)} fusion(f32[1024,2560]{1,0:T(8,128)} %fusion.110, bf16[1600,1024]{1,0:T(8,128)(2,1)S(1)} %get-tuple-element.471.refs_0_, bf16[1600,2560]{1,0:T(8,128)(2,1)} %pad_maximum_fusion), kind=kOutput, calls=%fused_computation.7 | convolution fusion | flops 8393850880 | bytes 27197440 | tf_op jit(solution)/shard_map/dot_general | solution.py:73
  543.5 11.2 weight_sums.7
  556.1 12.0 weight_sums.8
  569.4 12.7 weight_sums.6
  601.2 6.3 collective-permute-done.43
  608.0 13.3 convolution_convert_fusion.2
  626.6 12.7 weight_sums.9
  639.3 12.1 weight_sums.10
  654.5 13.4 weight_sums.11
  668.0 9.3 collective-permute-start.52
  677.3 15.0 %fusion.111 = f32[1024,2560]{1,0:T(8,128)} fusion(bf16[1600,1024]{1,0:T(8,128)(2,1)S(1)} %copy-done.14, bf16[1600,2560]{1,0:T(8,128)(2,1)} %pad_maximum_fusion.1), kind=kOutput, calls=%fused_computation.382 | convolution fusion | flops 8388608000 | bytes 21954560 | tf_op jit(solution)/shard_map/dot_general | solution.py:73
  700.8 14.5 %add_convert_fusion = bf16[1024,2560]{1,0:T(8,128)(2,1)S(1)} fusion(f32[1024,2560]{1,0:T(8,128)} %fusion.111, bf16[1600,1024]{1,0:T(8,128)(2,1)S(1)} %copy-done.12, bf16[1600,2560]{1,0:T(8,128)(2,1)} %pad_maximum_fusion), kind=kOutput, calls=%fused_computation.6 | convolution fusion | flops 8393850880 | bytes 27197440 | tf_op jit(solution)/shard_map/dot_general | solution.py:73
  722.4 5.9 collective-permute-start.55
  744.9 8.7 convolution_convert_fusion.5.grad_ref
  753.6 12.8 collective-permute-done.57
  793.1 46.4 %attend_backward.2 = (bf16[256,3840]{1,0:T(8,128)(2,1)}, f32[256,2560]{1,0:T(8,128)}, f32[256,2560]{1,0:T(8,128)}, f32[1024,256]{1,0:T(8,128)S(1)}, f32[1024,128]{1,0:T(8,128)S(1)}) custom-call(bf16[256,3840]{1,0:T(8,128)(2,1)} %get-tuple-element.869.query_ref, bf16[256,2560]{1,0:T(8,128)(2,1)S(1)} %convolution_convert_fusion.5.grad_ref, ...), custom_call_target="tpu_custom_call" | custom-call | flops 34896609280 | bytes 26214400 | tf_op jit(solution)/shard_map/attend_backward/pallas_call | solution.py:341
  870.8 10.0 convolution_convert_fusion
  880.8 8.7 convolution_convert_fusion.4.grad_ref
  889.5 17.3 %collective-permute-done.67 = bf16[256,288]{1,0:T(8,128)(2,1)S(1)} collective-permute-done((bf16[256,288]{1,0:T(8,128)(2,1)}, bf16[256,288]{1,0:T(8,128)(2,1)S(1)}, u32[]{:S(2)}, u32[]{:S(2)}) %collective-permute-start.67) | collective-permute-done | bytes 147488 | tf_op jit(solution)/shard_map/ppermute | solution.py:501
  906.8 8.3 collective-permute-done.66
  920.4 5.6 fusion.77
  942.6 46.6 %attend_backward.3 = (bf16[256,3840]{1,0:T(8,128)(2,1)}, f32[256,2560]{1,0:T(8,128)}, f32[256,2560]{1,0:T(8,128)}, f32[1024,256]{1,0:T(8,128)S(1)}, f32[1024,128]{1,0:T(8,128)S(1)}) custom-call(bf16[256,3840]{1,0:T(8,128)(2,1)} %get-tuple-element.868.query_ref, bf16[256,2560]{1,0:T(8,128)(2,1)S(1)} %convolution_convert_fusion.4.grad_ref, ...), custom_call_target="tpu_custom_call" | custom-call | flops 34896609280 | bytes 26214400 | tf_op jit(solution)/shard_map/attend_backward/pallas_call | solution.py:341
  1006.0 5.5 broadcast_select_fusion.6
  1040.2 5.3 fusion.69
  1045.7 5.9 multiply_reduce_fusion.2
  1052.0 6.4 fusion.3
  1058.4 14.9 %collective-permute-done.77 = bf16[1,2,160,2560]{3,2,1,0:T(8,128)(2,1)} collective-permute-done((bf16[1,2,160,2560]{3,2,1,0:T(8,128)(2,1)}, bf16[1,2,160,2560]{3,2,1,0:T(8,128)(2,1)}, u32[]{:S(2)}, u32[]{:S(2)}) %collective-permute-start.77) | collective-permute-done | bytes 1638432 | tf_op jit(solution)/shard_map/ppermute | solution.py:86
  1098.0 13.1 collective-permute-done.81
  1116.1 15.4 %collective-permute-done.82 = bf16[1,1,160,2560]{3,2,0,1:T(8,128)(2,1)S(1)} collective-permute-done((bf16[1,1,160,2560]{3,2,0,1:T(8,128)(2,1)S(1)}, bf16[1,1,160,2560]{3,2,0,1:T(8,128)(2,1)S(1)}, u32[]{:S(2)}, u32[]{:S(2)}) %collective-permute-start.82) | collective-permute-done | bytes 819232 | tf_op jit(solution)/shard_map/ppermute | solution.py:86
  1164.4 7.7 collective-permute-start.86
  1179.6 39.7 %collective-permute-done.90 = bf16[1,2,32,5120]{3,2,1,0:T(8,128)(2,1)} collective-permute-done((bf16[1,2,32,5120]{3,2,1,0:T(8,128)(2,1)}, bf16[1,2,32,5120]{3,2,1,0:T(8,128)(2,1)}, u32[]{:S(2)}, u32[]{:S(2)}) %collective-permute-start.90) | collective-permute-done | bytes 655392 | tf_op jit(solution)/shard_map/ppermute | solution.py:86
  1239.4 19.0 %collective-permute-done.94 = bf16[1,1,32,5120]{3,2,1,0:T(8,128)(2,1)S(1)} collective-permute-done((bf16[1,1,32,5120]{3,2,1,0:T(8,128)(2,1)S(1)}, bf16[1,1,32,5120]{3,2,1,0:T(8,128)(2,1)S(1)}, u32[]{:S(2)}, u32[]{:S(2)}) %collective-permute-start.94) | collective-permute-done | bytes 327712 | tf_op jit(solution)/shard_map/ppermute | solution.py:86
  1265.0 6.0 collective-permute-start.95
  1271.2 13.0 collective-permute-done.95
  1284.2 13.4 collective-permute-done.96
  1300.1 11.8 collective-permute-done.97
  1312.2 5.6 collective-permute-start.99
  1322.4 11.2 collective-permute-done.100
  1340.3 10.3 collective-permute-done.102
  (890 shorter events, 491.1 us)
Async XLA Ops:
  6.4 32.3 %collective-permute-start = (bf16[320,1152]{1,0:T(8,128)(2,1)S(1)}, bf16[320,1152]{1,0:T(8,128)(2,1)}, u32[]{:S(2)}, u32[]{:S(2)}) collective-permute-start(bf16[320,1152]{1,0:T(8,128)(2,1)S(1)} %pad.31), channel_id=1, source_target_pairs={{0,2},{1,3},{2,0},{3,1},{4,6},{5,7},{6,4},{7,5},{8,10},{9,11},{10,... | collective-permute-start | bytes 2211848 | tf_op jit(solution)/shard_map/ppermute | solution.py:86
  20.9 81.6 %collective-permute-start.23 = (bf16[800,2560]{1,0:T(8,128)(2,1)}, bf16[800,2560]{1,0:T(8,128)(2,1)}, u32[]{:S(2)}, u32[]{:S(2)}) collective-permute-start(bf16[800,2560]{1,0:T(8,128)(2,1)} %param.29), channel_id=1, source_target_pairs={{0,1},{1,0},{2,3},{3,2},{4,5},{5,4},{6,7},{7,6},{8,9},{9,8},{10,11... | collective-permute-start | bytes 12288008 | tf_op jit(solution)/shard_map/ppermute | solution.py:86
  32.4 77.9 %collective-permute-start.24 = (bf16[800,2560]{1,0:T(8,128)(2,1)}, bf16[800,2560]{1,0:T(8,128)(2,1)}, u32[]{:S(2)}, u32[]{:S(2)}) collective-permute-start(bf16[800,2560]{1,0:T(8,128)(2,1)} %param.30), channel_id=1, source_target_pairs={{0,1},{1,0},{2,3},{3,2},{4,5},{5,4},{6,7},{7,6},{8,9},{9,8},{10,11... | collective-permute-start | bytes 12288008 | tf_op jit(solution)/shard_map/ppermute | solution.py:86
  44.6 49.0 %collective-permute-start.4 = (bf16[640,1152]{1,0:T(8,128)(2,1)}, bf16[640,1152]{1,0:T(8,128)(2,1)}, u32[]{:S(2)}, u32[]{:S(2)}) collective-permute-start(bf16[640,1152]{1,0:T(8,128)(2,1)} %pad_maximum_fusion.14), channel_id=1, source_target_pairs={{0,4},{1,5},{2,6},{3,7},{4,0},{5,1},{6,2},{7,3},{8,12},{9,13},{10,... | collective-permute-start | bytes 4423688 | tf_op jit(solution)/shard_map/ppermute | solution.py:86
  46.3 47.3 %collective-permute-start.6 = (bf16[192,3840]{1,0:T(8,128)(2,1)}, bf16[192,3840]{1,0:T(8,128)(2,1)}, u32[]{:S(2)}, u32[]{:S(2)}) collective-permute-start(bf16[192,3840]{1,0:T(8,128)(2,1)} %pad_maximum_fusion.15), channel_id=1, source_target_pairs={{0,2},{1,3},{2,0},{3,1},{4,6},{5,7},{6,4},{7,5},{8,10},{9,11},{10,... | collective-permute-start | bytes 4423688 | tf_op jit(solution)/shard_map/ppermute | solution.py:86
  48.1 36.6 %collective-permute-start.5 = (bf16[64,2560]{1,0:T(8,128)(2,1)S(1)}, bf16[64,2560]{1,0:T(8,128)(2,1)S(1)}, u32[]{:S(2)}, u32[]{:S(2)}) collective-permute-start(bf16[64,2560]{1,0:T(8,128)(2,1)S(1)} %get-tuple-element.365), channel_id=1, source_target_pairs={{0,4},{1,5},{2,6},{3,7},{4,0},{5,1},{6,2},{7,3},{8,12},{9,13},{10,... | collective-permute-start | bytes 983048 | tf_op jit(solution)/shard_map/ppermute | solution.py:86
  92.8 24.7 %collective-permute-start.25 = (bf16[800,2560]{1,0:T(8,128)(2,1)}, bf16[800,2560]{1,0:T(8,128)(2,1)}, u32[]{:S(2)}, u32[]{:S(2)}) collective-permute-start(bf16[800,2560]{1,0:T(8,128)(2,1)} %param.31), channel_id=1, source_target_pairs={{0,1},{1,0},{2,3},{3,2},{4,5},{5,4},{6,7},{7,6},{8,9},{9,8},{10,11... | collective-permute-start | bytes 12288008 | tf_op jit(solution)/shard_map/ppermute | solution.py:86
  102.0 25.5 %collective-permute-start.8 = (bf16[1280,1152]{1,0:T(8,128)(2,1)}, bf16[1280,1152]{1,0:T(8,128)(2,1)}, u32[]{:S(2)}, u32[]{:S(2)}) collective-permute-start(bf16[1280,1152]{1,0:T(8,128)(2,1)} %pad_maximum_fusion.5.refs_0_), channel_id=1, source_target_pairs={{0,1},{1,0},{2,3},{3,2},{4,5},{5,4},{6,7},{7,6},{8,9},{9,8},{10,11... | collective-permute-start | bytes 8847368 | tf_op jit(solution)/shard_map/ppermute | solution.py:86
  102.5 23.5 %collective-permute-start.9 = (bf16[128,2560]{1,0:T(8,128)(2,1)}, bf16[128,2560]{1,0:T(8,128)(2,1)}, u32[]{:S(2)}, u32[]{:S(2)}) collective-permute-start(bf16[128,2560]{1,0:T(8,128)(2,1)} %pad_maximum_fusion.21.refs_2_), channel_id=1, source_target_pairs={{0,1},{1,0},{2,3},{3,2},{4,5},{5,4},{6,7},{7,6},{8,9},{9,8},{10,11... | collective-permute-start | bytes 1966088 | tf_op jit(solution)/shard_map/ppermute | solution.py:86
  102.5 25.0 %collective-permute-start.10 = (bf16[384,3840]{1,0:T(8,128)(2,1)S(1)}, bf16[384,3840]{1,0:T(8,128)(2,1)}, u32[]{:S(2)}, u32[]{:S(2)}) collective-permute-start(bf16[384,3840]{1,0:T(8,128)(2,1)S(1)} %pad_maximum_fusion.6.refs_4_), channel_id=1, source_target_pairs={{0,1},{1,0},{2,3},{3,2},{4,5},{5,4},{6,7},{7,6},{8,9},{9,8},{10,11... | collective-permute-start | bytes 8847368 | tf_op jit(solution)/shard_map/ppermute | solution.py:86
  117.5 34.3 %collective-permute-start.12 = (bf16[160,2560]{1,0:T(8,128)(2,1)}, bf16[160,2560]{1,0:T(8,128)(2,1)}, u32[]{:S(2)}, u32[]{:S(2)}) collective-permute-start(bf16[160,2560]{1,0:T(8,128)(2,1)} %get-tuple-element.388), channel_id=1, source_target_pairs={{0,2},{1,3},{2,0},{3,1},{4,6},{5,7},{6,4},{7,5},{8,10},{9,11},{10,... | collective-permute-start | bytes 2457608 | tf_op jit(solution)/shard_map/ppermute | solution.py:86
  126.0 25.9 %collective-permute-start.13 = (bf16[160,2560]{1,0:T(8,128)(2,1)}, bf16[160,2560]{1,0:T(8,128)(2,1)}, u32[]{:S(2)}, u32[]{:S(2)}) collective-permute-start(bf16[160,2560]{1,0:T(8,128)(2,1)} %get-tuple-element.389), channel_id=1, source_target_pairs={{0,4},{1,5},{2,6},{3,7},{4,0},{5,1},{6,2},{7,3},{8,12},{9,13},{10,... | collective-permute-start | bytes 2457608 | tf_op jit(solution)/shard_map/ppermute | solution.py:86
  179.1 66.2 %collective-permute-start.17 = (bf16[320,2560]{1,0:T(8,128)(2,1)}, bf16[320,2560]{1,0:T(8,128)(2,1)}, u32[]{:S(2)}, u32[]{:S(2)}) collective-permute-start(bf16[320,2560]{1,0:T(8,128)(2,1)} %pad_maximum_fusion.11), channel_id=1, source_target_pairs={{0,4},{1,5},{2,6},{3,7},{4,0},{5,1},{6,2},{7,3},{8,12},{9,13},{10,... | collective-permute-start | bytes 4915208 | tf_op jit(solution)/shard_map/ppermute | solution.py:86
  179.7 65.7 %collective-permute-start.18 = (bf16[320,2560]{1,0:T(8,128)(2,1)}, bf16[320,2560]{1,0:T(8,128)(2,1)}, u32[]{:S(2)}, u32[]{:S(2)}) collective-permute-start(bf16[320,2560]{1,0:T(8,128)(2,1)} %pad_maximum_fusion.12), channel_id=1, source_target_pairs={{0,2},{1,3},{2,0},{3,1},{4,6},{5,7},{6,4},{7,5},{8,10},{9,11},{10,... | collective-permute-start | bytes 4915208 | tf_op jit(solution)/shard_map/ppermute | solution.py:86
  184.4 60.9 %collective-permute-start.19 = (bf16[1,2,128,2560]{3,2,1,0:T(8,128)(2,1)S(1)}, bf16[1,2,128,2560]{3,2,1,0:T(8,128)(2,1)S(1)}, u32[]{:S(2)}, u32[]{:S(2)}) collective-permute-start(bf16[1,2,128,2560]{3,2,1,0:T(8,128)(2,1)S(1)} %get-tuple-element.413), channel_id=1, source_target_pairs={{0,2},{1,3},{2,0},{3,1},{4,6},{5,7},{6,4},{7,5},{8,10},{9,11},{10,... | collective-permute-start | bytes 3932168 | tf_op jit(solution)/shard_map/ppermute | solution.py:86
  185.7 59.7 %collective-permute-start.20 = (bf16[1,2,128,2560]{3,2,1,0:T(8,128)(2,1)S(1)}, bf16[1,2,128,2560]{3,2,1,0:T(8,128)(2,1)S(1)}, u32[]{:S(2)}, u32[]{:S(2)}) collective-permute-start(bf16[1,2,128,2560]{3,2,1,0:T(8,128)(2,1)S(1)} %get-tuple-element.415), channel_id=1, source_target_pairs={{0,4},{1,5},{2,6},{3,7},{4,0},{5,1},{6,2},{7,3},{8,12},{9,13},{10,... | collective-permute-start | bytes 3932168 | tf_op jit(solution)/shard_map/ppermute | solution.py:86
  261.6 58.9 %collective-permute-start.26 = (bf16[2,2,128,2560]{3,2,1,0:T(8,128)(2,1)S(1)}, bf16[2,2,128,2560]{3,2,1,0:T(8,128)(2,1)S(1)}, u32[]{:S(2)}, u32[]{:S(2)}) collective-permute-start(bf16[2,2,128,2560]{3,2,1,0:T(8,128)(2,1)S(1)} %constant_dynamic-update-slice_fusion.4), channel_id=1, source_target_pairs={{0,4},{1,5},{2,6},{3,7},{4,0},{5,1},{6,2},{7,3},{8,12},{9,13},{10,... | collective-permute-start | bytes 7864328 | tf_op jit(solution)/shard_map/ppermute | solution.py:86
  263.4 58.6 %collective-permute-start.27 = (bf16[2,2,128,2560]{3,2,1,0:T(8,128)(2,1)S(1)}, bf16[2,2,128,2560]{3,2,1,0:T(8,128)(2,1)S(1)}, u32[]{:S(2)}, u32[]{:S(2)}) collective-permute-start(bf16[2,2,128,2560]{3,2,1,0:T(8,128)(2,1)S(1)} %constant_dynamic-update-slice_fusion.6), channel_id=1, source_target_pairs={{0,2},{1,3},{2,0},{3,1},{4,6},{5,7},{6,4},{7,5},{8,10},{9,11},{10,... | collective-permute-start | bytes 7864328 | tf_op jit(solution)/shard_map/ppermute | solution.py:86
  347.7 29.4 %collective-permute-start.30 = (bf16[256,2560]{1,0:T(8,128)(2,1)S(1)}, bf16[256,2560]{1,0:T(8,128)(2,1)S(1)}, u32[]{:S(2)}, u32[]{:S(2)}) collective-permute-start(bf16[256,2560]{1,0:T(8,128)(2,1)S(1)} %pad_maximum_fusion.16), channel_id=1, source_target_pairs={{0,4},{1,5},{2,6},{3,7},{4,0},{5,1},{6,2},{7,3},{8,12},{9,13},{10,... | collective-permute-start | bytes 3932168 | tf_op jit(solution)/shard_map/ppermute | solution.py:86
  349.7 29.0 %collective-permute-start.31 = (bf16[256,2560]{1,0:T(8,128)(2,1)S(1)}, bf16[256,2560]{1,0:T(8,128)(2,1)S(1)}, u32[]{:S(2)}, u32[]{:S(2)}) collective-permute-start(bf16[256,2560]{1,0:T(8,128)(2,1)S(1)} %pad_maximum_fusion.17), channel_id=1, source_target_pairs={{0,2},{1,3},{2,0},{3,1},{4,6},{5,7},{6,4},{7,5},{8,10},{9,11},{10,... | collective-permute-start | bytes 3932168 | tf_op jit(solution)/shard_map/ppermute | solution.py:86
  399.2 38.1 %collective-permute-start.34 = (bf16[256,2560]{1,0:T(8,128)(2,1)S(1)}, bf16[256,2560]{1,0:T(8,128)(2,1)S(1)}, u32[]{:S(2)}, u32[]{:S(2)}) collective-permute-start(bf16[256,2560]{1,0:T(8,128)(2,1)S(1)} %constant_dynamic-update-slice_fusion.16), channel_id=1, source_target_pairs={{0,4},{1,5},{2,6},{3,7},{4,0},{5,1},{6,2},{7,3},{8,12},{9,13},{10,... | collective-permute-start | bytes 3932168 | tf_op jit(solution)/shard_map/ppermute | solution.py:86
  399.9 37.4 %collective-permute-start.35 = (bf16[256,2560]{1,0:T(8,128)(2,1)S(1)}, bf16[256,2560]{1,0:T(8,128)(2,1)}, u32[]{:S(2)}, u32[]{:S(2)}) collective-permute-start(bf16[256,2560]{1,0:T(8,128)(2,1)S(1)} %constant_dynamic-update-slice_fusion.18), channel_id=1, source_target_pairs={{0,2},{1,3},{2,0},{3,1},{4,6},{5,7},{6,4},{7,5},{8,10},{9,11},{10,... | collective-permute-start | bytes 3932168 | tf_op jit(solution)/shard_map/ppermute | solution.py:86
  439.9 27.1 %collective-permute-start.36 = (bf16[256,2560]{1,0:T(8,128)(2,1)}, bf16[256,2560]{1,0:T(8,128)(2,1)}, u32[]{:S(2)}, u32[]{:S(2)}) collective-permute-start(bf16[256,2560]{1,0:T(8,128)(2,1)} %get-tuple-element.861), channel_id=1, source_target_pairs={{0,4},{1,5},{2,6},{3,7},{4,0},{5,1},{6,2},{7,3},{8,12},{9,13},{10,... | collective-permute-start | bytes 3932168 | tf_op jit(solution)/shard_map/ppermute | solution.py:86
  441.3 26.8 %collective-permute-start.37 = (bf16[256,2560]{1,0:T(8,128)(2,1)S(1)}, bf16[256,2560]{1,0:T(8,128)(2,1)}, u32[]{:S(2)}, u32[]{:S(2)}) collective-permute-start(bf16[256,2560]{1,0:T(8,128)(2,1)S(1)} %get-tuple-element.860), channel_id=1, source_target_pairs={{0,2},{1,3},{2,0},{3,1},{4,6},{5,7},{6,4},{7,5},{8,10},{9,11},{10,... | collective-permute-start | bytes 3932168 | tf_op jit(solution)/shard_map/ppermute | solution.py:86
  472.3 25.6 %collective-permute-start.38 = (bf16[128,2560]{1,0:T(8,128)(2,1)S(1)}, bf16[128,2560]{1,0:T(8,128)(2,1)S(1)}, u32[]{:S(2)}, u32[]{:S(2)}) collective-permute-start(bf16[128,2560]{1,0:T(8,128)(2,1)S(1)} %get-tuple-element.900), channel_id=1, source_target_pairs={{0,2},{1,3},{2,0},{3,1},{4,6},{5,7},{6,4},{7,5},{8,10},{9,11},{10,... | collective-permute-start | bytes 1966088 | tf_op jit(solution)/shard_map/ppermute | solution.py:86
  473.9 24.0 %collective-permute-start.39 = (bf16[128,2560]{1,0:T(8,128)(2,1)S(1)}, bf16[128,2560]{1,0:T(8,128)(2,1)}, u32[]{:S(2)}, u32[]{:S(2)}) collective-permute-start(bf16[128,2560]{1,0:T(8,128)(2,1)S(1)} %get-tuple-element.898), channel_id=1, source_target_pairs={{0,4},{1,5},{2,6},{3,7},{4,0},{5,1},{6,2},{7,3},{8,12},{9,13},{10,... | collective-permute-start | bytes 1966088 | tf_op jit(solution)/shard_map/ppermute | solution.py:86
  541.4 40.7 %collective-permute-start.40 = (bf16[256,2560]{1,0:T(8,128)(2,1)}, bf16[256,2560]{1,0:T(8,128)(2,1)}, u32[]{:S(2)}, u32[]{:S(2)}) collective-permute-start(bf16[256,2560]{1,0:T(8,128)(2,1)} %get-tuple-element.857), channel_id=1, source_target_pairs={{0,4},{1,5},{2,6},{3,7},{4,0},{5,1},{6,2},{7,3},{8,12},{9,13},{10,... | collective-permute-start | bytes 3932168 | tf_op jit(solution)/shard_map/ppermute | solution.py:86
  543.0 39.2 %collective-permute-start.41 = (bf16[256,2560]{1,0:T(8,128)(2,1)}, bf16[256,2560]{1,0:T(8,128)(2,1)}, u32[]{:S(2)}, u32[]{:S(2)}) collective-permute-start(bf16[256,2560]{1,0:T(8,128)(2,1)} %get-tuple-element.856), channel_id=1, source_target_pairs={{0,2},{1,3},{2,0},{3,1},{4,6},{5,7},{6,4},{7,5},{8,10},{9,11},{10,... | collective-permute-start | bytes 3932168 | tf_op jit(solution)/shard_map/ppermute | solution.py:86
  625.5 42.4 %collective-permute-start.50 = (bf16[256,2560]{1,0:T(8,128)(2,1)}, bf16[256,2560]{1,0:T(8,128)(2,1)}, u32[]{:S(2)}, u32[]{:S(2)}) collective-permute-start(bf16[256,2560]{1,0:T(8,128)(2,1)} %get-tuple-element.853), channel_id=1, source_target_pairs={{0,4},{1,5},{2,6},{3,7},{4,0},{5,1},{6,2},{7,3},{8,12},{9,13},{10,... | collective-permute-start | bytes 3932168 | tf_op jit(solution)/shard_map/ppermute | solution.py:86
  626.0 41.9 %collective-permute-start.51 = (bf16[256,2560]{1,0:T(8,128)(2,1)}, bf16[256,2560]{1,0:T(8,128)(2,1)}, u32[]{:S(2)}, u32[]{:S(2)}) collective-permute-start(bf16[256,2560]{1,0:T(8,128)(2,1)} %get-tuple-element.852), channel_id=1, source_target_pairs={{0,2},{1,3},{2,0},{3,1},{4,6},{5,7},{6,4},{7,5},{8,10},{9,11},{10,... | collective-permute-start | bytes 3932168 | tf_op jit(solution)/shard_map/ppermute | solution.py:86
  668.0 52.6 %collective-permute-start.52 = (bf16[400,2560]{1,0:T(8,128)(2,1)S(1)}, bf16[400,2560]{1,0:T(8,128)(2,1)S(1)}, u32[]{:S(2)}, u32[]{:S(2)}) collective-permute-start(bf16[400,2560]{1,0:T(8,128)(2,1)S(1)} %get-tuple-element.502), channel_id=1, source_target_pairs={{0,8},{24,16},{1,9},{25,17},{2,10},{26,18},{3,11},{27,19},{4,12},{... | collective-permute-start | bytes 6144008 | tf_op jit(solution)/shard_map/ppermute | solution.py:435
  722.4 47.5 %collective-permute-start.55 = (bf16[400,2560]{1,0:T(8,128)(2,1)}, bf16[400,2560]{1,0:T(8,128)(2,1)}, u32[]{:S(2)}, u32[]{:S(2)}) collective-permute-start(bf16[400,2560]{1,0:T(8,128)(2,1)} %get-tuple-element.527), channel_id=1, source_target_pairs={{0,8},{24,16},{1,9},{25,17},{2,10},{26,18},{3,11},{27,19},{4,12},{... | collective-permute-start | bytes 6144008 | tf_op jit(solution)/shard_map/ppermute | solution.py:435
  728.4 41.5 %collective-permute-start.56 = (bf16[400,2560]{1,0:T(8,128)(2,1)}, bf16[400,2560]{1,0:T(8,128)(2,1)}, u32[]{:S(2)}, u32[]{:S(2)}) collective-permute-start(bf16[400,2560]{1,0:T(8,128)(2,1)} %add_convert_fusion.13), channel_id=1, source_target_pairs={{8,16},{16,8},{9,17},{17,9},{10,18},{18,10},{11,19},{19,11},{12,20... | collective-permute-start | bytes 6144008 | tf_op jit(solution)/shard_map/ppermute | solution.py:435
  737.1 29.2 %collective-permute-start.57 = (bf16[256,2560]{1,0:T(8,128)(2,1)}, bf16[256,2560]{1,0:T(8,128)(2,1)}, u32[]{:S(2)}, u32[]{:S(2)}) collective-permute-start(bf16[256,2560]{1,0:T(8,128)(2,1)} %get-tuple-element.849), channel_id=1, source_target_pairs={{0,4},{1,5},{2,6},{3,7},{4,0},{5,1},{6,2},{7,3},{8,12},{9,13},{10,... | collective-permute-start | bytes 3932168 | tf_op jit(solution)/shard_map/ppermute | solution.py:86
  738.6 29.0 %collective-permute-start.58 = (bf16[256,2560]{1,0:T(8,128)(2,1)}, bf16[256,2560]{1,0:T(8,128)(2,1)}, u32[]{:S(2)}, u32[]{:S(2)}) collective-permute-start(bf16[256,2560]{1,0:T(8,128)(2,1)} %get-tuple-element.848), channel_id=1, source_target_pairs={{0,2},{1,3},{2,0},{3,1},{4,6},{5,7},{6,4},{7,5},{8,10},{9,11},{10,... | collective-permute-start | bytes 3932168 | tf_op jit(solution)/shard_map/ppermute | solution.py:86
  778.3 67.2 %collective-permute-start.59 = (bf16[400,2560]{1,0:T(8,128)(2,1)}, bf16[400,2560]{1,0:T(8,128)(2,1)}, u32[]{:S(2)}, u32[]{:S(2)}) collective-permute-start(bf16[400,2560]{1,0:T(8,128)(2,1)} %broadcast_select_fusion.9), channel_id=1, source_target_pairs={{0,8},{24,16},{8,0},{16,24},{1,9},{25,17},{9,1},{17,25},{2,10},{26... | collective-permute-start | bytes 6144008 | tf_op jit(solution)/shard_map/ppermute | solution.py:435
  782.1 63.4 %collective-permute-start.60 = (bf16[400,2560]{1,0:T(8,128)(2,1)}, bf16[400,2560]{1,0:T(8,128)(2,1)}, u32[]{:S(2)}, u32[]{:S(2)}) collective-permute-start(bf16[400,2560]{1,0:T(8,128)(2,1)} %add_convert_fusion.11), channel_id=1, source_target_pairs={{8,16},{16,8},{9,17},{17,9},{10,18},{18,10},{11,19},{19,11},{12,20... | collective-permute-start | bytes 6144008 | tf_op jit(solution)/shard_map/ppermute | solution.py:435
  790.0 55.4 %collective-permute-start.61 = (bf16[128,2560]{1,0:T(8,128)(2,1)}, bf16[128,2560]{1,0:T(8,128)(2,1)}, u32[]{:S(2)}, u32[]{:S(2)}) collective-permute-start(bf16[128,2560]{1,0:T(8,128)(2,1)} %get-tuple-element.888), channel_id=1, source_target_pairs={{0,2},{1,3},{2,0},{3,1},{4,6},{5,7},{6,4},{7,5},{8,10},{9,11},{10,... | collective-permute-start | bytes 1966088 | tf_op jit(solution)/shard_map/ppermute | solution.py:86
  791.5 54.0 %collective-permute-start.62 = (bf16[128,2560]{1,0:T(8,128)(2,1)}, bf16[128,2560]{1,0:T(8,128)(2,1)}, u32[]{:S(2)}, u32[]{:S(2)}) collective-permute-start(bf16[128,2560]{1,0:T(8,128)(2,1)} %get-tuple-element.886), channel_id=1, source_target_pairs={{0,4},{1,5},{2,6},{3,7},{4,0},{5,1},{6,2},{7,3},{8,12},{9,13},{10,... | collective-permute-start | bytes 1966088 | tf_op jit(solution)/shard_map/ppermute | solution.py:86
  853.8 63.0 %collective-permute-start.63 = (bf16[400,2560]{1,0:T(8,128)(2,1)}, bf16[400,2560]{1,0:T(8,128)(2,1)}, u32[]{:S(2)}, u32[]{:S(2)}) collective-permute-start(bf16[400,2560]{1,0:T(8,128)(2,1)} %broadcast_select_fusion.8), channel_id=1, source_target_pairs={{0,8},{24,16},{8,0},{16,24},{1,9},{25,17},{9,1},{17,25},{2,10},{26... | collective-permute-start | bytes 6144008 | tf_op jit(solution)/shard_map/ppermute | solution.py:435
  854.2 62.7 %collective-permute-start.64 = (bf16[400,2560]{1,0:T(8,128)(2,1)}, bf16[400,2560]{1,0:T(8,128)(2,1)}, u32[]{:S(2)}, u32[]{:S(2)}) collective-permute-start(bf16[400,2560]{1,0:T(8,128)(2,1)} %add_convert_fusion.10), channel_id=1, source_target_pairs={{8,16},{16,8},{9,17},{17,9},{10,18},{18,10},{11,19},{19,11},{12,20... | collective-permute-start | bytes 6144008 | tf_op jit(solution)/shard_map/ppermute | solution.py:435
  861.1 45.7 %collective-permute-start.67 = (bf16[256,288]{1,0:T(8,128)(2,1)}, bf16[256,288]{1,0:T(8,128)(2,1)S(1)}, u32[]{:S(2)}, u32[]{:S(2)}) collective-permute-start(bf16[256,288]{1,0:T(8,128)(2,1)} %get-tuple-element.914), channel_id=1, source_target_pairs={{0,8},{8,16},{16,24},{24,0},{1,9},{9,17},{17,25},{25,1},{2,10},{10... | collective-permute-start | bytes 442376 | tf_op jit(solution)/shard_map/ppermute | solution.py:501
  863.0 52.1 %collective-permute-start.66 = (bf16[256,288]{1,0:T(8,128)(2,1)S(1)}, bf16[256,288]{1,0:T(8,128)(2,1)S(1)}, u32[]{:S(2)}, u32[]{:S(2)}) collective-permute-start(bf16[256,288]{1,0:T(8,128)(2,1)S(1)} %get-tuple-element.915), channel_id=1, source_target_pairs={{0,16},{8,24},{16,0},{24,8},{1,17},{9,25},{17,1},{25,9},{2,18},{10... | collective-permute-start | bytes 442376 | tf_op jit(solution)/shard_map/ppermute | solution.py:501
  864.2 50.9 %collective-permute-start.65 = (bf16[256,288]{1,0:T(8,128)(2,1)S(1)}, bf16[256,288]{1,0:T(8,128)(2,1)}, u32[]{:S(2)}, u32[]{:S(2)}) collective-permute-start(bf16[256,288]{1,0:T(8,128)(2,1)S(1)} %get-tuple-element.913), channel_id=1, source_target_pairs={{0,24},{8,0},{16,8},{24,16},{1,25},{9,1},{17,9},{25,17},{2,26},{10... | collective-permute-start | bytes 442376 | tf_op jit(solution)/shard_map/ppermute | solution.py:501
  937.1 57.0 %collective-permute-start.68 = (bf16[400,2560]{1,0:T(8,128)(2,1)}, bf16[400,2560]{1,0:T(8,128)(2,1)}, u32[]{:S(2)}, u32[]{:S(2)}) collective-permute-start(bf16[400,2560]{1,0:T(8,128)(2,1)} %broadcast_select_fusion.7), channel_id=1, source_target_pairs={{0,8},{24,16},{8,0},{16,24},{1,9},{25,17},{9,1},{17,25},{2,10},{26... | collective-permute-start | bytes 6144008 | tf_op jit(solution)/shard_map/ppermute | solution.py:435
  939.9 54.3 %collective-permute-start.69 = (bf16[400,2560]{1,0:T(8,128)(2,1)}, bf16[400,2560]{1,0:T(8,128)(2,1)}, u32[]{:S(2)}, u32[]{:S(2)}) collective-permute-start(bf16[400,2560]{1,0:T(8,128)(2,1)} %add_convert_fusion.7), channel_id=1, source_target_pairs={{8,16},{16,8},{9,17},{17,9},{10,18},{18,10},{11,19},{19,11},{12,20... | collective-permute-start | bytes 6144008 | tf_op jit(solution)/shard_map/ppermute | solution.py:435
  942.0 52.1 %collective-permute-start.70 = (bf16[4,1,160,2560]{3,2,0,1:T(8,128)(2,1)}, bf16[4,1,160,2560]{3,2,0,1:T(8,128)(2,1)}, u32[]{:S(2)}, u32[]{:S(2)}) collective-permute-start(bf16[4,1,160,2560]{3,2,0,1:T(8,128)(2,1)} %dynamic-slice_bitcast_fusion.1), channel_id=1, source_target_pairs={{0,1},{1,0},{2,3},{3,2},{4,5},{5,4},{6,7},{7,6},{8,9},{9,8},{10,11... | collective-permute-start | bytes 9830408 | tf_op jit(solution)/shard_map/ppermute | solution.py:86
  942.1 52.1 %collective-permute-start.71 = (bf16[4,1,160,2560]{3,2,0,1:T(8,128)(2,1)}, bf16[4,1,160,2560]{3,2,0,1:T(8,128)(2,1)}, u32[]{:S(2)}, u32[]{:S(2)}) collective-permute-start(bf16[4,1,160,2560]{3,2,0,1:T(8,128)(2,1)} %dynamic-slice_bitcast_fusion), channel_id=1, source_target_pairs={{0,1},{1,0},{2,3},{3,2},{4,5},{5,4},{6,7},{7,6},{8,9},{9,8},{10,11... | collective-permute-start | bytes 9830408 | tf_op jit(solution)/shard_map/ppermute | solution.py:86
  1028.3 48.1 %collective-permute-start.75 = (bf16[400,2560]{1,0:T(8,128)(2,1)}, bf16[400,2560]{1,0:T(8,128)(2,1)}, u32[]{:S(2)}, u32[]{:S(2)}) collective-permute-start(bf16[400,2560]{1,0:T(8,128)(2,1)} %broadcast_select_fusion.6), channel_id=1, source_target_pairs={{0,8},{24,16},{8,0},{16,24},{1,9},{25,17},{9,1},{17,25},{2,10},{26... | collective-permute-start | bytes 6144008 | tf_op jit(solution)/shard_map/ppermute | solution.py:435
  1028.4 48.0 %collective-permute-start.76 = (bf16[400,2560]{1,0:T(8,128)(2,1)}, bf16[400,2560]{1,0:T(8,128)(2,1)}, u32[]{:S(2)}, u32[]{:S(2)}) collective-permute-start(bf16[400,2560]{1,0:T(8,128)(2,1)} %add_convert_fusion.5), channel_id=1, source_target_pairs={{8,16},{16,8},{9,17},{17,9},{10,18},{18,10},{11,19},{19,11},{12,20... | collective-permute-start | bytes 6144008 | tf_op jit(solution)/shard_map/ppermute | solution.py:435
  1035.8 37.5 %collective-permute-start.77 = (bf16[1,2,160,2560]{3,2,1,0:T(8,128)(2,1)}, bf16[1,2,160,2560]{3,2,1,0:T(8,128)(2,1)}, u32[]{:S(2)}, u32[]{:S(2)}) collective-permute-start(bf16[1,2,160,2560]{3,2,1,0:T(8,128)(2,1)} %dynamic-slice_bitcast_fusion.5), channel_id=1, source_target_pairs={{0,4},{1,5},{2,6},{3,7},{4,0},{5,1},{6,2},{7,3},{8,12},{9,13},{10,... | collective-permute-start | bytes 4915208 | tf_op jit(solution)/shard_map/ppermute | solution.py:86
  1036.3 37.3 %collective-permute-start.78 = (bf16[2,1,160,2560]{3,2,0,1:T(8,128)(2,1)}, bf16[2,1,160,2560]{3,2,0,1:T(8,128)(2,1)}, u32[]{:S(2)}, u32[]{:S(2)}) collective-permute-start(bf16[2,1,160,2560]{3,2,0,1:T(8,128)(2,1)} %dynamic-slice_bitcast_fusion.4), channel_id=1, source_target_pairs={{0,2},{1,3},{2,0},{3,1},{4,6},{5,7},{6,4},{7,5},{8,10},{9,11},{10,... | collective-permute-start | bytes 4915208 | tf_op jit(solution)/shard_map/ppermute | solution.py:86
  1091.5 53.7 %collective-permute-start.83 = (bf16[4,1,320,1152]{3,2,0,1:T(8,128)(2,1)}, bf16[4,1,320,1152]{3,2,0,1:T(8,128)(2,1)S(1)}, u32[]{:S(2)}, u32[]{:S(2)}) collective-permute-start(bf16[4,1,320,1152]{3,2,0,1:T(8,128)(2,1)} %dynamic-slice_bitcast_fusion.3), channel_id=1, source_target_pairs={{0,1},{1,0},{2,3},{3,2},{4,5},{5,4},{6,7},{7,6},{8,9},{9,8},{10,11... | collective-permute-start | bytes 8847368 | tf_op jit(solution)/shard_map/ppermute | solution.py:86
  1091.5 53.7 %collective-permute-start.84 = (bf16[4,1,96,3840]{3,2,0,1:T(8,128)(2,1)}, bf16[4,1,96,3840]{3,2,0,1:T(8,128)(2,1)}, u32[]{:S(2)}, u32[]{:S(2)}) collective-permute-start(bf16[4,1,96,3840]{3,2,0,1:T(8,128)(2,1)} %dynamic-slice_bitcast_fusion.2), channel_id=1, source_target_pairs={{0,1},{1,0},{2,3},{3,2},{4,5},{5,4},{6,7},{7,6},{8,9},{9,8},{10,11... | collective-permute-start | bytes 8847368 | tf_op jit(solution)/shard_map/ppermute | solution.py:86
  1094.3 50.9 %collective-permute-start.79 = (bf16[400,2560]{1,0:T(8,128)(2,1)S(1)}, bf16[400,2560]{1,0:T(8,128)(2,1)}, u32[]{:S(2)}, u32[]{:S(2)}) collective-permute-start(bf16[400,2560]{1,0:T(8,128)(2,1)S(1)} %add_convert_fusion.4), channel_id=1, source_target_pairs={{8,0},{16,24},{9,1},{17,25},{10,2},{18,26},{11,3},{19,27},{12,4},{... | collective-permute-start | bytes 6144008 | tf_op jit(solution)/shard_map/ppermute | solution.py:435
  1095.6 49.6 %collective-permute-start.80 = (bf16[400,2560]{1,0:T(8,128)(2,1)S(1)}, bf16[400,2560]{1,0:T(8,128)(2,1)}, u32[]{:S(2)}, u32[]{:S(2)}) collective-permute-start(bf16[400,2560]{1,0:T(8,128)(2,1)S(1)} %add_convert_fusion.3), channel_id=1, source_target_pairs={{8,16},{16,8},{9,17},{17,9},{10,18},{18,10},{11,19},{19,11},{12,20... | collective-permute-start | bytes 6144008 | tf_op jit(solution)/shard_map/ppermute | solution.py:435
  1158.5 60.8 %collective-permute-start.87 = (bf16[400,2560]{1,0:T(8,128)(2,1)S(1)}, bf16[400,2560]{1,0:T(8,128)(2,1)S(1)}, u32[]{:S(2)}, u32[]{:S(2)}) collective-permute-start(bf16[400,2560]{1,0:T(8,128)(2,1)S(1)} %add_convert_fusion.2), channel_id=1, source_target_pairs={{8,0},{16,24},{9,1},{17,25},{10,2},{18,26},{11,3},{19,27},{12,4},{... | collective-permute-start | bytes 6144008 | tf_op jit(solution)/shard_map/ppermute | solution.py:435
  1164.4 54.9 %collective-permute-start.86 = (bf16[320,2560]{1,0:T(8,128)(2,1)}, bf16[320,2560]{1,0:T(8,128)(2,1)}, u32[]{:S(2)}, u32[]{:S(2)}) collective-permute-start(bf16[320,2560]{1,0:T(8,128)(2,1)} %pad_maximum_fusion.13), channel_id=1, source_target_pairs={{0,8},{24,16},{1,9},{25,17},{2,10},{26,18},{3,11},{27,19},{4,12},{... | collective-permute-start | bytes 4915208 | tf_op jit(solution)/shard_map/ppermute | solution.py:435
  1172.1 47.2 %collective-permute-start.88 = (bf16[1,2,320,1152]{3,2,1,0:T(8,128)(2,1)S(1)}, bf16[1,2,320,1152]{3,2,1,0:T(8,128)(2,1)}, u32[]{:S(2)}, u32[]{:S(2)}) collective-permute-start(bf16[1,2,320,1152]{3,2,1,0:T(8,128)(2,1)S(1)} %dynamic-slice_bitcast_fusion.7), channel_id=1, source_target_pairs={{0,4},{1,5},{2,6},{3,7},{4,0},{5,1},{6,2},{7,3},{8,12},{9,13},{10,... | collective-permute-start | bytes 4423688 | tf_op jit(solution)/shard_map/ppermute | solution.py:86
  1172.6 46.7 %collective-permute-start.89 = (bf16[2,1,96,3840]{3,2,0,1:T(8,128)(2,1)}, bf16[2,1,96,3840]{3,2,0,1:T(8,128)(2,1)}, u32[]{:S(2)}, u32[]{:S(2)}) collective-permute-start(bf16[2,1,96,3840]{3,2,0,1:T(8,128)(2,1)} %dynamic-slice_bitcast_fusion.6), channel_id=1, source_target_pairs={{0,2},{1,3},{2,0},{3,1},{4,6},{5,7},{6,4},{7,5},{8,10},{9,11},{10,... | collective-permute-start | bytes 4423688 | tf_op jit(solution)/shard_map/ppermute | solution.py:86
  1174.1 45.2 %collective-permute-start.90 = (bf16[1,2,32,5120]{3,2,1,0:T(8,128)(2,1)}, bf16[1,2,32,5120]{3,2,1,0:T(8,128)(2,1)}, u32[]{:S(2)}, u32[]{:S(2)}) collective-permute-start(bf16[1,2,32,5120]{3,2,1,0:T(8,128)(2,1)} %dynamic-slice_bitcast_fusion.9), channel_id=1, source_target_pairs={{0,4},{1,5},{2,6},{3,7},{4,0},{5,1},{6,2},{7,3},{8,12},{9,13},{10,... | collective-permute-start | bytes 1966088 | tf_op jit(solution)/shard_map/ppermute | solution.py:86
  1226.1 32.3 %collective-permute-start.91 = (bf16[320,2560]{1,0:T(8,128)(2,1)S(1)}, bf16[320,2560]{1,0:T(8,128)(2,1)S(1)}, u32[]{:S(2)}, u32[]{:S(2)}) collective-permute-start(bf16[320,2560]{1,0:T(8,128)(2,1)S(1)} %add_convert_fusion.15), channel_id=1, source_target_pairs={{8,16},{16,8},{9,17},{17,9},{10,18},{18,10},{11,19},{19,11},{12,20... | collective-permute-start | bytes 4915208 | tf_op jit(solution)/shard_map/ppermute | solution.py:435
  1235.0 23.4 %collective-permute-start.92 = (bf16[1,1,320,1152]{3,2,1,0:T(8,128)(2,1)S(1)}, bf16[1,1,320,1152]{3,2,1,0:T(8,128)(2,1)S(1)}, u32[]{:S(2)}, u32[]{:S(2)}) collective-permute-start(bf16[1,1,320,1152]{3,2,1,0:T(8,128)(2,1)S(1)} %constant_dynamic-slice_fusion.2), channel_id=1, source_target_pairs={{0,2},{1,3},{2,0},{3,1},{4,6},{5,7},{6,4},{7,5},{8,10},{9,11},{10,... | collective-permute-start | bytes 2211848 | tf_op jit(solution)/shard_map/ppermute | solution.py:86
  1259.0 38.5 %collective-permute-start.96 = (bf16[320,2560]{1,0:T(8,128)(2,1)S(1)}, bf16[320,2560]{1,0:T(8,128)(2,1)S(1)}, u32[]{:S(2)}, u32[]{:S(2)}) collective-permute-start(bf16[320,2560]{1,0:T(8,128)(2,1)S(1)} %add_convert_fusion.14), channel_id=1, source_target_pairs={{8,0},{16,24},{9,1},{17,25},{10,2},{18,26},{11,3},{19,27},{12,4},{... | collective-permute-start | bytes 4915208 | tf_op jit(solution)/shard_map/ppermute | solution.py:435
  (239 other events, 3089.5 us)

commit v2 on v1

--- a/solution.py
+++ b/solution.py
@@ -123,24 +123,21 @@
     me = lax.axis_index("fsdp").astype(jnp.int32).reshape(1)
     plan, sources, shapes = [], [], []
     for out, parts in enumerate(groups):
-        heights = [held.shape[0] * 2 // count for held, _, _ in parts]
+        heights = [sum(piece.shape[0] for piece, _ in part) // count for part in parts]
         offset = 0
-        for (held, other, order), rows in zip(parts, heights):
-            places = [0]
-            for bit in order:
-                places = places + [place ^ bit for place in places]
-            plan.append((out, rows, tuple(places), sum(heights), offset))
-            plan.append((out, rows, tuple(place ^ 1 for place in places), sum(heights), offset))
-            sources += [held, other]
+        for part, rows in zip(parts, heights):
+            for piece, places in part:
+                plan.append((out, rows, tuple(places), sum(heights), offset))
+                sources.append(piece)
             offset += rows
-        shapes.append(jax.ShapeDtypeStruct((count * sum(heights), parts[0][0].shape[1]), jnp.bfloat16))
+        shapes.append(jax.ShapeDtypeStruct((count * sum(heights), parts[0][0][0].shape[1]), jnp.bfloat16))
     anywhere = pl.BlockSpec(memory_space=pl.ANY)
     return pl.pallas_call(
         functools.partial(place_kernel, tuple(plan)),
         in_specs=[pl.BlockSpec(memory_space=pltpu.SMEM)] + [anywhere] * len(sources),
         out_specs=[pl.BlockSpec(memory_space=pltpu.VMEM)] * len(shapes),
         out_shape=shapes,
-        scratch_shapes=[pltpu.SemaphoreType.DMA((len(plan) * count // 2,))],
+        scratch_shapes=[pltpu.SemaphoreType.DMA((sum(len(of[2]) for of in plan),))],
         compiler_params=pltpu.CompilerParams(vmem_limit_bytes=32 * 2**20),
         name="place_shards",
     )(me, *sources)
@@ -226,7 +223,7 @@
     mixed_ref[0] = low(jnp.concatenate(mixed, axis=0).T)
 
 
-def attend_forward(query_low, latent, rope_keys, bias, cosine, ahead, behind, query_w, key_w, value_w, quads):
+def attend_forward(query_low, latent, rope_keys, bias, cosine, ahead, behind, query_w, latent_w, quads):
     batches, rows, rank = query_low.shape
     keys, width = latent.shape[1:]
     qw, kw, rw = QUAD * (DN + DR), QUAD * DN, QUAD * DR
@@ -246,7 +243,7 @@
             pl.BlockSpec((rows, rw), fixed),
             pl.BlockSpec((rank, qw), lambda b, j: (0, j)),
             pl.BlockSpec((width, kw), lambda b, j: (0, j)),
-            pl.BlockSpec((width, kw), lambda b, j: (0, j)),
+            pl.BlockSpec((width, kw), lambda b, j: (0, quads + j)),
         ],
         out_specs=[
             pl.BlockSpec((1, rows, qw), lambda b, j: (b, 0, j)),
@@ -265,7 +262,7 @@
             flops=int(flops), bytes_accessed=40 * 2**20, transcendentals=batches * quads * 4 * keys * rows
         ),
         name="attend_forward",
-    )(query_low, latent, rope_keys, bias, cosine, ahead, behind, query_w, key_w, value_w)
+    )(query_low, latent, rope_keys, bias, cosine, ahead, behind, query_w, latent_w, latent_w)
 
 
 def backward_kernel(
@@ -331,7 +328,7 @@
     latent_out[...] += matmul_right(key_grad, key_w[...]) + matmul_right(value_grad, value_w[...])
 
 
-def attend_backward(query, grad, latent, latent_flat, rope_keys, rope_flat, bias, totals, cos_flat, sin_flat, key_w, value_w, quads):
+def attend_backward(query, grad, latent, latent_flat, rope_keys, rope_flat, bias, totals, cos_flat, sin_flat, latent_w, quads):
     rows = query.shape[0]
     keys, width = latent.shape
     qw, kw, rw = QUAD * (DN + DR), QUAD * DN, QUAD * DR
@@ -353,7 +350,7 @@
             pl.BlockSpec((DR // 2, rows), fixed),
             pl.BlockSpec((DR // 2, rows), fixed),
             pl.BlockSpec((width, kw), step),
-            pl.BlockSpec((width, kw), step),
+            pl.BlockSpec((width, kw), lambda j: (0, quads + j)),
         ],
         out_specs=[
             pl.BlockSpec((rows, qw), step),
@@ -376,7 +373,7 @@
             flops=int(flops), bytes_accessed=25 * 2**20, transcendentals=quads * 4 * keys * rows
         ),
         name="attend_backward",
-    )(query, grad, latent, latent_flat, rope_keys, rope_flat, bias, totals, cos_flat, sin_flat, key_w, value_w)
+    )(query, grad, latent, latent_flat, rope_keys, rope_flat, bias, totals, cos_flat, sin_flat, latent_w, latent_w)
 
 
 class LineSum:
@@ -445,31 +442,133 @@
                 self.stage[item] = stage + 1 if stage < 2 * self.hops else None
 
 
-def weight_kernel(fresh, *refs):
-    first, second, first_rows, second_rows = refs[:4]
-    half = first.shape[0] // 2
-    total = matmul_plain(first[...], first_rows[...]) + matmul_plain(second[...], second_rows[...])
+def up_kernel(parts, gate_w, up_w, down_w, *refs):
+    rows_refs, grad_refs = refs[:parts], refs[parts : 2 * parts]
+    hidden_ref, gate_ref, up_ref = refs[2 * parts :]
+    start = 0
+    for rows_ref, grad_ref in zip(rows_refs, grad_refs):
+        cut = slice(start, start + rows_ref.shape[0])
+        start += rows_ref.shape[0]
+        gate_value = matmul_right(gate_w[...], rows_ref[...])
+        up_value = matmul_right(up_w[...], rows_ref[...])
+        hidden_grad = matmul_right(down_w[...], grad_ref[...])
+        sigmoid_gate = 1.0 / (1.0 + jnp.exp(-gate_value))
+        silu_gate = gate_value * sigmoid_gate
+        hidden_ref[:, cut] = low(silu_gate * up_value)
+        gate_ref[:, cut] = low(
+            hidden_grad * up_value * sigmoid_gate * (1.0 + gate_value * (1.0 - sigmoid_gate))
+        )
+        up_ref[:, cut] = low(hidden_grad * silu_gate)
+
+
+def hidden_tile(units):
+    return max(size for size in range(16, 401, 16) if units % size == 0)
+
+
+def feed_up(rows_parts, grad_parts, gate_all, up_all, down_all):
+    units, width = gate_all.shape
+    tile = hidden_tile(units)
+    rows = sum(part.shape[0] for part in rows_parts)
+    whole = [
+        pl.BlockSpec(part.shape, lambda i: (0, 0), pipeline_mode=pl.Buffered(1))
+        for part in (*rows_parts, *grad_parts)
+    ]
+    return pl.pallas_call(
+        functools.partial(up_kernel, len(rows_parts)),
+        grid=(units // tile,),
+        in_specs=[pl.BlockSpec((tile, width), lambda i: (i, 0))] * 3 + whole,
+        out_specs=[pl.BlockSpec((tile, rows), lambda i: (i, 0))] * 3,
+        out_shape=[jax.ShapeDtypeStruct((units, rows), jnp.bfloat16)] * 3,
+        compiler_params=pltpu.CompilerParams(
+            dimension_semantics=("arbitrary",), vmem_limit_bytes=52 * 2**20
+        ),
+        cost_estimate=pl.CostEstimate(
+            flops=6 * units * width * rows,
+            bytes_accessed=6 * units * width + 4 * rows * width + 6 * units * rows,
+            transcendentals=units * rows,
+        ),
+        name="feed_up",
+    )(gate_all, up_all, down_all, *rows_parts, *grad_parts)
+
+
+def down_kernel(pairs, slots, *refs):
+    units, weights = refs[:pairs], refs[pairs : 2 * pairs]
+    outs, turned = refs[2 * pairs : -pairs], refs[-pairs:]
+
+    @pl.when(pl.program_id(0) == 0)
+    def _():
+        for unit_ref, turned_ref in zip(units, turned):
+            turned_ref[...] = unit_ref[...].T
+
+    total = matmul_plain(turned[0][...], weights[0][...])
+    for place in range(1, pairs):
+        total += matmul_plain(turned[place][...], weights[place][...])
+    for out, starts in zip(outs, slots):
+        step = out.shape[0] // len(starts)
+        for place, start in enumerate(starts):
+            out[place * step : (place + 1) * step] = low(total[start : start + step])
+
+
+def feed_down(units, weights, slots):
+    parts = len(slots)
+    depth, rows = units[0].shape
+    width = weights[0].shape[1]
+    tile = 512 if width % 512 == 0 else width
+    return pl.pallas_call(
+        functools.partial(down_kernel, len(units), slots),
+        grid=(width // tile,),
+        in_specs=[pl.BlockSpec((depth, rows), lambda j: (0, 0), pipeline_mode=pl.Buffered(1))]
+        * len(units)
+        + [pl.BlockSpec((depth, tile), lambda j: (0, j))] * len(units),
+        out_specs=[pl.BlockSpec((rows // parts, tile), lambda j: (0, j))] * parts,
+        out_shape=[jax.ShapeDtypeStruct((rows // parts, width), jnp.bfloat16)] * parts,
+        scratch_shapes=[pltpu.VMEM((rows, depth), jnp.bfloat16)] * len(units),
+        compiler_params=pltpu.CompilerParams(
+            dimension_semantics=("arbitrary",), vmem_limit_bytes=48 * 2**20
+        ),
+        cost_estimate=pl.CostEstimate(
+            flops=2 * len(units) * depth * rows * width,
+            bytes_accessed=2 * len(units) * depth * (rows + width) + 2 * rows * width,
+            transcendentals=0,
+        ),
+        name="feed_down",
+    )(*units, *weights)
+
+
+def weight_kernel(lefts, counts, fresh, *refs):
+    left_refs, right_refs = refs[:lefts], refs[lefts : lefts + sum(counts)]
+    half = left_refs[0].shape[0] // 2
+    total, start = None, 0
+    for left, count in zip(left_refs, counts):
+        right = jnp.concatenate([ref[...] for ref in right_refs[start : start + count]], axis=0)
+        start += count
+        product = matmul_plain(left[...], right)
+        total = product if total is None else total + product
+    rest = refs[lefts + sum(counts) :]
     if fresh:
-        upper, lower = refs[4:]
+        upper, lower = rest
         upper[...] = low(total[:half])
         lower[...] = low(total[half:])
     else:
-        upper_in, lower_in, upper, lower = refs[4:]
+        upper_in, lower_in, upper, lower = rest
         upper[...] = low(total[:half] + upper_in[...].astype(jnp.float32))
         lower[...] = low(total[half:] + lower_in[...].astype(jnp.float32))
 
 
 def weight_sums(lefts, rights, place, held):
-    rows = lefts[0].shape[0] // 2
-    depth, width = rights[0].shape
+    rows, depth = lefts[0].shape[0] // 2, lefts[0].shape[1]
+    width = rights[0][0].shape[1]
     tile = 512 if width % 512 == 0 else width
     part = jax.ShapeDtypeStruct((rows // 2, width), jnp.bfloat16)
     part_spec = pl.BlockSpec((rows // 2, tile), lambda j: (0, j))
+    flat = [piece for pieces in rights for piece in pieces]
     return pl.pallas_call(
-        functools.partial(weight_kernel, held is None),
+        functools.partial(
+            weight_kernel, len(lefts), tuple(len(pieces) for pieces in rights), held is None
+        ),
         grid=(width // tile,),
-        in_specs=[pl.BlockSpec((rows, depth), lambda j: (place, 0))] * 2
-        + [pl.BlockSpec((depth, tile), lambda j: (0, j))] * 2
+        in_specs=[pl.BlockSpec((rows, depth), lambda j: (place, 0))] * len(lefts)
+        + [pl.BlockSpec((piece.shape[0], tile), lambda j: (0, j)) for piece in flat]
         + ([] if held is None else [part_spec] * 2),
         out_specs=[part_spec] * 2,
         out_shape=[part] * 2,
@@ -477,32 +576,12 @@
             dimension_semantics=("arbitrary",), vmem_limit_bytes=40 * 2**20
         ),
         cost_estimate=pl.CostEstimate(
-            flops=4 * rows * depth * width,
-            bytes_accessed=4 * (rows * depth + depth * width + rows * width),
+            flops=2 * len(lefts) * rows * depth * width,
+            bytes_accessed=2 * len(lefts) * (rows * depth + depth * width) + 2 * rows * width,
             transcendentals=0,
         ),
         name="weight_sums",
-    )(*lefts, *rights, *(held or ()))
-
-
-def spread_line(rows):
-    count = lax.axis_size("ctx")
-    return [rows] + [
-        lax.ppermute(rows, "ctx", [(i, (i + k) % count) for i in range(count)])
-        for k in range(1, count)
-    ]
-
-
-def collect_line(parts):
-    count = lax.axis_size("ctx")
-    rows = parts.shape[0] // count
-    total = parts[:rows].astype(jnp.float32)
-    for k in range(1, count):
-        got = lax.ppermute(
-            low(parts[k * rows : (k + 1) * rows]), "ctx", [(i, (i - k) % count) for i in range(count)]
-        )
-        total = total + got.astype(jnp.float32)
-    return total
+    )(*lefts, *flat, *(held or ()))
 
 
 def pad_columns(values, width):
@@ -541,7 +620,6 @@
     block_size = seq_rows // blocks
     quads = query_up.shape[1] // (QUAD * (DN + DR))
     query_rank = query_down.shape[1]
-    down_width = query_rank + KVR + DR
     bits = chip_bits()
 
     every_row = jnp.arange(seq_rows, dtype=jnp.int32)
@@ -555,14 +633,8 @@
         axis=1,
     )
     stored_pos = placed * block_size + every_row % block_size
-    near_pos = [
-        lax.dynamic_slice_in_dim(
-            stored_pos, (ctx_place - k) % ctx_count * local_rows, local_rows
-        )
-        for k in range(ctx_count)
-    ]
-    query_pos = near_pos[0]
-    key_pos = jnp.concatenate(near_pos)
+    query_pos = lax.dynamic_slice_in_dim(stored_pos, ctx_place * local_rows, local_rows)
+    key_pos = stored_pos
     local_cos, local_sin = rope_tables(query_pos, DR)
     half = DR // 2
     nothing = jnp.zeros_like(local_sin[:, :half])
@@ -575,16 +647,33 @@
     )
     bias = jnp.where(allowed, 0.0, lowest_score).astype(jnp.float32)
 
+    hold = lax.optimization_barrier
+    rows = batches * local_rows
+    half_rows = local_rows // 2
+    devices = lax.axis_size("fsdp")
+    one_way = tuple(bits)
+    other_way = tuple(bits[::-1])
+    both_ways = (one_way, other_way)
+    last = len(bits) - 1
+
+    def depart(wave, ways, place):
+        return [flip(held, way[place]) for held, way in zip(wave, ways)]
+
+    def join(wave, moved):
+        return [jnp.concatenate([held, got]) for held, got in zip(wave, moved)]
+
     shard_rows = query_down.shape[0]
     column = lambda gain: jnp.pad(gain[:, None], ((0, shard_rows - gain.shape[0]), (0, 0)))
-    down_shard = pad_columns(
+    gain_place = KVR + DR
+    small_shard = pad_columns(
         jnp.concatenate(
-            [query_down, latent_down]
-            + [column(gain) for gain in (attn_norm, mlp_norm, query_norm, latent_norm)],
+            [latent_down] + [column(gain) for gain in (attn_norm, mlp_norm, query_norm, latent_norm)],
             axis=1,
         ),
-        up_to(down_width + 4),
-    )
+        up_to(gain_place + 4),
+    )
+    small_wave = [small_shard[: shard_rows // 2], small_shard[shard_rows // 2 :]]
+    small_moved = depart(small_wave, both_ways, 0)
     by_quad = query_up.reshape(-1, quads, QUAD, DN + DR)
     query_shard = jnp.concatenate(
         [
@@ -597,74 +686,105 @@
     latent_shard = jnp.concatenate(
         [by_head[..., :DN].reshape(-1, H * DN), by_head[..., DN:].reshape(-1, H * DV)], axis=1
     )
-    out_half = attn_out.shape[0] // 2
-    one_way = tuple(bits)
-    other_way = tuple(bits[::-1])
-    hold = lax.optimization_barrier
-    rows = batches * local_rows
+    wave = [query_down, latent_shard, query_shard]
+    ways = (one_way, one_way, other_way)
+    moved = depart(wave, ways, 0)
+
+    def places_of(way, bit):
+        places = [0]
+        for step in way[:-1]:
+            places = places + [place ^ step for place in places]
+        return [place ^ bit for place in places], [place ^ way[-1] ^ bit for place in places]
+
+    def pieces_of(held, got, held_crossed, got_crossed, way):
+        pieces = []
+        for first, second, bit in ((held, got, 0), (held_crossed, got_crossed, 1)):
+            for piece, places in zip((first, second), places_of(way, bit)):
+                pieces.append((piece, places))
+        return pieces
+
+    small_moved, small_wave = hold((small_moved, small_wave))
+    small_wave = join(small_wave, small_moved)
+    for place in range(1, last):
+        small_wave = join(small_wave, depart(small_wave, both_ways, place))
+    small_moved = depart(small_wave, both_ways, last)
     lengths_live = query_pos[None, :] < lengths[:, None]
     live = lengths_live.astype(jnp.float32)[..., None]
-    out_grad = cotangent[0].astype(jnp.float32) * live
-    key_shard, value_shard = latent_shard[:, : H * DN], latent_shard[:, H * DN :]
-    upper_out, lower_out = attn_out[:out_half], attn_out[out_half:]
-    half_rows = local_rows // 2
-
-    wave = (down_shard, key_shard, query_shard, value_shard)
-    ways = (one_way, one_way, other_way, other_way)
-    partner_weights = [flip(weight, 1) for weight in (gate_weight, up_weight, down_weight)]
-    for place in range(len(bits)):
-        moved = [flip(held, way[place]) for held, way in zip(wave, ways)]
-        if place == 0:
-            branch_grad = low(branch_scale * out_grad)
-            moved, branch_grad, upper_out, lower_out = hold((moved, branch_grad, upper_out, lower_out))
-        else:
-            moved = hold(moved)
-        wave = [jnp.concatenate([held, got]) for held, got in zip(wave, moved)]
-        wave, branch_grad, upper_out, lower_out = hold((wave, branch_grad, upper_out, lower_out))
-    crossed = [flip(held, 1) for held in wave]
-    out_wave = (upper_out, lower_out)
-    out_ways = (one_way, other_way)
-    out_moved = [flip(held, way[0]) for held, way in zip(out_wave, out_ways)]
-    crossed, wave = hold((crossed, wave))
-    full_down, full_key, full_query, full_value = place_shards(
-        [[(held, other, way)] for held, other, way in zip(wave, crossed, ways)]
-    )
-    gains = full_down[:, down_width : down_width + 4].astype(jnp.float32).T
-    devices = lax.axis_size("fsdp")
+    flat_inputs = activations[0].reshape(rows, width)
+    inverse = lax.rsqrt(
+        jnp.mean(flat_inputs.astype(jnp.float32) ** 2, axis=-1, keepdims=True) + norm_eps
+    )
+    small_moved, small_wave, inverse, moved, wave = hold(
+        (small_moved, small_wave, inverse, moved, wave)
+    )
+    small_crossed = [flip(held, 1) for held in (*small_wave, *small_moved)]
+    wave = join(wave, moved)
+    for place in range(1, last):
+        wave = join(wave, depart(wave, ways, place))
+    small_crossed, small_wave, small_moved, wave = hold(
+        (small_crossed, small_wave, small_moved, wave)
+    )
+    moved = depart(wave, ways, last)
+    (full_small,) = place_shards(
+        [
+            [
+                pieces_of(small_wave[i], small_moved[i], small_crossed[i], small_crossed[2 + i], both_ways[i])
+                for i in range(2)
+            ]
+        ]
+    )
+    gains = full_small[:, gain_place : gain_place + 4].astype(jnp.float32).T
     spread_gain = lambda gain, size: gain.reshape(devices, -1)[:, : size // devices].reshape(-1)
     attn_gain = gains[0]
     mlp_gain = gains[1]
     query_gain = spread_gain(gains[2], query_rank)
     latent_gain = spread_gain(gains[3], KVR)
 
-    flat_inputs = activations[0].astype(jnp.float32).reshape(rows, width)
-    first_normed, first_plain, first_inverse = rms_scale(flat_inputs, attn_gain)
-    first_low = low(first_normed)
-    down_raw = matmul_plain(first_low, full_down)
-    query_mixed, query_plain, query_inverse = rms_scale(down_raw[:, :query_rank], query_gain)
-    query_low = low(query_mixed)
-    latent_raw = down_raw[:, query_rank:down_width]
+    first_inverse = inverse
+    first_low = low(flat_inputs.astype(jnp.float32) * first_inverse * attn_gain)
+    latent_raw = matmul_plain(first_low, full_small)
     latent_mixed, latent_plain, latent_inverse = rms_scale(latent_raw[:, :KVR], latent_gain)
     both_cos = jnp.tile(local_cos, (batches, 1))
     both_sin = jnp.tile(local_sin, (batches, 1))
-    key_rope_low = low(rope_apply(latent_raw[:, KVR:], both_cos, both_sin))
+    key_rope_low = low(rope_apply(latent_raw[:, KVR:gain_place], both_cos, both_sin))
     near_own = jnp.concatenate([low(latent_mixed), key_rope_low], axis=1).reshape(
-        batches, local_rows, KVR + DR
-    )
-    near_own, query_low, out_moved = hold((near_own, query_low, out_moved))
-    near = spread_line(near_own)
-    out_wave = [jnp.concatenate([held, got]) for held, got in zip(out_wave, out_moved)]
-    near, out_wave, branch_grad = hold((near, out_wave, branch_grad))
-    for place in range(1, len(bits) - 1):
-        out_moved = [flip(held, way[place]) for held, way in zip(out_wave, out_ways)]
-        out_wave = [jnp.concatenate([held, got]) for held, got in zip(out_wave, out_moved)]
-    out_moved = [flip(held, way[-1]) for held, way in zip(out_wave, out_ways)]
-    grad_wave = [branch_grad[None, :, :half_rows], branch_grad[None, :, half_rows:]]
-    grad_moved = [flip(held, way[0]) for held, way in zip(grad_wave, out_ways)]
-    near = jnp.stack(near, axis=1).reshape(batches, seq_rows, KVR + DR)
+        batches, local_rows, gain_place
+    )
+    near_own, moved, wave, attn_out = hold((near_own, moved, wave, attn_out))
+    near = lax.all_gather(near_own, "ctx", axis=1, tiled=True)
+    crossed = [flip(held, 1) for held in (*wave, *moved)]
+    out_half = attn_out.shape[0] // 2
+    out_wave = [attn_out[:out_half], attn_out[out_half:]]
+    out_moved = depart(out_wave, both_ways, 0)
+    branch_grad = low(branch_scale * (cotangent[0].astype(jnp.float32) * live))
+    crossed, wave, moved, branch_grad, bias, quad_cos, quad_ahead, quad_behind, query_gain = hold(
+        (crossed, wave, moved, branch_grad, bias, quad_cos, quad_ahead, quad_behind, query_gain)
+    )
+    full_down, full_latent, full_query = place_shards(
+        [
+            [pieces_of(wave[i], moved[i], crossed[i], crossed[3 + i], ways[i])]
+            for i in range(3)
+        ]
+    )
+    query_mixed, query_plain, query_inverse = rms_scale(
+        matmul_plain(first_low, full_down), query_gain
+    )
+    query_low = low(query_mixed)
+    query_low, out_moved, out_wave, branch_grad, near, own_weights = hold(
+        (query_low, out_moved, out_wave, branch_grad, near, (gate_weight, up_weight, down_weight))
+    )
     latent_all = near[..., :KVR]
     key_rope_all = near[..., KVR:]
     quad_rope = jnp.tile(key_rope_all, (1, 1, QUAD))
+    out_wave = join(out_wave, out_moved)
+    for place in range(1, last):
+        out_wave = join(out_wave, depart(out_wave, both_ways, place))
+    out_moved = depart(out_wave, both_ways, last)
+    other_weights = [flip(own_weights[0], 1)]
+    in_halves = lambda values, batch: [values[batch, :half_rows], values[batch, half_rows:]]
+    grad_wave = [in_halves(branch_grad, batch) for batch in range(batches)]
+    grad_moved = [None] * batches
+    grad_moved[0] = depart(grad_wave[0], both_ways, 0)
     query_turned, mixed, log_total = attend_forward(
         query_low.reshape(batches, local_rows, query_rank),
         latent_all,
@@ -674,85 +794,74 @@
         quad_ahead,
         quad_behind,
         full_query,
-        full_key,
-        full_value,
+        full_latent,
         quads,
     )
-    out_moved, mixed, grad_wave, grad_moved = hold((out_moved, mixed, grad_wave, grad_moved))
-    out_wave = [jnp.concatenate([held, got]) for held, got in zip(out_wave, out_moved)]
-    out_crossed = [flip(held, 1) for held in out_wave]
-    for place in range(1, len(bits)):
-        grad_wave = [jnp.concatenate([held, got]) for held, got in zip(grad_wave, grad_moved)]
-        grad_moved = [flip(held, way[place]) for held, way in zip(grad_wave, out_ways)]
-    gate_all, up_all, down_all = (
-        jnp.concatenate([weight, other])
-        for weight, other in zip((gate_weight, up_weight, down_weight), partner_weights)
-    )
-    out_wave, out_crossed, gate_all, up_all, down_all = hold(
-        (out_wave, out_crossed, gate_all, up_all, down_all)
-    )
+    out_moved, out_wave, mixed, grad_moved[0], grad_wave, other_weights, own_weights = hold(
+        (out_moved, out_wave, mixed, grad_moved[0], grad_wave, other_weights, own_weights)
+    )
+
+    def onward(wave, moved):
+        wave = join(wave, moved)
+        for place in range(1, last):
+            wave = join(wave, depart(wave, both_ways, place))
+        return wave, depart(wave, both_ways, last)
+
+    out_crossed = [flip(held, 1) for held in (*out_wave, *out_moved)]
+    out_wave, out_moved, out_crossed, grad_wave, grad_moved[0], other_weights, own_weights = hold(
+        (out_wave, out_moved, out_crossed, grad_wave, grad_moved[0], other_weights, own_weights)
+    )
+    grad_wave[0], grad_moved[0] = onward(grad_wave[0], grad_moved[0])
+    other_weights += [flip(weight, 1) for weight in own_weights[1:]]
     (full_out,) = place_shards(
-        [[(held, other, way) for held, other, way in zip(out_wave, out_crossed, out_ways)]]
+        [
+            [
+                pieces_of(out_wave[i], out_moved[i], out_crossed[i], out_crossed[2 + i], both_ways[i])
+                for i in range(2)
+            ]
+        ]
     )
     mixed_flat = mixed.reshape(rows, H * DV)
-    resid = flat_inputs + branch_scale * matmul_plain(mixed_flat, full_out)
-    second_normed, second_plain, second_inverse = rms_scale(resid, mlp_gain)
+    resid = flat_inputs.astype(jnp.float32) + branch_scale * matmul_plain(mixed_flat, full_out)
+    second_normed, _, second_inverse = rms_scale(resid, mlp_gain)
     second_low = low(second_normed).reshape(batches, local_rows, width)
     of_batch = lambda values, batch: values[batch * local_rows : (batch + 1) * local_rows]
-    second_low, grad_wave, grad_moved = hold((second_low, grad_wave, grad_moved))
-
-    def start_rows(batch):
-        return [second_low[batch, :half_rows], second_low[batch, half_rows:]]
-
-    def spread_rows(wave, place):
-        return [flip(held, way[place]) for held, way in zip(wave, out_ways)]
-
-    def join_rows(wave, moved):
-        return [jnp.concatenate([held, got]) for held, got in zip(wave, moved)]
-
-    rows_wave = [start_rows(batch) for batch in range(batches)]
-    rows_moved = spread_rows(rows_wave[0], 0)
-    grad_wave = join_rows(grad_wave, grad_moved)
-    grads_all = [
-        jnp.concatenate(
-            [held[:, batch].reshape(-1, width) for held in grad_wave]
-        )
-        for batch in range(batches)
-    ]
-    hidden_grads = [matmul_right(down_all, grads_all[0])]
-    rows_moved, grads_all, hidden_grads = hold((rows_moved, grads_all, hidden_grads))
-    rows_wave[0] = join_rows(rows_wave[0], rows_moved)
-    for place in range(1, len(bits) - 1):
-        rows_wave[0] = join_rows(rows_wave[0], spread_rows(rows_wave[0], place))
-    rows_moved = spread_rows(rows_wave[0], -1)
-    hidden_grads.append(matmul_right(down_all, grads_all[1]))
-    rows_moved, hidden_grads, rows_wave = hold((rows_moved, hidden_grads, rows_wave))
-    rows_all = [jnp.concatenate(join_rows(rows_wave[0], rows_moved))]
-
-    def ffn_gate(batch):
-        return matmul_right(gate_all, rows_all[batch])
-
-    def ffn_up(batch, gate_value):
-        up_value = matmul_right(up_all, rows_all[batch])
-        sigmoid_gate = jax.nn.sigmoid(gate_value)
-        silu_gate = gate_value * sigmoid_gate
-        hidden_low = low(silu_gate * up_value)
-        gate_grad = low(
-            hidden_grads[batch]
-            * up_value
-            * sigmoid_gate
-            * (1.0 + gate_value * (1.0 - sigmoid_gate))
-        )
-        up_grad = low(hidden_grads[batch] * silu_gate)
-        return hidden_low, gate_grad, up_grad
+    second_low, grad_wave, grad_moved[0], other_weights, own_weights = hold(
+        (second_low, grad_wave, grad_moved[0], other_weights, own_weights)
+    )
+
+    parts_of = lambda wave, moved: [wave[0], moved[0], wave[1], moved[1]]
+    grad_parts = [parts_of(grad_wave[0], grad_moved[0])]
+    rows_wave = [in_halves(second_low, batch) for batch in range(batches)]
+    rows_moved = [depart(rows_wave[0], both_ways, 0), None]
+    gate_all = jnp.concatenate([own_weights[0], other_weights[0]])
+    rows_moved[0], rows_wave[0], gate_all = hold((rows_moved[0], rows_wave[0], gate_all))
+    rows_wave[0], rows_moved[0] = onward(rows_wave[0], rows_moved[0])
+    up_all = jnp.concatenate([own_weights[1], other_weights[1]])
+    down_all = jnp.concatenate([own_weights[2], other_weights[2]])
+    rows_moved[0], rows_wave, grad_wave[1], grad_parts, up_all, down_all = hold(
+        (rows_moved[0], rows_wave, grad_wave[1], grad_parts, up_all, down_all)
+    )
+
+    quarter = sum(part.shape[0] for part in grad_parts[0]) // 4
+    slots = tuple((place * quarter,) for place in range(4))
+    rows_parts = [parts_of(rows_wave[0], rows_moved[0])]
+    grad_moved[1] = depart(grad_wave[1], both_ways, 0)
+    rows_moved[1] = depart(rows_wave[1], both_ways, 0)
+    units = [feed_up(rows_parts[0], grad_parts[0], gate_all, up_all, down_all)]
+    units, rows_moved[1], rows_wave[1], grad_wave[1], grad_moved[1] = hold(
+        (units, rows_moved[1], rows_wave[1], grad_wave[1], grad_moved[1])
+    )
+    rows_wave[1], rows_moved[1] = onward(rows_wave[1], rows_moved[1])
+    grad_wave[1], grad_moved[1] = onward(grad_wave[1], grad_moved[1])
+    branch_parts = feed_down([units[0][0]], [down_all], slots)
+    rows_grads = feed_down([units[0][1], units[0][2]], [gate_all, up_all], slots)
+    rows_grads, branch_parts, units, rows_moved[1], rows_wave[1], grad_wave[1], grad_moved[1] = hold(
+        (rows_grads, branch_parts, units, rows_moved[1], rows_wave[1], grad_wave[1], grad_moved[1])
+    )
 
     def scatter_first(parts):
-        quarter = parts.shape[0] // 4
-        first, second = parts[: 2 * quarter], parts[2 * quarter :]
-        return (
-            [first[:quarter], second[:quarter]],
-            [flip(first[quarter:], bits[-1]), flip(second[quarter:], bits[0])],
-        )
+        return [parts[0], parts[2]], [flip(parts[1], bits[-1]), flip(parts[3], bits[0])]
 
     def scatter_next(kept, got, place):
         joined = [low(add_up(held, value)) for held, value in zip(kept, got)]
@@ -764,73 +873,56 @@
         return [held[:half] for held in joined], moved
 
     def scatter_mid(kept, got):
-        for place in range(1, len(bits) - 1):
+        for place in range(1, last):
             kept, got = scatter_next(kept, got, place)
-        return scatter_next(kept, got, len(bits) - 1)
+        return scatter_next(kept, got, last)
 
     def scatter_end(kept, got):
         return jnp.concatenate([add_up(held, value) for held, value in zip(kept, got)])
 
-    rows_moved = spread_rows(rows_wave[1], 0)
-    gate_value = ffn_gate(0)
-    rows_moved, gate_value, rows_all = hold((rows_moved, gate_value, rows_all))
-    rows_wave[1] = join_rows(rows_wave[1], rows_moved)
-    for place in range(1, len(bits) - 1):
-        rows_wave[1] = join_rows(rows_wave[1], spread_rows(rows_wave[1], place))
-    rows_moved = spread_rows(rows_wave[1], -1)
-    ffn_parts = [ffn_up(0, gate_value)]
-    branch_part = low(matmul_left(ffn_parts[0][0], down_all))
-    rows_moved, ffn_parts, branch_part, rows_wave[1] = hold(
-        (rows_moved, ffn_parts, branch_part, rows_wave[1])
-    )
-    rows_all.append(jnp.concatenate(join_rows(rows_wave[1], rows_moved)))
-    first_out = scatter_first(branch_part)
-    gate_value = ffn_gate(1)
-    first_out, gate_value, rows_all = hold((first_out, gate_value, rows_all))
-    first_out = scatter_mid(*first_out)
-    ffn_parts.append(ffn_up(1, gate_value))
-    first_out, ffn_parts = hold((first_out, ffn_parts))
-
-    def rows_grad_of(batch):
-        return low(
-            matmul_left(ffn_parts[batch][1], gate_all) + matmul_left(ffn_parts[batch][2], up_all)
-        )
-
-    outputs = [low(of_batch(resid, 0) + branch_scale * scatter_end(*first_out))]
-    rows_grad = rows_grad_of(0)
-    outputs, rows_grad, ffn_parts = hold((outputs, rows_grad, ffn_parts))
-    first_grad_way = scatter_first(rows_grad)
-    gate_grads = [parts[1] for parts in ffn_parts]
-    up_grads = [parts[2] for parts in ffn_parts]
-    hiddens = [parts[0] for parts in ffn_parts]
-    jobs = [(hiddens, grads_all), (gate_grads, rows_all), (up_grads, rows_all)]
+    out_ways = [scatter_first(branch_parts)]
+    grad_ways = [scatter_first(rows_grads)]
+    rows_parts.append(parts_of(rows_wave[1], rows_moved[1]))
+    grad_parts.append(parts_of(grad_wave[1], grad_moved[1]))
+    units.append(feed_up(rows_parts[1], grad_parts[1], gate_all, up_all, down_all))
+    units, out_ways[0], rows_parts, grad_parts = hold((units, out_ways[0], rows_parts, grad_parts))
+
+    out_ways[0] = scatter_mid(*out_ways[0])
+    jobs = [
+        ([of[0] for of in units], grad_parts),
+        ([of[1] for of in units], rows_parts),
+        ([of[2] for of in units], rows_parts),
+    ]
     away = [weight_sums(lefts, rights, 1, None) for lefts, rights in jobs]
-    first_grad_way, away, ffn_parts = hold((first_grad_way, away, ffn_parts))
-    first_grad_way = scatter_mid(*first_grad_way)
+    away, grad_ways[0], out_ways[0], units = hold((away, grad_ways[0], out_ways[0], units))
+    grad_ways[0] = scatter_mid(*grad_ways[0])
     back = [[flip(part, 1) for part in parts] for parts in away]
-    branch_part = low(matmul_left(ffn_parts[1][0], down_all))
-    first_grad_way, back, branch_part = hold((first_grad_way, back, branch_part))
-    second_out = scatter_first(branch_part)
-    own = [weight_sums(*jobs[i], 0, back[i]) for i in range(1)]
+    branch_parts = feed_down([units[1][0]], [down_all], slots)
+    back[0], branch_parts, out_ways[0] = hold((back[0], branch_parts, out_ways[0]))
+    out_ways.append(scatter_first(branch_parts))
+    own = [weight_sums(*jobs[0], 0, back[0])]
     line = LineSum()
     line.add(*own[0])
-    sends, second_out, first_grad_way, ffn_parts = hold(
-        (line.sends(), second_out, first_grad_way, ffn_parts)
+    sends, units, grad_ways[0], out_ways[0] = hold(
+        (line.sends(), units, grad_ways[0], out_ways[0])
     )
 
     got = line.move(sends)
-    second_out = scatter_mid(*second_out)
     own += [weight_sums(*jobs[i], 0, back[i]) for i in range(1, 3)]
-    rows_grad = rows_grad_of(1)
-    got, own, rows_grad, second_out = hold((got, own, rows_grad, second_out))
+    rows_grads = feed_down([units[1][1], units[1][2]], [gate_all, up_all], slots)
+    got, own, rows_grads, out_ways[1] = hold((got, own, rows_grads, out_ways[1]))
     line.absorb(got)
     line.add(*own[1], *own[2])
 
+    def collect(part):
+        return lax.psum_scatter(part, "ctx", scatter_dimension=0, tiled=True).astype(jnp.float32)
+
     def grads_begin(batch, second_grad):
+        second_plain = of_batch(resid, batch) * of_batch(second_inverse, batch)
         second_back, mlp_gain_grad = rms_back(
-            second_grad, of_batch(second_plain, batch), of_batch(second_inverse, batch), mlp_gain
+            second_grad, second_plain, of_batch(second_inverse, batch), mlp_gain
         )
-        resid_grad = out_grad[batch] + second_back
+        resid_grad = cotangent[0, batch].astype(jnp.float32) * live[batch] + second_back
         attn_grad = low(branch_scale * resid_grad)
         mixed_grad = low(matmul_right(attn_grad, full_out))
         return resid_grad, attn_grad, mixed_grad, mlp_gain_grad
@@ -847,59 +939,65 @@
             log_total[batch],
             local_cos[:, :half].T,
             local_sin[:, :half].T,
-            full_key,
-            full_value,
+            full_latent,
             quads,
         )
         key_rope_grad = rope_grad_all.reshape(seq_rows, QUAD, DR).sum(axis=1)
         latent_part = low(jnp.concatenate([latent_grad_all, key_rope_grad], axis=1))
         return query_raw_grad, key_up_part, value_up_part, latent_part
 
-    def grads_end(batch, query_raw_grad, collected, resid_grad):
-        latent_back, latent_gain_grad = rms_back(
-            collected[:, :KVR], of_batch(latent_plain, batch), of_batch(latent_inverse, batch), latent_gain
-        )
-        latent_raw_grad = low(
-            jnp.concatenate(
-                [latent_back, rope_back(collected[:, KVR:], local_cos, local_sin)], axis=-1
-            )
-        )
+    def query_end(batch, query_raw_grad):
         query_mixed_grad = matmul_right(query_raw_grad, full_query)
         query_back, query_gain_grad = rms_back(
             query_mixed_grad, of_batch(query_plain, batch), of_batch(query_inverse, batch), query_gain
         )
-        down_grad = pad_columns(
-            jnp.concatenate([low(query_back), latent_raw_grad], axis=1), full_down.shape[1]
+        return low(query_back), query_gain_grad
+
+    def grads_end(batch, query_back, collected, resid_grad):
+        latent_back, latent_gain_grad = rms_back(
+            collected[:, :KVR], of_batch(latent_plain, batch), of_batch(latent_inverse, batch), latent_gain
         )
-        first_grad = matmul_right(down_grad, full_down)
+        latent_raw_grad = pad_columns(
+            low(
+                jnp.concatenate(
+                    [latent_back, rope_back(collected[:, KVR:], local_cos, local_sin)], axis=-1
+                )
+            ),
+            full_small.shape[1],
+        )
+        first_grad = matmul_right(query_back, full_down) + matmul_right(latent_raw_grad, full_small)
+        first_plain = of_batch(flat_inputs, batch).astype(jnp.float32) * of_batch(first_inverse, batch)
         first_back, attn_gain_grad = rms_back(
-            first_grad, of_batch(first_plain, batch), of_batch(first_inverse, batch), attn_gain
+            first_grad, first_plain, of_batch(first_inverse, batch), attn_gain
         )
-        return low(resid_grad + first_back), down_grad, attn_gain_grad, query_gain_grad, latent_gain_grad
-
-    sends, rows_grad, first_grad_way, second_out = hold(
-        (line.sends(), rows_grad, first_grad_way, second_out)
+        return low(resid_grad + first_back), latent_raw_grad, attn_gain_grad, latent_gain_grad
+
+    sends, rows_grads, grad_ways[0], out_ways[1] = hold(
+        (line.sends(), rows_grads, grad_ways[0], out_ways[1])
     )
     got = line.move(sends)
-    second_grad_way = scatter_first(rows_grad)
-    begun = [grads_begin(0, scatter_end(*first_grad_way))]
-    outputs.append(low(of_batch(resid, 1) + branch_scale * scatter_end(*second_out)))
-    got, begun, second_grad_way, outputs = hold((got, begun, second_grad_way, outputs))
+    grad_ways.append(scatter_first(rows_grads))
+    out_ways[1] = scatter_mid(*out_ways[1])
+    begun = [grads_begin(0, scatter_end(*grad_ways[0]))]
+    outputs = [low(of_batch(resid, 0) + branch_scale * scatter_end(*out_ways[0]))]
+    got, begun, grad_ways[1], outputs = hold((got, begun, grad_ways[1], outputs))
     line.absorb(got)
 
-    sends, second_grad_way, begun = hold((line.sends(), second_grad_way, begun))
+    sends, grad_ways[1], begun = hold((line.sends(), grad_ways[1], begun))
     got = line.move(sends)
-    second_grad_way = scatter_mid(*second_grad_way)
+    grad_ways[1] = scatter_mid(*grad_ways[1])
     attended = [grads_attend(0, begun[0][2])]
-    got, attended, second_grad_way, begun = hold((got, attended, second_grad_way, begun))
+    got, attended, grad_ways[1], begun = hold((got, attended, grad_ways[1], begun))
     line.absorb(got)
 
-    sends, second_grad_way, attended = hold((line.sends(), second_grad_way, attended))
+    sends, grad_ways[1], out_ways[1], attended = hold(
+        (line.sends(), grad_ways[1], out_ways[1], attended)
+    )
     got = line.move(sends)
-    begun.append(grads_begin(1, scatter_end(*second_grad_way)))
-    collected = [collect_line(attended[0][3])]
+    begun.append(grads_begin(1, scatter_end(*grad_ways[1])))
+    outputs.append(low(of_batch(resid, 1) + branch_scale * scatter_end(*out_ways[1])))
     out_sum = low(matmul_left(mixed_flat, jnp.concatenate([begun[0][1], begun[1][1]])))
-    got, begun, collected, out_sum = hold((got, begun, collected, out_sum))
+    got, begun, out_sum, outputs = hold((got, begun, out_sum, outputs))
     line.absorb(got)
     in_shards = lambda values: values.reshape(devices, -1, values.shape[-1])
     back_way = [1] + bits[::-1]
@@ -915,8 +1013,9 @@
     )
     got = line.move(sends)
     out_got = [job.move(value) for job, value in zip(out_steps, out_sends)]
+    collected = [collect(attended[0][3])]
     attended.append(grads_attend(1, begun[1][2]))
-    got, attended, out_got = hold((got, attended, out_got))
+    got, attended, out_got, begun = hold((got, attended, out_got, begun))
     line.absorb(got)
     for job, value in zip(out_steps, out_got):
         job.absorb(value)
@@ -925,52 +1024,60 @@
         (line.sends(), attended, [job.send() for job in out_steps])
     )
     got = line.move(sends)
+    collected.append(collect(attended[1][3]))
     out_got = [job.move(value) for job, value in zip(out_steps, out_sends)]
-    collected.append(collect_line(attended[1][3]))
     latent_up_sum = low(
         jnp.concatenate([attended[0][1] + attended[1][1], attended[0][2] + attended[1][2]], axis=1)
     )
     query_sum = low(matmul_left(query_low, jnp.concatenate([attended[0][0], attended[1][0]])))
-    ended = [
-        grads_end(batch, attended[batch][0], collected[batch], begun[batch][0])
-        for batch in range(batches)
-    ]
-    input_grads = [ended[batch][0] for batch in range(batches)]
-    gain_sums = [
-        ended[0][2] + ended[1][2],
-        begun[0][3] + begun[1][3],
-        ended[0][3] + ended[1][3],
-        ended[0][4] + ended[1][4],
-    ]
-    places = lax.broadcasted_iota(jnp.int32, full_down.shape, 1) - down_width
-    down_sum = matmul_left(first_low, jnp.concatenate([ended[0][1], ended[1][1]]))
-    gathered_gain = lambda gain: jnp.pad(
-        gain.reshape(devices, -1), ((0, 0), (0, shard_rows - gain.shape[0] // devices))
-    ).reshape(-1)
-    gain_columns = gain_sums[:2] + [gathered_gain(gain) for gain in gain_sums[2:]]
-    for place, gain in enumerate(gain_columns):
-        down_sum = jnp.where(places == place, gain[:, None], down_sum)
-    down_sum = low(down_sum)
-    got, out_got, latent_up_sum, query_sum, down_sum = hold(
-        (got, out_got, latent_up_sum, query_sum, down_sum)
+    query_ends = [query_end(batch, attended[batch][0]) for batch in range(batches)]
+    down_sum = low(matmul_left(first_low, jnp.concatenate([query_ends[0][0], query_ends[1][0]])))
+    got, out_got, latent_up_sum, query_sum, down_sum, query_ends = hold(
+        (got, out_got, latent_up_sum, query_sum, down_sum, query_ends)
     )
     line.absorb(got)
     for job, value in zip(out_steps, out_got):
         job.absorb(value)
-
     steps = [
-        ScatterWhole(in_shards(down_sum), back_way),
         ScatterWhole(in_shards(query_sum), back_other),
         ScatterWhole(in_shards(latent_up_sum), back_way),
+        ScatterWhole(in_shards(down_sum), back_way),
     ]
-    while line.busy() or steps:
-        jobs = [job for job in out_steps + steps if job.order]
-        sends, values = hold((line.sends(), [job.send() for job in jobs]))
+
+    small_steps = None
+    while line.busy() or steps or small_steps != []:
+        running = [job for job in out_steps + steps + (small_steps or []) if job.order]
+        sends, values, query_ends, collected = hold(
+            (line.sends(), [job.send() for job in running], query_ends, collected)
+        )
         got = line.move(sends)
-        values = [job.move(value) for job, value in zip(jobs, values)]
-        got, values = hold((got, values))
+        values = [job.move(value) for job, value in zip(running, values)]
+        if small_steps is None:
+            ended = [
+                grads_end(batch, query_ends[batch][0], collected[batch], begun[batch][0])
+                for batch in range(batches)
+            ]
+            input_grads = [of[0] for of in ended]
+            small_sum = matmul_left(first_low, jnp.concatenate([of[1] for of in ended]))
+            places = lax.broadcasted_iota(jnp.int32, full_small.shape, 1) - gain_place
+            gathered_gain = lambda gain: jnp.pad(
+                gain.reshape(devices, -1), ((0, 0), (0, shard_rows - gain.shape[0] // devices))
+            ).reshape(-1)
+            gain_columns = [
+                ended[0][2] + ended[1][2],
+                begun[0][3] + begun[1][3],
+                gathered_gain(query_ends[0][1] + query_ends[1][1]),
+                gathered_gain(ended[0][3] + ended[1][3]),
+            ]
+            for place, gain in enumerate(gain_columns):
+                small_sum = jnp.where(places == place, gain[:, None], small_sum)
+            small_sum = low(small_sum)
+            got, values, small_sum = hold((got, values, small_sum))
+            small_steps = [ScatterWhole(in_shards(small_sum), back_other)]
+        else:
+            got, values = hold((got, values))
         line.absorb(got)
-        for job, value in zip(jobs, values):
+        for job, value in zip(running, values):
             job.absorb(value)
         if out_steps and not any(job.order for job in out_steps):
             line.add(jnp.concatenate([job.held[0] for job in out_steps]))
@@ -978,9 +1085,12 @@
         if steps and not any(job.order for job in steps):
             line.add(*[job.held[0] for job in steps])
             steps = []
+        if small_steps and not small_steps[0].order:
+            line.add(small_steps[0].held[0])
+            small_steps = []
     totals = [total.astype(jnp.float32) for total in line.held]
     ffn_totals = [jnp.concatenate(totals[2 * i : 2 * i + 2]) for i in (1, 2, 0)]
-    out_total, down_total, query_total, latent_total = totals[6:]
+    out_total, query_total, latent_total, down_total, small_total = totals[6:]
     by_quad = query_total.reshape(-1, quads, QUAD * (DN + DR))
     query_up_total = jnp.concatenate(
         [
@@ -999,15 +1109,15 @@
     return (
         jnp.stack(outputs)[None],
         jnp.stack(input_grads)[None],
-        down_total[:, down_width],
-        down_total[:, :query_rank],
-        down_total[: query_norm.shape[0], down_width + 2],
+        small_total[:, gain_place],
+        down_total,
+        small_total[: query_norm.shape[0], gain_place + 2],
         query_up_total,
-        down_total[:, query_rank:down_width],
-        down_total[: latent_norm.shape[0], down_width + 3],
+        small_total[:, :gain_place],
+        small_total[: latent_norm.shape[0], gain_place + 3],
         latent_up_total,
         out_total,
-        down_total[:, down_width + 1],
+        small_total[:, gain_place + 1],
         ffn_totals[0],
         ffn_totals[1],
         ffn_totals[2],

time: 1380 us -> 1300 us (0.942)
  matrix products: 239 us -> 69 us
  Pallas kernels: 236 us -> 391 us
  waiting for transfers between devices: 341 us -> 295 us
  other arithmetic: 248 us -> 208 us
  local copies, waits for them, and re-layouts: 152 us -> 167 us
    pallas_call x6 -> x12, Pallas kernels: 74 us -> 227 us  [the longest x4 81.9 us: feed_down(): pl.pallas_call(functools.partial(down_kernel, len(units), slots), grid=(w...]
    dot_general x9 -> x4, matrix products: 114 us -> 22.2 us  [matmul_left(): lax.dot_general(left, right, (((0,), (0,)), ((), ())), preferred_element_...]
    dot_general x12 -> x8, matrix products: 109 us -> 32.4 us  [matmul_right(): lax.dot_general(left, right, (((1,), (1,)), ((), ())), preferred_element_...]
    ppermute x70 -> x87, waiting for transfers between devices: 223 us -> 166 us  [flip(): return lax.ppermute(values, 'fsdp', [(i, i ^ bit) for i in range(count)])]
    ppermute x9 -> x0, waiting for transfers between devices: 38.7 us -> none  [the longest x6 25.6 us: collect_line(): lax.ppermute(low(parts[k * rows:(k + 1) * rows]), 'ctx', [(i, (i - k) % c...]
    ppermute x26 -> x29, waiting for transfers between devices: 79.5 us -> 110 us  [move(): lax.ppermute(value, 'ctx', pairs)]
    concatenate x19 -> x9, other arithmetic: 48.5 us -> 27.5 us  [the longest x1 7.32 us: body(): up_all = jnp.concatenate([own_weights[1], other_weights[1]])]
    ppermute x9 -> x0, starting transfers between devices: 16.1 us -> none  [the longest x6 10.6 us: collect_line(): lax.ppermute(low(parts[k * rows:(k + 1) * rows]), 'ctx', [(i, (i - k) % c...]
  transfers between devices with their start and end apart: 105 -> 119, of which waited for: 34 -> 36; matrix products, arithmetic and copies ran while one was open for 33% -> 21% of each run, Pallas kernels for 17% -> 30%
where the time goes in v2:
time: 1300 us; the launch traced here: 1290 us
  Pallas kernels  391 us (30%)
  waiting for transfers between devices  295 us (23%)
  other arithmetic  208 us (16%)
  local copies, waits for them, and re-layouts  167 us (13%)
  starting transfers between devices  141 us (11%)
  matrix products  69 us (5%)
  between operations  17.3 us (1%)
    ppermute x87, waiting for transfers between devices, flip(): return lax.ppermute(values, 'fsdp', [(i, i ^ bit) for i in range(count)])  166 us
    ppermute x29, waiting for transfers between devices, move(): lax.ppermute(value, 'ctx', pairs)  110 us
    pallas_call x2, Pallas kernels, attend_backward(): pl.pallas_call(backward_kernel, grid=(quads,), in_specs=[pl.BlockSpec((ro...  93.8 us
    convert_element_type x47, other arithmetic, low(): return values.astype(jnp.bfloat16)  84.5 us
    pallas_call x4, Pallas kernels, feed_down(): pl.pallas_call(functools.partial(down_kernel, len(units), slots), grid=(w...  81.9 us
    pallas_call x6, Pallas kernels, weight_sums(): pl.pallas_call(functools.partial(weight_kernel, len(lefts), tuple((len(pi...  77 us
    ppermute x29, starting transfers between devices, move(): lax.ppermute(value, 'ctx', pairs)  72.5 us
    pallas_call x2, Pallas kernels, feed_up(): pl.pallas_call(functools.partial(up_kernel, len(rows_parts)), grid=(units...  67.9 us
  transfers between devices with their start and end apart: 119, of which 36 were waited for; matrix products, arithmetic and copies ran while one was open for 21% of the time, Pallas kernels for 30%

profile of v2, /device:TPU:0, one launch (start us, length us, event | category | flops | bytes accessed | tf_op | source)
XLA Modules:
  0.0 1288.2 jit_solution(18007903233043624711)
XLA Ops:
  39.9 7.5 collective-permute-done.3.refs_5_
  76.5 27.6 %collective-permute-done.12.refs_5_ = bf16[64,5120]{1,0:T(8,128)(2,1)} collective-permute-done((bf16[64,5120]{1,0:T(8,128)(2,1)}, bf16[64,5120]{1,0:T(8,128)(2,1)}, u32[]{:S(2)}, u32[]{:S(2)}) %collective-permute-start.12) | collective-permute-done | bytes 655392 | tf_op jit(solution)/shard_map/ppermute | solution.py:86
  123.2 7.5 place_shards.4
  138.1 4.9 all-gather.2.cloned.1.call-done
  165.9 51.9 %attend_forward.1 = (bf16[2,256,3840]{2,1,0:T(8,128)(2,1)}, bf16[2,256,2560]{2,1,0:T(8,128)(2,1)}, f32[2,10,4,256]{3,2,1,0:T(4,128)S(1)}) custom-call(bf16[2,256,768]{2,1,0:T(8,128)(2,1)S(1)} %bitcast.252, bf16[2,1024,256]{2,1,0:T(8,128)(2,1)S(1)} %copy.209.latent_ref, bf16[2,1024,128]{2,1,0:T(8,128)(2,1)S(1)} %copy-done.26, ...), custom_call_target="tpu_custom_call" | custom-call | flops 29863444480 | bytes 41943040 | tf_op jit(solution)/shard_map/attend_forward/pallas_call | solution.py:233
  233.7 4.5 slice_bitcast_fusion
  243.6 9.2 place_shards.5
  252.8 10.9 multiply_reduce_fusion
  266.0 6.1 collective-permute-done.32.refs_7_.refs_5_
  276.6 7.3 pad_maximum_fusion.gate_w.refs_2_
  283.9 6.8 collective-permute-done.35
  296.4 7.3 pad_maximum_fusion.2.down_w.refs_1_
  303.7 7.3 pad_maximum_fusion.1.up_w.refs_3_
  311.0 10.7 collective-permute-done.38.refs_3_.refs_5_
  327.8 34.0 %feed_up.2 = (bf16[1600,1024]{1,0:T(8,128)(2,1)}, bf16[1600,1024]{1,0:T(8,128)(2,1)}, bf16[1600,1024]{1,0:T(8,128)(2,1)}) custom-call(bf16[1600,2560]{1,0:T(8,128)(2,1)} %pad_maximum_fusion.gate_w.refs_2_, bf16[1600,2560]{1,0:T(8,128)(2,1)} %pad_maximum_fusion.1.up_w.refs_3_, bf16[1600,2560]{1,0:T(8,128)(2,1)} %pad_maximum_fusion.2.down_w.refs_1_, ...), custom_call_target="tpu_custom_call" | custom-call | flops 25165824000 | bytes 44892160 | tf_op jit(solution)/shard_map/feed_up/pallas_call | solution.py:476
  366.6 14.0 %feed_down.5 = (bf16[256,2560]{1,0:T(8,128)(2,1)S(1)}, bf16[256,2560]{1,0:T(8,128)(2,1)S(1)}, bf16[256,2560]{1,0:T(8,128)(2,1)S(1)}, bf16[256,2560]{1,0:T(8,128)(2,1)S(1)}) custom-call(bf16[1600,1024]{1,0:T(8,128)(2,1)} %get-tuple-element.660.refs_0_, bf16[1600,2560]{1,0:T(8,128)(2,1)} %pad_maximum_fusion.2.down_w.refs_1_), custom_call_target="tpu_custom_call" | custom-call | flops 8388608000 | bytes 16711680 | tf_op jit(solution)/shard_map/feed_down/pallas_call | solution.py:517
  382.9 26.8 %feed_down.4 = (bf16[256,2560]{1,0:T(8,128)(2,1)S(1)}, bf16[256,2560]{1,0:T(8,128)(2,1)}, bf16[256,2560]{1,0:T(8,128)(2,1)S(1)}, bf16[256,2560]{1,0:T(8,128)(2,1)}) custom-call(bf16[1600,1024]{1,0:T(8,128)(2,1)} %get-tuple-element.672.refs_0_, bf16[1600,1024]{1,0:T(8,128)(2,1)} %get-tuple-element.684.refs_1_.refs_0_, ...), custom_call_target="tpu_custom_call" | custom-call | flops 16777216000 | bytes 28180480 | tf_op jit(solution)/shard_map/feed_down/pallas_call | solution.py:517
  409.6 7.1 collective-permute-done.44.refs_3_.refs_9_
  425.4 33.9 %feed_up.3 = (bf16[1600,1024]{1,0:T(8,128)(2,1)}, bf16[1600,1024]{1,0:T(8,128)(2,1)}, bf16[1600,1024]{1,0:T(8,128)(2,1)}) custom-call(bf16[1600,2560]{1,0:T(8,128)(2,1)} %pad_maximum_fusion.gate_w.refs_2_, bf16[1600,2560]{1,0:T(8,128)(2,1)} %pad_maximum_fusion.1.up_w.refs_3_, bf16[1600,2560]{1,0:T(8,128)(2,1)} %pad_maximum_fusion.2.down_w.refs_1_, ...), custom_call_target="tpu_custom_call" | custom-call | flops 25165824000 | bytes 44892160 | tf_op jit(solution)/shard_map/feed_up/pallas_call | solution.py:476
  466.8 12.7 weight_sums.8
  480.9 13.0 %weight_sums.7 = (bf16[400,2560]{1,0:T(8,128)(2,1)}, bf16[400,2560]{1,0:T(8,128)(2,1)}) custom-call(bf16[1600,1024]{1,0:T(8,128)(2,1)} %get-tuple-element.672.refs_0_, bf16[1600,1024]{1,0:T(8,128)(2,1)} %get-tuple-element.730.refs_1_.refs_0_, bf16[256,2560]{1,0:T(8,128)(2,1)S(1)} %constant_dynamic-update-slice_fusion.14.refs_0_.refs_2_, ...), custom_call_target="tpu_custom_call" | custom-call | flops 8388608000 | bytes 17858560 | tf_op jit(solution)/shard_map/weight_sums/pallas_call | solution.py:565
  496.5 13.0 %weight_sums.6 = (bf16[400,2560]{1,0:T(8,128)(2,1)}, bf16[400,2560]{1,0:T(8,128)(2,1)}) custom-call(bf16[1600,1024]{1,0:T(8,128)(2,1)} %get-tuple-element.660.refs_0_, bf16[1600,1024]{1,0:T(8,128)(2,1)} %get-tuple-element.698.refs_1_.refs_0_, bf16[256,2560]{1,0:T(8,128)(2,1)S(1)} %copy-done.34, bf16[256,2560]{1,0:T(8,128)(2,1)S(1)} %copy-done.69, ...), custom_call_target="tpu_custom_call" | custom-call | flops 8388608000 | bytes 17858560 | tf_op jit(solution)/shard_map/weight_sums/pallas_call | solution.py:565
  514.5 14.7 %feed_down.6 = (bf16[256,2560]{1,0:T(8,128)(2,1)S(1)}, bf16[256,2560]{1,0:T(8,128)(2,1)}, bf16[256,2560]{1,0:T(8,128)(2,1)S(1)}, bf16[256,2560]{1,0:T(8,128)(2,1)}) custom-call(bf16[1600,1024]{1,0:T(8,128)(2,1)} %get-tuple-element.698.refs_1_.refs_0_, bf16[1600,2560]{1,0:T(8,128)(2,1)} %pad_maximum_fusion.2.down_w.refs_1_), custom_call_target="tpu_custom_call" | custom-call | flops 8388608000 | bytes 16711680 | tf_op jit(solution)/shard_map/feed_down/pallas_call | solution.py:517
  536.5 13.1 %weight_sums.9 = (bf16[400,2560]{1,0:T(8,128)(2,1)}, bf16[400,2560]{1,0:T(8,128)(2,1)S(1)}) custom-call(bf16[1600,1024]{1,0:T(8,128)(2,1)} %get-tuple-element.660.refs_0_, bf16[1600,1024]{1,0:T(8,128)(2,1)} %get-tuple-element.698.refs_1_.refs_0_, bf16[256,2560]{1,0:T(8,128)(2,1)S(1)} %copy-done.34, bf16[256,2560]{1,0:T(8,128)(2,1)S(1)} %copy-done.70, ...), custom_call_target="tpu_custom_call" | custom-call | flops 8388608000 | bytes 17858560 | tf_op jit(solution)/shard_map/weight_sums/pallas_call | solution.py:565
  549.6 6.1 collective-permute-start.57
  560.0 12.8 weight_sums.11
  576.8 12.5 weight_sums.10
  592.0 26.4 %feed_down.7 = (bf16[256,2560]{1,0:T(8,128)(2,1)S(1)}, bf16[256,2560]{1,0:T(8,128)(2,1)}, bf16[256,2560]{1,0:T(8,128)(2,1)S(1)}, bf16[256,2560]{1,0:T(8,128)(2,1)S(1)}) custom-call(bf16[1600,1024]{1,0:T(8,128)(2,1)} %get-tuple-element.730.refs_1_.refs_0_, bf16[1600,1024]{1,0:T(8,128)(2,1)} %get-tuple-element.731.refs_1_, ...), custom_call_target="tpu_custom_call" | custom-call | flops 16777216000 | bytes 28180480 | tf_op jit(solution)/shard_map/feed_down/pallas_call | solution.py:517
  618.5 4.5 add_convert_fusion.11
  644.8 8.7 convolution_convert_fusion.4.grad_ref
  653.5 10.8 collective-permute-done.66
  664.2 8.4 collective-permute-done.64
  693.2 46.7 %attend_backward.2 = (bf16[256,3840]{1,0:T(8,128)(2,1)}, f32[256,2560]{1,0:T(8,128)}, f32[256,2560]{1,0:T(8,128)}, f32[1024,256]{1,0:T(8,128)S(1)}, f32[1024,128]{1,0:T(8,128)S(1)}) custom-call(bf16[256,3840]{1,0:T(8,128)(2,1)} %get-tuple-element.1077.query_ref, bf16[256,2560]{1,0:T(8,128)(2,1)S(1)} %convolution_convert_fusion.4.grad_ref, ...), custom_call_target="tpu_custom_call" | custom-call | flops 34896609280 | bytes 26214400 | tf_op jit(solution)/shard_map/attend_backward/pallas_call | solution.py:338
  746.1 5.0 broadcast_select_fusion.8
  753.4 6.5 collective-permute-done.72
  770.8 9.8 convolution_convert_fusion.3.grad_ref
  780.6 5.0 broadcast_select_fusion.1
  785.6 10.0 convolution_convert_fusion
  795.6 11.5 collective-permute-done.74
  807.1 6.3 fusion.93
  836.1 47.1 %attend_backward.3 = (bf16[256,3840]{1,0:T(8,128)(2,1)}, f32[256,2560]{1,0:T(8,128)}, f32[256,2560]{1,0:T(8,128)}, f32[1024,256]{1,0:T(8,128)S(1)}, f32[1024,128]{1,0:T(8,128)S(1)}) custom-call(bf16[256,3840]{1,0:T(8,128)(2,1)} %get-tuple-element.1076.query_ref, bf16[256,2560]{1,0:T(8,128)(2,1)S(1)} %copy-done.73, bf16[1024,256]{1,0:T(8,128)(2,1)S(1)} %copy-done.24, ...), custom_call_target="tpu_custom_call" | custom-call | flops 34896609280 | bytes 26214400 | tf_op jit(solution)/shard_map/attend_backward/pallas_call | solution.py:338
  896.8 4.5 maximum_convert_fusion.2
  906.1 5.0 fusion.1
  911.1 4.6 add_convert_fusion.4
  945.6 5.1 convolution_convert_fusion.1
  950.7 13.4 %reduce-scatter.5.cloned.1.call-done = bf16[256,288]{1,0:T(8,128)(2,1)} async-done(((bf16[1024,288]{1,0:T(8,128)(2,1)}), bf16[256,288]{1,0:T(8,128)(2,1)}) %reduce-scatter.5.cloned.1.call-update) | async-done | bytes 147472 | tf_op jit(solution)/shard_map/reduce_scatter | solution.py:918
  965.5 18.1 %collective-permute-done.80 = bf16[400,2560]{1,0:T(8,128)(2,1)} collective-permute-done((bf16[400,2560]{1,0:T(8,128)(2,1)}, bf16[400,2560]{1,0:T(8,128)(2,1)}, u32[]{:S(2)}, u32[]{:S(2)}) %collective-permute-start.80) | collective-permute-done | bytes 2048032 | tf_op jit(solution)/shard_map/ppermute | solution.py:432
  1016.0 15.6 %collective-permute-done.86 = bf16[1,1,160,2560]{3,2,1,0:T(8,128)(2,1)S(1)} collective-permute-done((bf16[1,1,160,2560]{3,2,1,0:T(8,128)(2,1)S(1)}, bf16[1,1,160,2560]{3,2,1,0:T(8,128)(2,1)S(1)}, u32[]{:S(2)}, u32[]{:S(2)}) %collective-permute-start.86) | collective-permute-done | bytes 819232 | tf_op jit(solution)/shard_map/ppermute | solution.py:86
  1041.6 16.3 %collective-permute-done.84 = bf16[400,2560]{1,0:T(8,128)(2,1)} collective-permute-done((bf16[400,2560]{1,0:T(8,128)(2,1)}, bf16[400,2560]{1,0:T(8,128)(2,1)}, u32[]{:S(2)}, u32[]{:S(2)}) %collective-permute-start.84) | collective-permute-done | bytes 2048032 | tf_op jit(solution)/shard_map/ppermute | solution.py:432
  1078.5 6.7 collective-permute-start.91
  1094.6 15.4 %collective-permute-done.95 = bf16[1,2,320,768]{3,2,1,0:T(8,128)(2,1)} collective-permute-done((bf16[1,2,320,768]{3,2,1,0:T(8,128)(2,1)}, bf16[1,2,320,768]{3,2,1,0:T(8,128)(2,1)}, u32[]{:S(2)}, u32[]{:S(2)}) %collective-permute-start.95) | collective-permute-done | bytes 983072 | tf_op jit(solution)/shard_map/ppermute | solution.py:86
  1110.0 9.2 collective-permute-done.93
  1119.8 7.5 collective-permute-done.92
  1135.2 4.5 maximum_convert_fusion
  1145.3 24.9 %collective-permute-done.99 = bf16[1,1,32,5120]{3,2,1,0:T(8,128)(2,1)S(1)} collective-permute-done((bf16[1,1,32,5120]{3,2,1,0:T(8,128)(2,1)S(1)}, bf16[1,1,32,5120]{3,2,1,0:T(8,128)(2,1)S(1)}, u32[]{:S(2)}, u32[]{:S(2)}) %collective-permute-start.99) | collective-permute-done | bytes 327712 | tf_op jit(solution)/shard_map/ppermute | solution.py:86
  1172.4 4.7 collective-permute-start.102
  1178.4 5.0 collective-permute-done.104
  1183.4 7.3 collective-permute-done.102
  1190.7 17.8 %collective-permute-done.103 = bf16[320,2560]{1,0:T(8,128)(2,1)S(1)} collective-permute-done((bf16[320,2560]{1,0:T(8,128)(2,1)S(1)}, bf16[320,2560]{1,0:T(8,128)(2,1)S(1)}, u32[]{:S(2)}, u32[]{:S(2)}) %collective-permute-start.103) | collective-permute-done | bytes 1638432 | tf_op jit(solution)/shard_map/ppermute | solution.py:432
  1212.8 4.5 maximum_convert_fusion.1
  1219.0 10.0 collective-permute-start.107
  1244.3 6.0 collective-permute-start.110
  1260.6 9.2 collective-permute-done.113
  1272.2 5.8 collective-permute-done.115
  (939 shorter events, 460.4 us)
Async XLA Ops:
  7.2 135.8 %all-gather.2.cloned.1.call-start = ((), (), s32[]{:S(2)}) async-start(), calls=%async_computation.2 | async-start | bytes 1474560 | tf_op jit(solution)/shard_map/all_gather | solution.py:754
  60.2 43.9 %collective-permute-start.13 = (bf16[192,3840]{1,0:T(8,128)(2,1)}, bf16[192,3840]{1,0:T(8,128)(2,1)}, u32[]{:S(2)}, u32[]{:S(2)}) collective-permute-start(bf16[192,3840]{1,0:T(8,128)(2,1)} %pad_maximum_fusion.8.refs_8_), channel_id=1, source_target_pairs={{0,2},{1,3},{2,0},{3,1},{4,6},{5,7},{6,4},{7,5},{8,10},{9,11},{10,... | collective-permute-start | bytes 4423688 | tf_op jit(solution)/shard_map/ppermute | solution.py:86
  66.6 37.5 %collective-permute-start.11 = (bf16[640,768]{1,0:T(8,128)(2,1)S(1)}, bf16[640,768]{1,0:T(8,128)(2,1)}, u32[]{:S(2)}, u32[]{:S(2)}) collective-permute-start(bf16[640,768]{1,0:T(8,128)(2,1)S(1)} %pad_maximum_fusion.10.refs_0_), channel_id=1, source_target_pairs={{0,4},{1,5},{2,6},{3,7},{4,0},{5,1},{6,2},{7,3},{8,12},{9,13},{10,... | collective-permute-start | bytes 2949128 | tf_op jit(solution)/shard_map/ppermute | solution.py:86
  69.5 34.6 %collective-permute-start.12 = (bf16[64,5120]{1,0:T(8,128)(2,1)}, bf16[64,5120]{1,0:T(8,128)(2,1)}, u32[]{:S(2)}, u32[]{:S(2)}) collective-permute-start(bf16[64,5120]{1,0:T(8,128)(2,1)} %pad_maximum_fusion.13.refs_4_), channel_id=1, source_target_pairs={{0,4},{1,5},{2,6},{3,7},{4,0},{5,1},{6,2},{7,3},{8,12},{9,13},{10,... | collective-permute-start | bytes 1966088 | tf_op jit(solution)/shard_map/ppermute | solution.py:86
  109.5 791.8 %reduce-scatter.3.cloned.1.call-start = ((), (), s32[]{:S(2)}) async-start(), calls=%async_computation.3 | async-start | bytes 983040 | tf_op jit(solution)/shard_map/reduce_scatter | solution.py:918
  156.4 62.0 %collective-permute-start.23 = (bf16[320,2560]{1,0:T(8,128)(2,1)}, bf16[320,2560]{1,0:T(8,128)(2,1)}, u32[]{:S(2)}, u32[]{:S(2)}) collective-permute-start(bf16[320,2560]{1,0:T(8,128)(2,1)} %constant_dynamic-update-slice_fusion.8.refs_4_), channel_id=1, source_target_pairs={{0,2},{1,3},{2,0},{3,1},{4,6},{5,7},{6,4},{7,5},{8,10},{9,11},{10,... | collective-permute-start | bytes 4915208 | tf_op jit(solution)/shard_map/ppermute | solution.py:86
  157.4 61.0 %collective-permute-start.26 = (bf16[800,2560]{1,0:T(8,128)(2,1)}, bf16[800,2560]{1,0:T(8,128)(2,1)S(1)}, u32[]{:S(2)}, u32[]{:S(2)}) collective-permute-start(bf16[800,2560]{1,0:T(8,128)(2,1)} %param.29), channel_id=1, source_target_pairs={{0,1},{1,0},{2,3},{3,2},{4,5},{5,4},{6,7},{7,6},{8,9},{9,8},{10,11... | collective-permute-start | bytes 12288008 | tf_op jit(solution)/shard_map/ppermute | solution.py:86
  161.6 56.8 %collective-permute-start.22 = (bf16[320,2560]{1,0:T(8,128)(2,1)}, bf16[320,2560]{1,0:T(8,128)(2,1)}, u32[]{:S(2)}, u32[]{:S(2)}) collective-permute-start(bf16[320,2560]{1,0:T(8,128)(2,1)} %constant_dynamic-update-slice_fusion.6.refs_0_), channel_id=1, source_target_pairs={{0,4},{1,5},{2,6},{3,7},{4,0},{5,1},{6,2},{7,3},{8,12},{9,13},{10,... | collective-permute-start | bytes 4915208 | tf_op jit(solution)/shard_map/ppermute | solution.py:86
  164.3 54.1 %collective-permute-start.24 = (bf16[128,2560]{1,0:T(8,128)(2,1)S(1)}, bf16[128,2560]{1,0:T(8,128)(2,1)S(1)}, u32[]{:S(2)}, u32[]{:S(2)}) collective-permute-start(bf16[128,2560]{1,0:T(8,128)(2,1)S(1)} %get-tuple-element.578), channel_id=1, source_target_pairs={{0,2},{1,3},{2,0},{3,1},{4,6},{5,7},{6,4},{7,5},{8,10},{9,11},{10,... | collective-permute-start | bytes 1966088 | tf_op jit(solution)/shard_map/ppermute | solution.py:86
  164.9 53.5 %collective-permute-start.25 = (bf16[128,2560]{1,0:T(8,128)(2,1)S(1)}, bf16[128,2560]{1,0:T(8,128)(2,1)S(1)}, u32[]{:S(2)}, u32[]{:S(2)}) collective-permute-start(bf16[128,2560]{1,0:T(8,128)(2,1)S(1)} %get-tuple-element.580), channel_id=1, source_target_pairs={{0,4},{1,5},{2,6},{3,7},{4,0},{5,1},{6,2},{7,3},{8,12},{9,13},{10,... | collective-permute-start | bytes 1966088 | tf_op jit(solution)/shard_map/ppermute | solution.py:86
  238.3 34.8 %collective-permute-start.33 = (bf16[800,2560]{1,0:T(8,128)(2,1)S(1)}, bf16[800,2560]{1,0:T(8,128)(2,1)}, u32[]{:S(2)}, u32[]{:S(2)}) collective-permute-start(bf16[800,2560]{1,0:T(8,128)(2,1)S(1)} %copy-done.111), channel_id=1, source_target_pairs={{0,1},{1,0},{2,3},{3,2},{4,5},{5,4},{6,7},{7,6},{8,9},{9,8},{10,11... | collective-permute-start | bytes 12288008 | tf_op jit(solution)/shard_map/ppermute | solution.py:86
  239.7 33.4 %collective-permute-start.34 = (bf16[800,2560]{1,0:T(8,128)(2,1)S(1)}, bf16[800,2560]{1,0:T(8,128)(2,1)}, u32[]{:S(2)}, u32[]{:S(2)}) collective-permute-start(bf16[800,2560]{1,0:T(8,128)(2,1)S(1)} %copy-done.110), channel_id=1, source_target_pairs={{0,1},{1,0},{2,3},{3,2},{4,5},{5,4},{6,7},{7,6},{8,9},{9,8},{10,11... | collective-permute-start | bytes 12288008 | tf_op jit(solution)/shard_map/ppermute | solution.py:86
  240.8 31.3 %collective-permute-start.32 = (bf16[256,2560]{1,0:T(8,128)(2,1)S(1)}, bf16[256,2560]{1,0:T(8,128)(2,1)S(1)}, u32[]{:S(2)}, u32[]{:S(2)}) collective-permute-start(bf16[256,2560]{1,0:T(8,128)(2,1)S(1)} %constant_dynamic-update-slice_fusion.12.refs_6_.refs_4_), channel_id=1, source_target_pairs={{0,2},{1,3},{2,0},{3,1},{4,6},{5,7},{6,4},{7,5},{8,10},{9,11},{10,... | collective-permute-start | bytes 3932168 | tf_op jit(solution)/shard_map/ppermute | solution.py:86
  242.1 31.0 %collective-permute-start.31 = (bf16[256,2560]{1,0:T(8,128)(2,1)S(1)}, bf16[256,2560]{1,0:T(8,128)(2,1)S(1)}, u32[]{:S(2)}, u32[]{:S(2)}) collective-permute-start(bf16[256,2560]{1,0:T(8,128)(2,1)S(1)} %constant_dynamic-update-slice_fusion.10.refs_4_.refs_2_), channel_id=1, source_target_pairs={{0,4},{1,5},{2,6},{3,7},{4,0},{5,1},{6,2},{7,3},{8,12},{9,13},{10,... | collective-permute-start | bytes 3932168 | tf_op jit(solution)/shard_map/ppermute | solution.py:86
  323.7 38.0 %collective-permute-start.39 = (bf16[128,2560]{1,0:T(8,128)(2,1)}, bf16[128,2560]{1,0:T(8,128)(2,1)S(1)}, u32[]{:S(2)}, u32[]{:S(2)}) collective-permute-start(bf16[128,2560]{1,0:T(8,128)(2,1)} %get-tuple-element.634), channel_id=1, source_target_pairs={{0,2},{1,3},{2,0},{3,1},{4,6},{5,7},{6,4},{7,5},{8,10},{9,11},{10,... | collective-permute-start | bytes 1966088 | tf_op jit(solution)/shard_map/ppermute | solution.py:86
  324.7 37.1 %collective-permute-start.40 = (bf16[128,2560]{1,0:T(8,128)(2,1)}, bf16[128,2560]{1,0:T(8,128)(2,1)S(1)}, u32[]{:S(2)}, u32[]{:S(2)}) collective-permute-start(bf16[128,2560]{1,0:T(8,128)(2,1)} %get-tuple-element.636), channel_id=1, source_target_pairs={{0,4},{1,5},{2,6},{3,7},{4,0},{5,1},{6,2},{7,3},{8,12},{9,13},{10,... | collective-permute-start | bytes 1966088 | tf_op jit(solution)/shard_map/ppermute | solution.py:86
  326.2 35.6 %collective-permute-start.41 = (bf16[128,2560]{1,0:T(8,128)(2,1)S(1)}, bf16[128,2560]{1,0:T(8,128)(2,1)S(1)}, u32[]{:S(2)}, u32[]{:S(2)}) collective-permute-start(bf16[128,2560]{1,0:T(8,128)(2,1)S(1)} %copy-done.124), channel_id=1, source_target_pairs={{0,2},{1,3},{2,0},{3,1},{4,6},{5,7},{6,4},{7,5},{8,10},{9,11},{10,... | collective-permute-start | bytes 1966088 | tf_op jit(solution)/shard_map/ppermute | solution.py:86
  327.2 34.6 %collective-permute-start.42 = (bf16[128,2560]{1,0:T(8,128)(2,1)}, bf16[128,2560]{1,0:T(8,128)(2,1)S(1)}, u32[]{:S(2)}, u32[]{:S(2)}) collective-permute-start(bf16[128,2560]{1,0:T(8,128)(2,1)} %get-tuple-element.640), channel_id=1, source_target_pairs={{0,4},{1,5},{2,6},{3,7},{4,0},{5,1},{6,2},{7,3},{8,12},{9,13},{10,... | collective-permute-start | bytes 1966088 | tf_op jit(solution)/shard_map/ppermute | solution.py:86
  362.0 47.7 %collective-permute-start.46 = (bf16[256,2560]{1,0:T(8,128)(2,1)S(1)}, bf16[256,2560]{1,0:T(8,128)(2,1)}, u32[]{:S(2)}, u32[]{:S(2)}) collective-permute-start(bf16[256,2560]{1,0:T(8,128)(2,1)S(1)} %constant_dynamic-update-slice_fusion.24.refs_6_.refs_8_), channel_id=1, source_target_pairs={{0,2},{1,3},{2,0},{3,1},{4,6},{5,7},{6,4},{7,5},{8,10},{9,11},{10,... | collective-permute-start | bytes 3932168 | tf_op jit(solution)/shard_map/ppermute | solution.py:86
  363.1 46.5 %collective-permute-start.45 = (bf16[256,2560]{1,0:T(8,128)(2,1)S(1)}, bf16[256,2560]{1,0:T(8,128)(2,1)}, u32[]{:S(2)}, u32[]{:S(2)}) collective-permute-start(bf16[256,2560]{1,0:T(8,128)(2,1)S(1)} %constant_dynamic-update-slice_fusion.22.refs_4_.refs_6_), channel_id=1, source_target_pairs={{0,4},{1,5},{2,6},{3,7},{4,0},{5,1},{6,2},{7,3},{8,12},{9,13},{10,... | collective-permute-start | bytes 3932168 | tf_op jit(solution)/shard_map/ppermute | solution.py:86
  364.8 52.0 %collective-permute-start.44 = (bf16[256,2560]{1,0:T(8,128)(2,1)S(1)}, bf16[256,2560]{1,0:T(8,128)(2,1)}, u32[]{:S(2)}, u32[]{:S(2)}) collective-permute-start(bf16[256,2560]{1,0:T(8,128)(2,1)S(1)} %constant_dynamic-update-slice_fusion.20.refs_2_.refs_8_), channel_id=1, source_target_pairs={{0,2},{1,3},{2,0},{3,1},{4,6},{5,7},{6,4},{7,5},{8,10},{9,11},{10,... | collective-permute-start | bytes 3932168 | tf_op jit(solution)/shard_map/ppermute | solution.py:86
  366.0 54.0 %collective-permute-start.43 = (bf16[256,2560]{1,0:T(8,128)(2,1)S(1)}, bf16[256,2560]{1,0:T(8,128)(2,1)}, u32[]{:S(2)}, u32[]{:S(2)}) collective-permute-start(bf16[256,2560]{1,0:T(8,128)(2,1)S(1)} %constant_dynamic-update-slice_fusion.18.refs_0_.refs_6_), channel_id=1, source_target_pairs={{0,4},{1,5},{2,6},{3,7},{4,0},{5,1},{6,2},{7,3},{8,12},{9,13},{10,... | collective-permute-start | bytes 3932168 | tf_op jit(solution)/shard_map/ppermute | solution.py:86
  420.0 39.2 %collective-permute-start.47 = (bf16[256,2560]{1,0:T(8,128)(2,1)}, bf16[256,2560]{1,0:T(8,128)(2,1)S(1)}, u32[]{:S(2)}, u32[]{:S(2)}) collective-permute-start(bf16[256,2560]{1,0:T(8,128)(2,1)} %copy-done.72), channel_id=1, source_target_pairs={{0,4},{1,5},{2,6},{3,7},{4,0},{5,1},{6,2},{7,3},{8,12},{9,13},{10,... | collective-permute-start | bytes 3932168 | tf_op jit(solution)/shard_map/ppermute | solution.py:86
  421.5 37.8 %collective-permute-start.48 = (bf16[256,2560]{1,0:T(8,128)(2,1)}, bf16[256,2560]{1,0:T(8,128)(2,1)S(1)}, u32[]{:S(2)}, u32[]{:S(2)}) collective-permute-start(bf16[256,2560]{1,0:T(8,128)(2,1)} %copy-done.71), channel_id=1, source_target_pairs={{0,2},{1,3},{2,0},{3,1},{4,6},{5,7},{6,4},{7,5},{8,10},{9,11},{10,... | collective-permute-start | bytes 3932168 | tf_op jit(solution)/shard_map/ppermute | solution.py:86
  422.5 87.0 %collective-permute-start.49 = (bf16[256,2560]{1,0:T(8,128)(2,1)}, bf16[256,2560]{1,0:T(8,128)(2,1)}, u32[]{:S(2)}, u32[]{:S(2)}) collective-permute-start(bf16[256,2560]{1,0:T(8,128)(2,1)} %get-tuple-element.690), channel_id=1, source_target_pairs={{0,4},{1,5},{2,6},{3,7},{4,0},{5,1},{6,2},{7,3},{8,12},{9,13},{10,... | collective-permute-start | bytes 3932168 | tf_op jit(solution)/shard_map/ppermute | solution.py:86
  422.8 86.7 %collective-permute-start.50 = (bf16[256,2560]{1,0:T(8,128)(2,1)}, bf16[256,2560]{1,0:T(8,128)(2,1)}, u32[]{:S(2)}, u32[]{:S(2)}) collective-permute-start(bf16[256,2560]{1,0:T(8,128)(2,1)} %get-tuple-element.691), channel_id=1, source_target_pairs={{0,2},{1,3},{2,0},{3,1},{4,6},{5,7},{6,4},{7,5},{8,10},{9,11},{10,... | collective-permute-start | bytes 3932168 | tf_op jit(solution)/shard_map/ppermute | solution.py:86
  463.1 46.4 %collective-permute-start.52 = (bf16[128,2560]{1,0:T(8,128)(2,1)}, bf16[128,2560]{1,0:T(8,128)(2,1)S(1)}, u32[]{:S(2)}, u32[]{:S(2)}) collective-permute-start(bf16[128,2560]{1,0:T(8,128)(2,1)} %get-tuple-element.1106), channel_id=1, source_target_pairs={{0,4},{1,5},{2,6},{3,7},{4,0},{5,1},{6,2},{7,3},{8,12},{9,13},{10,... | collective-permute-start | bytes 1966088 | tf_op jit(solution)/shard_map/ppermute | solution.py:86
  465.8 43.7 %collective-permute-start.51 = (bf16[128,2560]{1,0:T(8,128)(2,1)}, bf16[128,2560]{1,0:T(8,128)(2,1)}, u32[]{:S(2)}, u32[]{:S(2)}) collective-permute-start(bf16[128,2560]{1,0:T(8,128)(2,1)} %get-tuple-element.1108), channel_id=1, source_target_pairs={{0,2},{1,3},{2,0},{3,1},{4,6},{5,7},{6,4},{7,5},{8,10},{9,11},{10,... | collective-permute-start | bytes 1966088 | tf_op jit(solution)/shard_map/ppermute | solution.py:86
  514.0 44.1 %collective-permute-start.60 = (bf16[400,2560]{1,0:T(8,128)(2,1)}, bf16[400,2560]{1,0:T(8,128)(2,1)}, u32[]{:S(2)}, u32[]{:S(2)}) collective-permute-start(bf16[400,2560]{1,0:T(8,128)(2,1)} %get-tuple-element.726), channel_id=1, source_target_pairs={{0,1},{1,0},{2,3},{3,2},{4,5},{5,4},{6,7},{7,6},{8,9},{9,8},{10,11... | collective-permute-start | bytes 6144008 | tf_op jit(solution)/shard_map/ppermute | solution.py:86
  514.0 44.9 %collective-permute-start.61 = (bf16[400,2560]{1,0:T(8,128)(2,1)S(1)}, bf16[400,2560]{1,0:T(8,128)(2,1)}, u32[]{:S(2)}, u32[]{:S(2)}) collective-permute-start(bf16[400,2560]{1,0:T(8,128)(2,1)S(1)} %copy-done.64), channel_id=1, source_target_pairs={{0,1},{1,0},{2,3},{3,2},{4,5},{5,4},{6,7},{7,6},{8,9},{9,8},{10,11... | collective-permute-start | bytes 6144008 | tf_op jit(solution)/shard_map/ppermute | solution.py:86
  533.4 40.8 %collective-permute-start.58 = (bf16[400,2560]{1,0:T(8,128)(2,1)}, bf16[400,2560]{1,0:T(8,128)(2,1)}, u32[]{:S(2)}, u32[]{:S(2)}) collective-permute-start(bf16[400,2560]{1,0:T(8,128)(2,1)} %get-tuple-element.722), channel_id=1, source_target_pairs={{0,1},{1,0},{2,3},{3,2},{4,5},{5,4},{6,7},{7,6},{8,9},{9,8},{10,11... | collective-permute-start | bytes 6144008 | tf_op jit(solution)/shard_map/ppermute | solution.py:86
  533.4 40.8 %collective-permute-start.59 = (bf16[400,2560]{1,0:T(8,128)(2,1)}, bf16[400,2560]{1,0:T(8,128)(2,1)}, u32[]{:S(2)}, u32[]{:S(2)}) collective-permute-start(bf16[400,2560]{1,0:T(8,128)(2,1)} %get-tuple-element.723), channel_id=1, source_target_pairs={{0,1},{1,0},{2,3},{3,2},{4,5},{5,4},{6,7},{7,6},{8,9},{9,8},{10,11... | collective-permute-start | bytes 6144008 | tf_op jit(solution)/shard_map/ppermute | solution.py:86
  549.6 68.8 %collective-permute-start.57 = (bf16[400,2560]{1,0:T(8,128)(2,1)}, bf16[400,2560]{1,0:T(8,128)(2,1)}, u32[]{:S(2)}, u32[]{:S(2)}) collective-permute-start(bf16[400,2560]{1,0:T(8,128)(2,1)} %get-tuple-element.720), channel_id=1, source_target_pairs={{0,8},{24,16},{1,9},{25,17},{2,10},{26,18},{3,11},{27,19},{4,12},{... | collective-permute-start | bytes 6144008 | tf_op jit(solution)/shard_map/ppermute | solution.py:432
  558.1 60.4 %collective-permute-start.62 = (bf16[256,2560]{1,0:T(8,128)(2,1)}, bf16[256,2560]{1,0:T(8,128)(2,1)}, u32[]{:S(2)}, u32[]{:S(2)}) collective-permute-start(bf16[256,2560]{1,0:T(8,128)(2,1)} %get-tuple-element.738), channel_id=1, source_target_pairs={{0,4},{1,5},{2,6},{3,7},{4,0},{5,1},{6,2},{7,3},{8,12},{9,13},{10,... | collective-permute-start | bytes 3932168 | tf_op jit(solution)/shard_map/ppermute | solution.py:86
  558.9 59.6 %collective-permute-start.63 = (bf16[256,2560]{1,0:T(8,128)(2,1)}, bf16[256,2560]{1,0:T(8,128)(2,1)}, u32[]{:S(2)}, u32[]{:S(2)}) collective-permute-start(bf16[256,2560]{1,0:T(8,128)(2,1)} %get-tuple-element.739), channel_id=1, source_target_pairs={{0,2},{1,3},{2,0},{3,1},{4,6},{5,7},{6,4},{7,5},{8,10},{9,11},{10,... | collective-permute-start | bytes 3932168 | tf_op jit(solution)/shard_map/ppermute | solution.py:86
  627.7 45.0 %collective-permute-start.64 = (bf16[400,2560]{1,0:T(8,128)(2,1)S(1)}, bf16[400,2560]{1,0:T(8,128)(2,1)}, u32[]{:S(2)}, u32[]{:S(2)}) collective-permute-start(bf16[400,2560]{1,0:T(8,128)(2,1)S(1)} %copy-done.13), channel_id=1, source_target_pairs={{0,8},{24,16},{1,9},{25,17},{2,10},{26,18},{3,11},{27,19},{4,12},{... | collective-permute-start | bytes 6144008 | tf_op jit(solution)/shard_map/ppermute | solution.py:432
  630.3 42.4 %collective-permute-start.65 = (bf16[400,2560]{1,0:T(8,128)(2,1)}, bf16[400,2560]{1,0:T(8,128)(2,1)}, u32[]{:S(2)}, u32[]{:S(2)}) collective-permute-start(bf16[400,2560]{1,0:T(8,128)(2,1)} %add_convert_fusion.11), channel_id=1, source_target_pairs={{8,16},{16,8},{9,17},{17,9},{10,18},{18,10},{11,19},{19,11},{12,20... | collective-permute-start | bytes 6144008 | tf_op jit(solution)/shard_map/ppermute | solution.py:432
  632.2 32.0 %collective-permute-start.66 = (bf16[256,2560]{1,0:T(8,128)(2,1)}, bf16[256,2560]{1,0:T(8,128)(2,1)}, u32[]{:S(2)}, u32[]{:S(2)}) collective-permute-start(bf16[256,2560]{1,0:T(8,128)(2,1)} %get-tuple-element.762), channel_id=1, source_target_pairs={{0,4},{1,5},{2,6},{3,7},{4,0},{5,1},{6,2},{7,3},{8,12},{9,13},{10,... | collective-permute-start | bytes 3932168 | tf_op jit(solution)/shard_map/ppermute | solution.py:86
  633.5 30.8 %collective-permute-start.67 = (bf16[256,2560]{1,0:T(8,128)(2,1)S(1)}, bf16[256,2560]{1,0:T(8,128)(2,1)}, u32[]{:S(2)}, u32[]{:S(2)}) collective-permute-start(bf16[256,2560]{1,0:T(8,128)(2,1)S(1)} %get-tuple-element.763), channel_id=1, source_target_pairs={{0,2},{1,3},{2,0},{3,1},{4,6},{5,7},{6,4},{7,5},{8,10},{9,11},{10,... | collective-permute-start | bytes 3932168 | tf_op jit(solution)/shard_map/ppermute | solution.py:86
  637.4 115.9 %collective-permute-start.73 = (bf16[128,2560]{1,0:T(8,128)(2,1)}, bf16[128,2560]{1,0:T(8,128)(2,1)}, u32[]{:S(2)}, u32[]{:S(2)}) collective-permute-start(bf16[128,2560]{1,0:T(8,128)(2,1)} %get-tuple-element.1094), channel_id=1, source_target_pairs={{0,4},{1,5},{2,6},{3,7},{4,0},{5,1},{6,2},{7,3},{8,12},{9,13},{10,... | collective-permute-start | bytes 1966088 | tf_op jit(solution)/shard_map/ppermute | solution.py:86
  683.1 61.9 %collective-permute-start.71 = (bf16[128,2560]{1,0:T(8,128)(2,1)}, bf16[128,2560]{1,0:T(8,128)(2,1)}, u32[]{:S(2)}, u32[]{:S(2)}) collective-permute-start(bf16[128,2560]{1,0:T(8,128)(2,1)} %get-tuple-element.1098), channel_id=1, source_target_pairs={{0,4},{1,5},{2,6},{3,7},{4,0},{5,1},{6,2},{7,3},{8,12},{9,13},{10,... | collective-permute-start | bytes 1966088 | tf_op jit(solution)/shard_map/ppermute | solution.py:86
  687.3 58.8 %collective-permute-start.70 = (bf16[128,2560]{1,0:T(8,128)(2,1)}, bf16[128,2560]{1,0:T(8,128)(2,1)}, u32[]{:S(2)}, u32[]{:S(2)}) collective-permute-start(bf16[128,2560]{1,0:T(8,128)(2,1)} %get-tuple-element.1100), channel_id=1, source_target_pairs={{0,2},{1,3},{2,0},{3,1},{4,6},{5,7},{6,4},{7,5},{8,10},{9,11},{10,... | collective-permute-start | bytes 1966088 | tf_op jit(solution)/shard_map/ppermute | solution.py:86
  688.3 57.8 %collective-permute-start.68 = (bf16[400,2560]{1,0:T(8,128)(2,1)}, bf16[400,2560]{1,0:T(8,128)(2,1)}, u32[]{:S(2)}, u32[]{:S(2)}) collective-permute-start(bf16[400,2560]{1,0:T(8,128)(2,1)} %broadcast_select_fusion.9), channel_id=1, source_target_pairs={{0,8},{24,16},{8,0},{16,24},{1,9},{25,17},{9,1},{17,25},{2,10},{26... | collective-permute-start | bytes 6144008 | tf_op jit(solution)/shard_map/ppermute | solution.py:432
  691.2 54.9 %collective-permute-start.69 = (bf16[400,2560]{1,0:T(8,128)(2,1)}, bf16[400,2560]{1,0:T(8,128)(2,1)}, u32[]{:S(2)}, u32[]{:S(2)}) collective-permute-start(bf16[400,2560]{1,0:T(8,128)(2,1)} %add_convert_fusion.10), channel_id=1, source_target_pairs={{8,16},{16,8},{9,17},{17,9},{10,18},{18,10},{11,19},{19,11},{12,20... | collective-permute-start | bytes 6144008 | tf_op jit(solution)/shard_map/ppermute | solution.py:432
  763.3 43.8 %collective-permute-start.74 = (bf16[400,2560]{1,0:T(8,128)(2,1)}, bf16[400,2560]{1,0:T(8,128)(2,1)S(1)}, u32[]{:S(2)}, u32[]{:S(2)}) collective-permute-start(bf16[400,2560]{1,0:T(8,128)(2,1)} %broadcast_select_fusion.8), channel_id=1, source_target_pairs={{0,8},{24,16},{8,0},{16,24},{1,9},{25,17},{9,1},{17,25},{2,10},{26... | collective-permute-start | bytes 6144008 | tf_op jit(solution)/shard_map/ppermute | solution.py:432
  764.0 43.1 %collective-permute-start.75 = (bf16[400,2560]{1,0:T(8,128)(2,1)S(1)}, bf16[400,2560]{1,0:T(8,128)(2,1)}, u32[]{:S(2)}, u32[]{:S(2)}) collective-permute-start(bf16[400,2560]{1,0:T(8,128)(2,1)S(1)} %add_convert_fusion.7), channel_id=1, source_target_pairs={{8,16},{16,8},{9,17},{17,9},{10,18},{18,10},{11,19},{19,11},{12,20... | collective-permute-start | bytes 6144008 | tf_op jit(solution)/shard_map/ppermute | solution.py:432
  825.9 76.4 %collective-permute-start.78 = (bf16[4,1,160,2560]{3,2,0,1:T(8,128)(2,1)}, bf16[4,1,160,2560]{3,2,0,1:T(8,128)(2,1)}, u32[]{:S(2)}, u32[]{:S(2)}) collective-permute-start(bf16[4,1,160,2560]{3,2,0,1:T(8,128)(2,1)} %dynamic-slice_bitcast_fusion.1), channel_id=1, source_target_pairs={{0,1},{1,0},{2,3},{3,2},{4,5},{5,4},{6,7},{7,6},{8,9},{9,8},{10,11... | collective-permute-start | bytes 9830408 | tf_op jit(solution)/shard_map/ppermute | solution.py:86
  825.9 76.4 %collective-permute-start.79 = (bf16[4,1,160,2560]{3,2,0,1:T(8,128)(2,1)}, bf16[4,1,160,2560]{3,2,0,1:T(8,128)(2,1)}, u32[]{:S(2)}, u32[]{:S(2)}) collective-permute-start(bf16[4,1,160,2560]{3,2,0,1:T(8,128)(2,1)} %dynamic-slice_bitcast_fusion), channel_id=1, source_target_pairs={{0,1},{1,0},{2,3},{3,2},{4,5},{5,4},{6,7},{7,6},{8,9},{9,8},{10,11... | collective-permute-start | bytes 9830408 | tf_op jit(solution)/shard_map/ppermute | solution.py:86
  826.4 75.9 %collective-permute-start.76 = (bf16[400,2560]{1,0:T(8,128)(2,1)}, bf16[400,2560]{1,0:T(8,128)(2,1)}, u32[]{:S(2)}, u32[]{:S(2)}) collective-permute-start(bf16[400,2560]{1,0:T(8,128)(2,1)} %broadcast_select_fusion.7), channel_id=1, source_target_pairs={{0,8},{24,16},{8,0},{16,24},{1,9},{25,17},{9,1},{17,25},{2,10},{26... | collective-permute-start | bytes 6144008 | tf_op jit(solution)/shard_map/ppermute | solution.py:432
  829.3 73.0 %collective-permute-start.77 = (bf16[400,2560]{1,0:T(8,128)(2,1)}, bf16[400,2560]{1,0:T(8,128)(2,1)}, u32[]{:S(2)}, u32[]{:S(2)}) collective-permute-start(bf16[400,2560]{1,0:T(8,128)(2,1)} %add_convert_fusion.5), channel_id=1, source_target_pairs={{8,16},{16,8},{9,17},{17,9},{10,18},{18,10},{11,19},{19,11},{12,20... | collective-permute-start | bytes 6144008 | tf_op jit(solution)/shard_map/ppermute | solution.py:432
  831.3 132.9 %reduce-scatter.5.cloned.1.call-start = ((), (), s32[]{:S(2)}) async-start(), calls=%async_computation.4 | async-start | bytes 983040 | tf_op jit(solution)/shard_map/reduce_scatter | solution.py:918
  924.5 59.1 %collective-permute-start.80 = (bf16[400,2560]{1,0:T(8,128)(2,1)}, bf16[400,2560]{1,0:T(8,128)(2,1)}, u32[]{:S(2)}, u32[]{:S(2)}) collective-permute-start(bf16[400,2560]{1,0:T(8,128)(2,1)} %broadcast_select_fusion.6), channel_id=1, source_target_pairs={{0,8},{24,16},{8,0},{16,24},{1,9},{25,17},{9,1},{17,25},{2,10},{26... | collective-permute-start | bytes 6144008 | tf_op jit(solution)/shard_map/ppermute | solution.py:432
  925.4 58.2 %collective-permute-start.81 = (bf16[400,2560]{1,0:T(8,128)(2,1)}, bf16[400,2560]{1,0:T(8,128)(2,1)}, u32[]{:S(2)}, u32[]{:S(2)}) collective-permute-start(bf16[400,2560]{1,0:T(8,128)(2,1)} %add_convert_fusion.4), channel_id=1, source_target_pairs={{8,16},{16,8},{9,17},{17,9},{10,18},{18,10},{11,19},{19,11},{12,20... | collective-permute-start | bytes 6144008 | tf_op jit(solution)/shard_map/ppermute | solution.py:432
  927.5 37.5 %collective-permute-start.82 = (bf16[1,2,160,2560]{3,2,1,0:T(8,128)(2,1)}, bf16[1,2,160,2560]{3,2,1,0:T(8,128)(2,1)}, u32[]{:S(2)}, u32[]{:S(2)}) collective-permute-start(bf16[1,2,160,2560]{3,2,1,0:T(8,128)(2,1)} %dynamic-slice_bitcast_fusion.5), channel_id=1, source_target_pairs={{0,4},{1,5},{2,6},{3,7},{4,0},{5,1},{6,2},{7,3},{8,12},{9,13},{10,... | collective-permute-start | bytes 4915208 | tf_op jit(solution)/shard_map/ppermute | solution.py:86
  928.5 37.0 %collective-permute-start.83 = (bf16[2,1,160,2560]{3,2,0,1:T(8,128)(2,1)}, bf16[2,1,160,2560]{3,2,0,1:T(8,128)(2,1)}, u32[]{:S(2)}, u32[]{:S(2)}) collective-permute-start(bf16[2,1,160,2560]{3,2,0,1:T(8,128)(2,1)} %dynamic-slice_bitcast_fusion.4), channel_id=1, source_target_pairs={{0,2},{1,3},{2,0},{3,1},{4,6},{5,7},{6,4},{7,5},{8,10},{9,11},{10,... | collective-permute-start | bytes 4915208 | tf_op jit(solution)/shard_map/ppermute | solution.py:86
  1007.4 50.5 %collective-permute-start.88 = (bf16[4,1,96,3840]{3,2,0,1:T(8,128)(2,1)}, bf16[4,1,96,3840]{3,2,0,1:T(8,128)(2,1)}, u32[]{:S(2)}, u32[]{:S(2)}) collective-permute-start(bf16[4,1,96,3840]{3,2,0,1:T(8,128)(2,1)} %dynamic-slice_bitcast_fusion.2), channel_id=1, source_target_pairs={{0,1},{1,0},{2,3},{3,2},{4,5},{5,4},{6,7},{7,6},{8,9},{9,8},{10,11... | collective-permute-start | bytes 8847368 | tf_op jit(solution)/shard_map/ppermute | solution.py:86
  1007.4 50.5 %collective-permute-start.84 = (bf16[400,2560]{1,0:T(8,128)(2,1)}, bf16[400,2560]{1,0:T(8,128)(2,1)}, u32[]{:S(2)}, u32[]{:S(2)}) collective-permute-start(bf16[400,2560]{1,0:T(8,128)(2,1)} %add_convert_fusion.2), channel_id=1, source_target_pairs={{8,0},{16,24},{9,1},{17,25},{10,2},{18,26},{11,3},{19,27},{12,4},{... | collective-permute-start | bytes 6144008 | tf_op jit(solution)/shard_map/ppermute | solution.py:432
  1008.7 49.2 %collective-permute-start.85 = (bf16[400,2560]{1,0:T(8,128)(2,1)}, bf16[400,2560]{1,0:T(8,128)(2,1)}, u32[]{:S(2)}, u32[]{:S(2)}) collective-permute-start(bf16[400,2560]{1,0:T(8,128)(2,1)} %add_convert_fusion.1), channel_id=1, source_target_pairs={{8,16},{16,8},{9,17},{17,9},{10,18},{18,10},{11,19},{19,11},{12,20... | collective-permute-start | bytes 6144008 | tf_op jit(solution)/shard_map/ppermute | solution.py:432
  1077.2 50.1 %collective-permute-start.92 = (bf16[400,2560]{1,0:T(8,128)(2,1)S(1)}, bf16[400,2560]{1,0:T(8,128)(2,1)S(1)}, u32[]{:S(2)}, u32[]{:S(2)}) collective-permute-start(bf16[400,2560]{1,0:T(8,128)(2,1)S(1)} %add_convert_fusion), channel_id=1, source_target_pairs={{8,0},{16,24},{9,1},{17,25},{10,2},{18,26},{11,3},{19,27},{12,4},{... | collective-permute-start | bytes 6144008 | tf_op jit(solution)/shard_map/ppermute | solution.py:432
  1078.5 41.3 %collective-permute-start.91 = (bf16[320,2560]{1,0:T(8,128)(2,1)S(1)}, bf16[320,2560]{1,0:T(8,128)(2,1)S(1)}, u32[]{:S(2)}, u32[]{:S(2)}) collective-permute-start(bf16[320,2560]{1,0:T(8,128)(2,1)S(1)} %pad_maximum_fusion.7), channel_id=1, source_target_pairs={{0,8},{24,16},{1,9},{25,17},{2,10},{26,18},{3,11},{27,19},{4,12},{... | collective-permute-start | bytes 4915208 | tf_op jit(solution)/shard_map/ppermute | solution.py:432
  1085.2 34.0 %collective-permute-start.93 = (bf16[2,1,96,3840]{3,2,0,1:T(8,128)(2,1)}, bf16[2,1,96,3840]{3,2,0,1:T(8,128)(2,1)}, u32[]{:S(2)}, u32[]{:S(2)}) collective-permute-start(bf16[2,1,96,3840]{3,2,0,1:T(8,128)(2,1)} %dynamic-slice_bitcast_fusion.6), channel_id=1, source_target_pairs={{0,2},{1,3},{2,0},{3,1},{4,6},{5,7},{6,4},{7,5},{8,10},{9,11},{10,... | collective-permute-start | bytes 4423688 | tf_op jit(solution)/shard_map/ppermute | solution.py:86
  1132.7 37.5 %collective-permute-start.97 = (bf16[320,2560]{1,0:T(8,128)(2,1)S(1)}, bf16[320,2560]{1,0:T(8,128)(2,1)S(1)}, u32[]{:S(2)}, u32[]{:S(2)}) collective-permute-start(bf16[320,2560]{1,0:T(8,128)(2,1)S(1)} %add_convert_fusion.13), channel_id=1, source_target_pairs={{8,16},{16,8},{9,17},{17,9},{10,18},{18,10},{11,19},{19,11},{12,20... | collective-permute-start | bytes 4915208 | tf_op jit(solution)/shard_map/ppermute | solution.py:432
  1139.6 30.5 %collective-permute-start.98 = (bf16[1,1,96,3840]{3,2,0,1:T(8,128)(2,1)S(1)}, bf16[1,1,96,3840]{3,2,0,1:T(8,128)(2,1)S(1)}, u32[]{:S(2)}, u32[]{:S(2)}) collective-permute-start(bf16[1,1,96,3840]{3,2,0,1:T(8,128)(2,1)S(1)} %constant_dynamic-slice_fusion.3), channel_id=1, source_target_pairs={{0,4},{1,5},{2,6},{3,7},{4,0},{5,1},{6,2},{7,3},{8,12},{9,13},{10,... | collective-permute-start | bytes 2211848 | tf_op jit(solution)/shard_map/ppermute | solution.py:86
  1170.9 37.5 %collective-permute-start.103 = (bf16[320,2560]{1,0:T(8,128)(2,1)S(1)}, bf16[320,2560]{1,0:T(8,128)(2,1)S(1)}, u32[]{:S(2)}, u32[]{:S(2)}) collective-permute-start(bf16[320,2560]{1,0:T(8,128)(2,1)S(1)} %add_convert_fusion.12), channel_id=1, source_target_pairs={{8,0},{16,24},{9,1},{17,25},{10,2},{18,26},{11,3},{19,27},{12,4},{... | collective-permute-start | bytes 4915208 | tf_op jit(solution)/shard_map/ppermute | solution.py:432
  (272 other events, 2829.9 us)
Sparse Core Ops, SparseCore 0:
  109.6 33.3 all-gather.1
  831.4 33.3 reduce-scatter.2
  929.5 34.5 reduce-scatter.4

commit v3 on v2

--- a/solution.py
+++ b/solution.py
@@ -997,7 +997,8 @@
     begun.append(grads_begin(1, scatter_end(*grad_ways[1])))
     outputs.append(low(of_batch(resid, 1) + branch_scale * scatter_end(*out_ways[1])))
     out_sum = low(matmul_left(mixed_flat, jnp.concatenate([begun[0][1], begun[1][1]])))
-    got, begun, out_sum, outputs = hold((got, begun, out_sum, outputs))
+    query_ends = [query_end(0, attended[0][0])]
+    got, begun, out_sum, outputs, query_ends = hold((got, begun, out_sum, outputs, query_ends))
     line.absorb(got)
     in_shards = lambda values: values.reshape(devices, -1, values.shape[-1])
     back_way = [1] + bits[::-1]
@@ -1030,7 +1031,7 @@
         jnp.concatenate([attended[0][1] + attended[1][1], attended[0][2] + attended[1][2]], axis=1)
     )
     query_sum = low(matmul_left(query_low, jnp.concatenate([attended[0][0], attended[1][0]])))
-    query_ends = [query_end(batch, attended[batch][0]) for batch in range(batches)]
+    query_ends.append(query_end(1, attended[1][0]))
     down_sum = low(matmul_left(first_low, jnp.concatenate([query_ends[0][0], query_ends[1][0]])))
     got, out_got, latent_up_sum, query_sum, down_sum, query_ends = hold(
         (got, out_got, latent_up_sum, query_sum, down_sum, query_ends)

time: 1300 us -> 1320 us (1.015)
  waiting for transfers between devices: 295 us -> 311 us
    ppermute x29, waiting for transfers between devices: 110 us -> 125 us  [move(): lax.ppermute(value, 'ctx', pairs)]
    unnamed x453 -> x467, local copies, waits for them, and re-layouts: 61.4 us -> 62.4 us
    convert_element_type x47 -> x48, other arithmetic: 84.5 us -> 84 us  [low(): return values.astype(jnp.bfloat16)]
  transfers between devices with their start and end apart: 119 -> 119, of which waited for: 36 -> 36; matrix products, arithmetic and copies ran while one was open for 21% -> 19% of each run, Pallas kernels for 30% -> 30%
where the time goes in v3:
time: 1320 us; the launch traced here: 1310 us
  Pallas kernels  391 us (30%)
  waiting for transfers between devices  311 us (24%)
  other arithmetic  207 us (16%)
  local copies, waits for them, and re-layouts  169 us (13%)
  starting transfers between devices  139 us (11%)
  matrix products  73.4 us (6%)
  between operations  17.3 us (1%)
    ppermute x87, waiting for transfers between devices, flip(): return lax.ppermute(values, 'fsdp', [(i, i ^ bit) for i in range(count)])  164 us
    ppermute x29, waiting for transfers between devices, move(): lax.ppermute(value, 'ctx', pairs)  125 us
    pallas_call x2, Pallas kernels, attend_backward(): pl.pallas_call(backward_kernel, grid=(quads,), in_specs=[pl.BlockSpec((ro...  93.4 us
    convert_element_type x48, other arithmetic, low(): return values.astype(jnp.bfloat16)  84 us
    pallas_call x4, Pallas kernels, feed_down(): pl.pallas_call(functools.partial(down_kernel, len(units), slots), grid=(w...  82 us
    pallas_call x6, Pallas kernels, weight_sums(): pl.pallas_call(functools.partial(weight_kernel, len(lefts), tuple((len(pi...  77 us
    ppermute x29, starting transfers between devices, move(): lax.ppermute(value, 'ctx', pairs)  69.6 us
    ppermute x87, starting transfers between devices, flip(): return lax.ppermute(values, 'fsdp', [(i, i ^ bit) for i in range(count)])  68.2 us
  transfers between devices with their start and end apart: 119, of which 36 were waited for; matrix products, arithmetic and copies ran while one was open for 19% of the time, Pallas kernels for 30%

profile of v3, /device:TPU:0, one launch (start us, length us, event | category | flops | bytes accessed | tf_op | source)
XLA Modules:
  0.0 1307.2 jit_solution(17836555852570716624)
XLA Ops:
  39.9 7.5 collective-permute-done.3.refs_5_
  76.6 27.5 %collective-permute-done.12.refs_5_ = bf16[64,5120]{1,0:T(8,128)(2,1)} collective-permute-done((bf16[64,5120]{1,0:T(8,128)(2,1)}, bf16[64,5120]{1,0:T(8,128)(2,1)}, u32[]{:S(2)}, u32[]{:S(2)}) %collective-permute-start.12) | collective-permute-done | bytes 655392 | tf_op jit(solution)/shard_map/ppermute | solution.py:86
  123.2 7.5 place_shards.4
  138.1 4.8 all-gather.2.cloned.1.call-done
  165.9 51.9 %attend_forward.1 = (bf16[2,256,3840]{2,1,0:T(8,128)(2,1)}, bf16[2,256,2560]{2,1,0:T(8,128)(2,1)}, f32[2,10,4,256]{3,2,1,0:T(4,128)S(1)}) custom-call(bf16[2,256,768]{2,1,0:T(8,128)(2,1)S(1)} %bitcast.252, bf16[2,1024,256]{2,1,0:T(8,128)(2,1)S(1)} %copy.209.latent_ref, bf16[2,1024,128]{2,1,0:T(8,128)(2,1)S(1)} %copy-done.26, ...), custom_call_target="tpu_custom_call" | custom-call | flops 29863444480 | bytes 41943040 | tf_op jit(solution)/shard_map/attend_forward/pallas_call | solution.py:233
  233.7 4.5 slice_bitcast_fusion
  243.6 9.1 place_shards.5
  252.7 10.9 multiply_reduce_fusion
  265.9 6.2 collective-permute-done.32.refs_7_.refs_5_
  276.6 7.3 pad_maximum_fusion.gate_w.refs_2_
  283.9 6.7 collective-permute-done.35
  296.4 7.3 pad_maximum_fusion.2.down_w.refs_1_
  303.7 7.3 pad_maximum_fusion.1.up_w.refs_3_
  311.0 10.7 collective-permute-done.38.refs_3_.refs_5_
  327.7 34.0 %feed_up.2 = (bf16[1600,1024]{1,0:T(8,128)(2,1)}, bf16[1600,1024]{1,0:T(8,128)(2,1)}, bf16[1600,1024]{1,0:T(8,128)(2,1)}) custom-call(bf16[1600,2560]{1,0:T(8,128)(2,1)} %pad_maximum_fusion.gate_w.refs_2_, bf16[1600,2560]{1,0:T(8,128)(2,1)} %pad_maximum_fusion.1.up_w.refs_3_, bf16[1600,2560]{1,0:T(8,128)(2,1)} %pad_maximum_fusion.2.down_w.refs_1_, ...), custom_call_target="tpu_custom_call" | custom-call | flops 25165824000 | bytes 44892160 | tf_op jit(solution)/shard_map/feed_up/pallas_call | solution.py:476
  366.5 14.0 %feed_down.5 = (bf16[256,2560]{1,0:T(8,128)(2,1)S(1)}, bf16[256,2560]{1,0:T(8,128)(2,1)S(1)}, bf16[256,2560]{1,0:T(8,128)(2,1)S(1)}, bf16[256,2560]{1,0:T(8,128)(2,1)S(1)}) custom-call(bf16[1600,1024]{1,0:T(8,128)(2,1)} %get-tuple-element.662.refs_0_, bf16[1600,2560]{1,0:T(8,128)(2,1)} %pad_maximum_fusion.2.down_w.refs_1_), custom_call_target="tpu_custom_call" | custom-call | flops 8388608000 | bytes 16711680 | tf_op jit(solution)/shard_map/feed_down/pallas_call | solution.py:517
  382.7 26.8 %feed_down.4 = (bf16[256,2560]{1,0:T(8,128)(2,1)S(1)}, bf16[256,2560]{1,0:T(8,128)(2,1)}, bf16[256,2560]{1,0:T(8,128)(2,1)S(1)}, bf16[256,2560]{1,0:T(8,128)(2,1)}) custom-call(bf16[1600,1024]{1,0:T(8,128)(2,1)} %get-tuple-element.674.refs_0_, bf16[1600,1024]{1,0:T(8,128)(2,1)} %get-tuple-element.686.refs_1_.refs_0_, ...), custom_call_target="tpu_custom_call" | custom-call | flops 16777216000 | bytes 28180480 | tf_op jit(solution)/shard_map/feed_down/pallas_call | solution.py:517
  409.5 7.1 collective-permute-done.44.refs_3_.refs_9_
  425.3 33.9 %feed_up.3 = (bf16[1600,1024]{1,0:T(8,128)(2,1)}, bf16[1600,1024]{1,0:T(8,128)(2,1)}, bf16[1600,1024]{1,0:T(8,128)(2,1)}) custom-call(bf16[1600,2560]{1,0:T(8,128)(2,1)} %pad_maximum_fusion.gate_w.refs_2_, bf16[1600,2560]{1,0:T(8,128)(2,1)} %pad_maximum_fusion.1.up_w.refs_3_, bf16[1600,2560]{1,0:T(8,128)(2,1)} %pad_maximum_fusion.2.down_w.refs_1_, ...), custom_call_target="tpu_custom_call" | custom-call | flops 25165824000 | bytes 44892160 | tf_op jit(solution)/shard_map/feed_up/pallas_call | solution.py:476
  466.9 12.7 weight_sums.8
  480.9 13.0 weight_sums.7
  496.6 13.0 weight_sums.6
  514.5 14.7 %feed_down.6 = (bf16[256,2560]{1,0:T(8,128)(2,1)S(1)}, bf16[256,2560]{1,0:T(8,128)(2,1)}, bf16[256,2560]{1,0:T(8,128)(2,1)S(1)}, bf16[256,2560]{1,0:T(8,128)(2,1)}) custom-call(bf16[1600,1024]{1,0:T(8,128)(2,1)} %get-tuple-element.700.refs_1_.refs_0_, bf16[1600,2560]{1,0:T(8,128)(2,1)} %pad_maximum_fusion.2.down_w.refs_1_), custom_call_target="tpu_custom_call" | custom-call | flops 8388608000 | bytes 16711680 | tf_op jit(solution)/shard_map/feed_down/pallas_call | solution.py:517
  536.5 13.1 weight_sums.9
  549.6 6.2 collective-permute-start.57
  560.1 12.8 weight_sums.11
  576.9 12.5 weight_sums.10
  592.1 26.4 %feed_down.7 = (bf16[256,2560]{1,0:T(8,128)(2,1)S(1)}, bf16[256,2560]{1,0:T(8,128)(2,1)}, bf16[256,2560]{1,0:T(8,128)(2,1)S(1)}, bf16[256,2560]{1,0:T(8,128)(2,1)S(1)}) custom-call(bf16[1600,1024]{1,0:T(8,128)(2,1)} %get-tuple-element.732.refs_1_.refs_0_, bf16[1600,1024]{1,0:T(8,128)(2,1)} %get-tuple-element.733.refs_1_, ...), custom_call_target="tpu_custom_call" | custom-call | flops 16777216000 | bytes 28180480 | tf_op jit(solution)/shard_map/feed_down/pallas_call | solution.py:517
  618.6 4.5 add_convert_fusion.11
  644.9 8.7 convolution_convert_fusion.4.grad_ref
  653.6 10.8 collective-permute-done.66
  664.4 8.4 collective-permute-done.64
  693.3 46.7 %attend_backward.2 = (bf16[256,3840]{1,0:T(8,128)(2,1)}, f32[256,2560]{1,0:T(8,128)}, f32[256,2560]{1,0:T(8,128)}, f32[1024,256]{1,0:T(8,128)S(1)}, f32[1024,128]{1,0:T(8,128)S(1)}) custom-call(bf16[256,3840]{1,0:T(8,128)(2,1)} %get-tuple-element.1079.query_ref, bf16[256,2560]{1,0:T(8,128)(2,1)S(1)} %convolution_convert_fusion.4.grad_ref, ...), custom_call_target="tpu_custom_call" | custom-call | flops 34896609280 | bytes 26214400 | tf_op jit(solution)/shard_map/attend_backward/pallas_call | solution.py:338
  746.2 5.0 broadcast_select_fusion.8
  753.5 6.4 collective-permute-done.72
  759.9 5.5 multiply_reduce_fusion.8
  774.4 9.8 convolution_convert_fusion.3.grad_ref
  786.8 5.1 broadcast_select_fusion.1
  791.9 10.0 convolution_convert_fusion
  801.9 26.0 %collective-permute-done.74 = bf16[400,2560]{1,0:T(8,128)(2,1)S(1)} collective-permute-done((bf16[400,2560]{1,0:T(8,128)(2,1)}, bf16[400,2560]{1,0:T(8,128)(2,1)S(1)}, u32[]{:S(2)}, u32[]{:S(2)}) %collective-permute-start.74) | collective-permute-done | bytes 2048032 | tf_op jit(solution)/shard_map/ppermute | solution.py:432
  828.0 7.1 fusion.93
  856.2 46.6 %attend_backward.3 = (bf16[256,3840]{1,0:T(8,128)(2,1)}, f32[256,2560]{1,0:T(8,128)}, f32[256,2560]{1,0:T(8,128)}, f32[1024,256]{1,0:T(8,128)S(1)}, f32[1024,128]{1,0:T(8,128)S(1)}) custom-call(bf16[256,3840]{1,0:T(8,128)(2,1)} %get-tuple-element.1078.query_ref, bf16[256,2560]{1,0:T(8,128)(2,1)S(1)} %copy-done.73, bf16[1024,256]{1,0:T(8,128)(2,1)S(1)} %copy-done.24, ...), custom_call_target="tpu_custom_call" | custom-call | flops 34896609280 | bytes 26214400 | tf_op jit(solution)/shard_map/attend_backward/pallas_call | solution.py:338
  925.8 5.0 fusion.1
  930.8 4.6 add_convert_fusion.4
  938.0 4.8 broadcast_select_fusion.6
  962.5 5.1 convolution_convert_fusion.1
  967.6 17.4 %reduce-scatter.5.cloned.1.call-done = bf16[256,288]{1,0:T(8,128)(2,1)} async-done(((bf16[1024,288]{1,0:T(8,128)(2,1)}), bf16[256,288]{1,0:T(8,128)(2,1)}) %reduce-scatter.5.cloned.1.call-update) | async-done | bytes 147472 | tf_op jit(solution)/shard_map/reduce_scatter | solution.py:918
  986.5 18.2 %collective-permute-done.80 = bf16[400,2560]{1,0:T(8,128)(2,1)} collective-permute-done((bf16[400,2560]{1,0:T(8,128)(2,1)}, bf16[400,2560]{1,0:T(8,128)(2,1)}, u32[]{:S(2)}, u32[]{:S(2)}) %collective-permute-start.80) | collective-permute-done | bytes 2048032 | tf_op jit(solution)/shard_map/ppermute | solution.py:432
  1037.1 15.6 %collective-permute-done.86 = bf16[1,1,160,2560]{3,2,1,0:T(8,128)(2,1)S(1)} collective-permute-done((bf16[1,1,160,2560]{3,2,1,0:T(8,128)(2,1)S(1)}, bf16[1,1,160,2560]{3,2,1,0:T(8,128)(2,1)S(1)}, u32[]{:S(2)}, u32[]{:S(2)}) %collective-permute-start.86) | collective-permute-done | bytes 819232 | tf_op jit(solution)/shard_map/ppermute | solution.py:86
  1062.6 16.3 %collective-permute-done.84 = bf16[400,2560]{1,0:T(8,128)(2,1)} collective-permute-done((bf16[400,2560]{1,0:T(8,128)(2,1)}, bf16[400,2560]{1,0:T(8,128)(2,1)}, u32[]{:S(2)}, u32[]{:S(2)}) %collective-permute-start.84) | collective-permute-done | bytes 2048032 | tf_op jit(solution)/shard_map/ppermute | solution.py:432
  1099.6 5.3 collective-permute-start.91
  1107.1 5.0 collective-permute-done.94
  1118.3 13.9 %collective-permute-done.95 = bf16[1,2,320,768]{3,2,1,0:T(8,128)(2,1)} collective-permute-done((bf16[1,2,320,768]{3,2,1,0:T(8,128)(2,1)}, bf16[1,2,320,768]{3,2,1,0:T(8,128)(2,1)}, u32[]{:S(2)}, u32[]{:S(2)}) %collective-permute-start.95) | collective-permute-done | bytes 983072 | tf_op jit(solution)/shard_map/ppermute | solution.py:86
  1132.2 6.8 collective-permute-done.93
  1139.9 7.1 collective-permute-done.92
  1165.1 24.6 %collective-permute-done.99 = bf16[1,1,32,5120]{3,2,1,0:T(8,128)(2,1)S(1)} collective-permute-done((bf16[1,1,32,5120]{3,2,1,0:T(8,128)(2,1)S(1)}, bf16[1,1,32,5120]{3,2,1,0:T(8,128)(2,1)S(1)}, u32[]{:S(2)}, u32[]{:S(2)}) %collective-permute-start.99) | collective-permute-done | bytes 327712 | tf_op jit(solution)/shard_map/ppermute | solution.py:86
  1192.0 4.7 collective-permute-start.102
  1198.2 4.7 collective-permute-done.104
  1202.9 7.1 collective-permute-done.102
  1210.0 17.8 %collective-permute-done.103 = bf16[320,2560]{1,0:T(8,128)(2,1)S(1)} collective-permute-done((bf16[320,2560]{1,0:T(8,128)(2,1)S(1)}, bf16[320,2560]{1,0:T(8,128)(2,1)S(1)}, u32[]{:S(2)}, u32[]{:S(2)}) %collective-permute-start.103) | collective-permute-done | bytes 1638432 | tf_op jit(solution)/shard_map/ppermute | solution.py:432
  1238.3 9.9 collective-permute-start.107
  1263.2 6.0 collective-permute-start.110
  1279.5 9.4 collective-permute-done.113
  1291.2 5.8 collective-permute-done.115
  (953 shorter events, 464.9 us)
Async XLA Ops:
  7.2 135.7 %all-gather.2.cloned.1.call-start = ((), (), s32[]{:S(2)}) async-start(), calls=%async_computation.2 | async-start | bytes 1474560 | tf_op jit(solution)/shard_map/all_gather | solution.py:754
  60.2 43.9 %collective-permute-start.13 = (bf16[192,3840]{1,0:T(8,128)(2,1)}, bf16[192,3840]{1,0:T(8,128)(2,1)}, u32[]{:S(2)}, u32[]{:S(2)}) collective-permute-start(bf16[192,3840]{1,0:T(8,128)(2,1)} %pad_maximum_fusion.8.refs_8_), channel_id=1, source_target_pairs={{0,2},{1,3},{2,0},{3,1},{4,6},{5,7},{6,4},{7,5},{8,10},{9,11},{10,... | collective-permute-start | bytes 4423688 | tf_op jit(solution)/shard_map/ppermute | solution.py:86
  66.6 37.5 %collective-permute-start.11 = (bf16[640,768]{1,0:T(8,128)(2,1)S(1)}, bf16[640,768]{1,0:T(8,128)(2,1)}, u32[]{:S(2)}, u32[]{:S(2)}) collective-permute-start(bf16[640,768]{1,0:T(8,128)(2,1)S(1)} %pad_maximum_fusion.10.refs_0_), channel_id=1, source_target_pairs={{0,4},{1,5},{2,6},{3,7},{4,0},{5,1},{6,2},{7,3},{8,12},{9,13},{10,... | collective-permute-start | bytes 2949128 | tf_op jit(solution)/shard_map/ppermute | solution.py:86
  69.5 34.6 %collective-permute-start.12 = (bf16[64,5120]{1,0:T(8,128)(2,1)}, bf16[64,5120]{1,0:T(8,128)(2,1)}, u32[]{:S(2)}, u32[]{:S(2)}) collective-permute-start(bf16[64,5120]{1,0:T(8,128)(2,1)} %pad_maximum_fusion.13.refs_4_), channel_id=1, source_target_pairs={{0,4},{1,5},{2,6},{3,7},{4,0},{5,1},{6,2},{7,3},{8,12},{9,13},{10,... | collective-permute-start | bytes 1966088 | tf_op jit(solution)/shard_map/ppermute | solution.py:86
  109.4 811.6 %reduce-scatter.3.cloned.1.call-start = ((), (), s32[]{:S(2)}) async-start(), calls=%async_computation.3 | async-start | bytes 983040 | tf_op jit(solution)/shard_map/reduce_scatter | solution.py:918
  156.4 62.0 %collective-permute-start.23 = (bf16[320,2560]{1,0:T(8,128)(2,1)}, bf16[320,2560]{1,0:T(8,128)(2,1)}, u32[]{:S(2)}, u32[]{:S(2)}) collective-permute-start(bf16[320,2560]{1,0:T(8,128)(2,1)} %constant_dynamic-update-slice_fusion.8.refs_4_), channel_id=1, source_target_pairs={{0,2},{1,3},{2,0},{3,1},{4,6},{5,7},{6,4},{7,5},{8,10},{9,11},{10,... | collective-permute-start | bytes 4915208 | tf_op jit(solution)/shard_map/ppermute | solution.py:86
  157.4 61.1 %collective-permute-start.26 = (bf16[800,2560]{1,0:T(8,128)(2,1)}, bf16[800,2560]{1,0:T(8,128)(2,1)S(1)}, u32[]{:S(2)}, u32[]{:S(2)}) collective-permute-start(bf16[800,2560]{1,0:T(8,128)(2,1)} %param.29), channel_id=1, source_target_pairs={{0,1},{1,0},{2,3},{3,2},{4,5},{5,4},{6,7},{7,6},{8,9},{9,8},{10,11... | collective-permute-start | bytes 12288008 | tf_op jit(solution)/shard_map/ppermute | solution.py:86
  161.6 56.9 %collective-permute-start.22 = (bf16[320,2560]{1,0:T(8,128)(2,1)}, bf16[320,2560]{1,0:T(8,128)(2,1)}, u32[]{:S(2)}, u32[]{:S(2)}) collective-permute-start(bf16[320,2560]{1,0:T(8,128)(2,1)} %constant_dynamic-update-slice_fusion.6.refs_0_), channel_id=1, source_target_pairs={{0,4},{1,5},{2,6},{3,7},{4,0},{5,1},{6,2},{7,3},{8,12},{9,13},{10,... | collective-permute-start | bytes 4915208 | tf_op jit(solution)/shard_map/ppermute | solution.py:86
  164.3 54.1 %collective-permute-start.24 = (bf16[128,2560]{1,0:T(8,128)(2,1)S(1)}, bf16[128,2560]{1,0:T(8,128)(2,1)S(1)}, u32[]{:S(2)}, u32[]{:S(2)}) collective-permute-start(bf16[128,2560]{1,0:T(8,128)(2,1)S(1)} %get-tuple-element.580), channel_id=1, source_target_pairs={{0,2},{1,3},{2,0},{3,1},{4,6},{5,7},{6,4},{7,5},{8,10},{9,11},{10,... | collective-permute-start | bytes 1966088 | tf_op jit(solution)/shard_map/ppermute | solution.py:86
  164.9 53.6 %collective-permute-start.25 = (bf16[128,2560]{1,0:T(8,128)(2,1)S(1)}, bf16[128,2560]{1,0:T(8,128)(2,1)S(1)}, u32[]{:S(2)}, u32[]{:S(2)}) collective-permute-start(bf16[128,2560]{1,0:T(8,128)(2,1)S(1)} %get-tuple-element.582), channel_id=1, source_target_pairs={{0,4},{1,5},{2,6},{3,7},{4,0},{5,1},{6,2},{7,3},{8,12},{9,13},{10,... | collective-permute-start | bytes 1966088 | tf_op jit(solution)/shard_map/ppermute | solution.py:86
  238.3 34.7 %collective-permute-start.33 = (bf16[800,2560]{1,0:T(8,128)(2,1)S(1)}, bf16[800,2560]{1,0:T(8,128)(2,1)}, u32[]{:S(2)}, u32[]{:S(2)}) collective-permute-start(bf16[800,2560]{1,0:T(8,128)(2,1)S(1)} %copy-done.115), channel_id=1, source_target_pairs={{0,1},{1,0},{2,3},{3,2},{4,5},{5,4},{6,7},{7,6},{8,9},{9,8},{10,11... | collective-permute-start | bytes 12288008 | tf_op jit(solution)/shard_map/ppermute | solution.py:86
  239.7 33.3 %collective-permute-start.34 = (bf16[800,2560]{1,0:T(8,128)(2,1)S(1)}, bf16[800,2560]{1,0:T(8,128)(2,1)}, u32[]{:S(2)}, u32[]{:S(2)}) collective-permute-start(bf16[800,2560]{1,0:T(8,128)(2,1)S(1)} %copy-done.114), channel_id=1, source_target_pairs={{0,1},{1,0},{2,3},{3,2},{4,5},{5,4},{6,7},{7,6},{8,9},{9,8},{10,11... | collective-permute-start | bytes 12288008 | tf_op jit(solution)/shard_map/ppermute | solution.py:86
  240.9 31.3 %collective-permute-start.32 = (bf16[256,2560]{1,0:T(8,128)(2,1)S(1)}, bf16[256,2560]{1,0:T(8,128)(2,1)S(1)}, u32[]{:S(2)}, u32[]{:S(2)}) collective-permute-start(bf16[256,2560]{1,0:T(8,128)(2,1)S(1)} %constant_dynamic-update-slice_fusion.12.refs_6_.refs_4_), channel_id=1, source_target_pairs={{0,2},{1,3},{2,0},{3,1},{4,6},{5,7},{6,4},{7,5},{8,10},{9,11},{10,... | collective-permute-start | bytes 3932168 | tf_op jit(solution)/shard_map/ppermute | solution.py:86
  242.0 31.0 %collective-permute-start.31 = (bf16[256,2560]{1,0:T(8,128)(2,1)S(1)}, bf16[256,2560]{1,0:T(8,128)(2,1)S(1)}, u32[]{:S(2)}, u32[]{:S(2)}) collective-permute-start(bf16[256,2560]{1,0:T(8,128)(2,1)S(1)} %constant_dynamic-update-slice_fusion.10.refs_4_.refs_2_), channel_id=1, source_target_pairs={{0,4},{1,5},{2,6},{3,7},{4,0},{5,1},{6,2},{7,3},{8,12},{9,13},{10,... | collective-permute-start | bytes 3932168 | tf_op jit(solution)/shard_map/ppermute | solution.py:86
  323.7 38.0 %collective-permute-start.39 = (bf16[128,2560]{1,0:T(8,128)(2,1)}, bf16[128,2560]{1,0:T(8,128)(2,1)S(1)}, u32[]{:S(2)}, u32[]{:S(2)}) collective-permute-start(bf16[128,2560]{1,0:T(8,128)(2,1)} %get-tuple-element.636), channel_id=1, source_target_pairs={{0,2},{1,3},{2,0},{3,1},{4,6},{5,7},{6,4},{7,5},{8,10},{9,11},{10,... | collective-permute-start | bytes 1966088 | tf_op jit(solution)/shard_map/ppermute | solution.py:86
  324.7 36.9 %collective-permute-start.40 = (bf16[128,2560]{1,0:T(8,128)(2,1)}, bf16[128,2560]{1,0:T(8,128)(2,1)S(1)}, u32[]{:S(2)}, u32[]{:S(2)}) collective-permute-start(bf16[128,2560]{1,0:T(8,128)(2,1)} %get-tuple-element.638), channel_id=1, source_target_pairs={{0,4},{1,5},{2,6},{3,7},{4,0},{5,1},{6,2},{7,3},{8,12},{9,13},{10,... | collective-permute-start | bytes 1966088 | tf_op jit(solution)/shard_map/ppermute | solution.py:86
  326.2 35.5 %collective-permute-start.41 = (bf16[128,2560]{1,0:T(8,128)(2,1)S(1)}, bf16[128,2560]{1,0:T(8,128)(2,1)S(1)}, u32[]{:S(2)}, u32[]{:S(2)}) collective-permute-start(bf16[128,2560]{1,0:T(8,128)(2,1)S(1)} %copy-done.128), channel_id=1, source_target_pairs={{0,2},{1,3},{2,0},{3,1},{4,6},{5,7},{6,4},{7,5},{8,10},{9,11},{10,... | collective-permute-start | bytes 1966088 | tf_op jit(solution)/shard_map/ppermute | solution.py:86
  327.2 34.5 %collective-permute-start.42 = (bf16[128,2560]{1,0:T(8,128)(2,1)}, bf16[128,2560]{1,0:T(8,128)(2,1)S(1)}, u32[]{:S(2)}, u32[]{:S(2)}) collective-permute-start(bf16[128,2560]{1,0:T(8,128)(2,1)} %get-tuple-element.642), channel_id=1, source_target_pairs={{0,4},{1,5},{2,6},{3,7},{4,0},{5,1},{6,2},{7,3},{8,12},{9,13},{10,... | collective-permute-start | bytes 1966088 | tf_op jit(solution)/shard_map/ppermute | solution.py:86
  361.8 47.7 %collective-permute-start.46 = (bf16[256,2560]{1,0:T(8,128)(2,1)S(1)}, bf16[256,2560]{1,0:T(8,128)(2,1)}, u32[]{:S(2)}, u32[]{:S(2)}) collective-permute-start(bf16[256,2560]{1,0:T(8,128)(2,1)S(1)} %constant_dynamic-update-slice_fusion.24.refs_6_.refs_8_), channel_id=1, source_target_pairs={{0,2},{1,3},{2,0},{3,1},{4,6},{5,7},{6,4},{7,5},{8,10},{9,11},{10,... | collective-permute-start | bytes 3932168 | tf_op jit(solution)/shard_map/ppermute | solution.py:86
  363.1 46.4 %collective-permute-start.45 = (bf16[256,2560]{1,0:T(8,128)(2,1)S(1)}, bf16[256,2560]{1,0:T(8,128)(2,1)}, u32[]{:S(2)}, u32[]{:S(2)}) collective-permute-start(bf16[256,2560]{1,0:T(8,128)(2,1)S(1)} %constant_dynamic-update-slice_fusion.22.refs_4_.refs_6_), channel_id=1, source_target_pairs={{0,4},{1,5},{2,6},{3,7},{4,0},{5,1},{6,2},{7,3},{8,12},{9,13},{10,... | collective-permute-start | bytes 3932168 | tf_op jit(solution)/shard_map/ppermute | solution.py:86
  364.8 51.9 %collective-permute-start.44 = (bf16[256,2560]{1,0:T(8,128)(2,1)S(1)}, bf16[256,2560]{1,0:T(8,128)(2,1)}, u32[]{:S(2)}, u32[]{:S(2)}) collective-permute-start(bf16[256,2560]{1,0:T(8,128)(2,1)S(1)} %constant_dynamic-update-slice_fusion.20.refs_2_.refs_8_), channel_id=1, source_target_pairs={{0,2},{1,3},{2,0},{3,1},{4,6},{5,7},{6,4},{7,5},{8,10},{9,11},{10,... | collective-permute-start | bytes 3932168 | tf_op jit(solution)/shard_map/ppermute | solution.py:86
  365.9 54.0 %collective-permute-start.43 = (bf16[256,2560]{1,0:T(8,128)(2,1)S(1)}, bf16[256,2560]{1,0:T(8,128)(2,1)}, u32[]{:S(2)}, u32[]{:S(2)}) collective-permute-start(bf16[256,2560]{1,0:T(8,128)(2,1)S(1)} %constant_dynamic-update-slice_fusion.18.refs_0_.refs_6_), channel_id=1, source_target_pairs={{0,4},{1,5},{2,6},{3,7},{4,0},{5,1},{6,2},{7,3},{8,12},{9,13},{10,... | collective-permute-start | bytes 3932168 | tf_op jit(solution)/shard_map/ppermute | solution.py:86
  419.9 39.3 %collective-permute-start.47 = (bf16[256,2560]{1,0:T(8,128)(2,1)}, bf16[256,2560]{1,0:T(8,128)(2,1)S(1)}, u32[]{:S(2)}, u32[]{:S(2)}) collective-permute-start(bf16[256,2560]{1,0:T(8,128)(2,1)} %copy-done.72), channel_id=1, source_target_pairs={{0,4},{1,5},{2,6},{3,7},{4,0},{5,1},{6,2},{7,3},{8,12},{9,13},{10,... | collective-permute-start | bytes 3932168 | tf_op jit(solution)/shard_map/ppermute | solution.py:86
  421.5 37.8 %collective-permute-start.48 = (bf16[256,2560]{1,0:T(8,128)(2,1)}, bf16[256,2560]{1,0:T(8,128)(2,1)S(1)}, u32[]{:S(2)}, u32[]{:S(2)}) collective-permute-start(bf16[256,2560]{1,0:T(8,128)(2,1)} %copy-done.71), channel_id=1, source_target_pairs={{0,2},{1,3},{2,0},{3,1},{4,6},{5,7},{6,4},{7,5},{8,10},{9,11},{10,... | collective-permute-start | bytes 3932168 | tf_op jit(solution)/shard_map/ppermute | solution.py:86
  422.4 87.1 %collective-permute-start.49 = (bf16[256,2560]{1,0:T(8,128)(2,1)}, bf16[256,2560]{1,0:T(8,128)(2,1)}, u32[]{:S(2)}, u32[]{:S(2)}) collective-permute-start(bf16[256,2560]{1,0:T(8,128)(2,1)} %get-tuple-element.692), channel_id=1, source_target_pairs={{0,4},{1,5},{2,6},{3,7},{4,0},{5,1},{6,2},{7,3},{8,12},{9,13},{10,... | collective-permute-start | bytes 3932168 | tf_op jit(solution)/shard_map/ppermute | solution.py:86
  422.8 86.8 %collective-permute-start.50 = (bf16[256,2560]{1,0:T(8,128)(2,1)}, bf16[256,2560]{1,0:T(8,128)(2,1)}, u32[]{:S(2)}, u32[]{:S(2)}) collective-permute-start(bf16[256,2560]{1,0:T(8,128)(2,1)} %get-tuple-element.693), channel_id=1, source_target_pairs={{0,2},{1,3},{2,0},{3,1},{4,6},{5,7},{6,4},{7,5},{8,10},{9,11},{10,... | collective-permute-start | bytes 3932168 | tf_op jit(solution)/shard_map/ppermute | solution.py:86
  463.1 46.5 %collective-permute-start.52 = (bf16[128,2560]{1,0:T(8,128)(2,1)}, bf16[128,2560]{1,0:T(8,128)(2,1)S(1)}, u32[]{:S(2)}, u32[]{:S(2)}) collective-permute-start(bf16[128,2560]{1,0:T(8,128)(2,1)} %get-tuple-element.1106), channel_id=1, source_target_pairs={{0,4},{1,5},{2,6},{3,7},{4,0},{5,1},{6,2},{7,3},{8,12},{9,13},{10,... | collective-permute-start | bytes 1966088 | tf_op jit(solution)/shard_map/ppermute | solution.py:86
  465.9 43.7 %collective-permute-start.51 = (bf16[128,2560]{1,0:T(8,128)(2,1)}, bf16[128,2560]{1,0:T(8,128)(2,1)}, u32[]{:S(2)}, u32[]{:S(2)}) collective-permute-start(bf16[128,2560]{1,0:T(8,128)(2,1)} %get-tuple-element.1108), channel_id=1, source_target_pairs={{0,2},{1,3},{2,0},{3,1},{4,6},{5,7},{6,4},{7,5},{8,10},{9,11},{10,... | collective-permute-start | bytes 1966088 | tf_op jit(solution)/shard_map/ppermute | solution.py:86
  514.0 44.2 %collective-permute-start.60 = (bf16[400,2560]{1,0:T(8,128)(2,1)}, bf16[400,2560]{1,0:T(8,128)(2,1)}, u32[]{:S(2)}, u32[]{:S(2)}) collective-permute-start(bf16[400,2560]{1,0:T(8,128)(2,1)} %get-tuple-element.728), channel_id=1, source_target_pairs={{0,1},{1,0},{2,3},{3,2},{4,5},{5,4},{6,7},{7,6},{8,9},{9,8},{10,11... | collective-permute-start | bytes 6144008 | tf_op jit(solution)/shard_map/ppermute | solution.py:86
  514.0 45.0 %collective-permute-start.61 = (bf16[400,2560]{1,0:T(8,128)(2,1)S(1)}, bf16[400,2560]{1,0:T(8,128)(2,1)}, u32[]{:S(2)}, u32[]{:S(2)}) collective-permute-start(bf16[400,2560]{1,0:T(8,128)(2,1)S(1)} %copy-done.64), channel_id=1, source_target_pairs={{0,1},{1,0},{2,3},{3,2},{4,5},{5,4},{6,7},{7,6},{8,9},{9,8},{10,11... | collective-permute-start | bytes 6144008 | tf_op jit(solution)/shard_map/ppermute | solution.py:86
  533.3 40.9 %collective-permute-start.58 = (bf16[400,2560]{1,0:T(8,128)(2,1)}, bf16[400,2560]{1,0:T(8,128)(2,1)}, u32[]{:S(2)}, u32[]{:S(2)}) collective-permute-start(bf16[400,2560]{1,0:T(8,128)(2,1)} %get-tuple-element.724), channel_id=1, source_target_pairs={{0,1},{1,0},{2,3},{3,2},{4,5},{5,4},{6,7},{7,6},{8,9},{9,8},{10,11... | collective-permute-start | bytes 6144008 | tf_op jit(solution)/shard_map/ppermute | solution.py:86
  533.4 40.9 %collective-permute-start.59 = (bf16[400,2560]{1,0:T(8,128)(2,1)}, bf16[400,2560]{1,0:T(8,128)(2,1)}, u32[]{:S(2)}, u32[]{:S(2)}) collective-permute-start(bf16[400,2560]{1,0:T(8,128)(2,1)} %get-tuple-element.725), channel_id=1, source_target_pairs={{0,1},{1,0},{2,3},{3,2},{4,5},{5,4},{6,7},{7,6},{8,9},{9,8},{10,11... | collective-permute-start | bytes 6144008 | tf_op jit(solution)/shard_map/ppermute | solution.py:86
  549.6 69.0 %collective-permute-start.57 = (bf16[400,2560]{1,0:T(8,128)(2,1)}, bf16[400,2560]{1,0:T(8,128)(2,1)}, u32[]{:S(2)}, u32[]{:S(2)}) collective-permute-start(bf16[400,2560]{1,0:T(8,128)(2,1)} %get-tuple-element.722), channel_id=1, source_target_pairs={{0,8},{24,16},{1,9},{25,17},{2,10},{26,18},{3,11},{27,19},{4,12},{... | collective-permute-start | bytes 6144008 | tf_op jit(solution)/shard_map/ppermute | solution.py:432
  558.2 60.4 %collective-permute-start.62 = (bf16[256,2560]{1,0:T(8,128)(2,1)}, bf16[256,2560]{1,0:T(8,128)(2,1)}, u32[]{:S(2)}, u32[]{:S(2)}) collective-permute-start(bf16[256,2560]{1,0:T(8,128)(2,1)} %get-tuple-element.740), channel_id=1, source_target_pairs={{0,4},{1,5},{2,6},{3,7},{4,0},{5,1},{6,2},{7,3},{8,12},{9,13},{10,... | collective-permute-start | bytes 3932168 | tf_op jit(solution)/shard_map/ppermute | solution.py:86
  559.0 59.6 %collective-permute-start.63 = (bf16[256,2560]{1,0:T(8,128)(2,1)}, bf16[256,2560]{1,0:T(8,128)(2,1)}, u32[]{:S(2)}, u32[]{:S(2)}) collective-permute-start(bf16[256,2560]{1,0:T(8,128)(2,1)} %get-tuple-element.741), channel_id=1, source_target_pairs={{0,2},{1,3},{2,0},{3,1},{4,6},{5,7},{6,4},{7,5},{8,10},{9,11},{10,... | collective-permute-start | bytes 3932168 | tf_op jit(solution)/shard_map/ppermute | solution.py:86
  627.8 45.0 %collective-permute-start.64 = (bf16[400,2560]{1,0:T(8,128)(2,1)S(1)}, bf16[400,2560]{1,0:T(8,128)(2,1)}, u32[]{:S(2)}, u32[]{:S(2)}) collective-permute-start(bf16[400,2560]{1,0:T(8,128)(2,1)S(1)} %copy-done.13), channel_id=1, source_target_pairs={{0,8},{24,16},{1,9},{25,17},{2,10},{26,18},{3,11},{27,19},{4,12},{... | collective-permute-start | bytes 6144008 | tf_op jit(solution)/shard_map/ppermute | solution.py:432
  630.4 42.4 %collective-permute-start.65 = (bf16[400,2560]{1,0:T(8,128)(2,1)}, bf16[400,2560]{1,0:T(8,128)(2,1)}, u32[]{:S(2)}, u32[]{:S(2)}) collective-permute-start(bf16[400,2560]{1,0:T(8,128)(2,1)} %add_convert_fusion.11), channel_id=1, source_target_pairs={{8,16},{16,8},{9,17},{17,9},{10,18},{18,10},{11,19},{19,11},{12,20... | collective-permute-start | bytes 6144008 | tf_op jit(solution)/shard_map/ppermute | solution.py:432
  632.4 32.0 %collective-permute-start.66 = (bf16[256,2560]{1,0:T(8,128)(2,1)}, bf16[256,2560]{1,0:T(8,128)(2,1)}, u32[]{:S(2)}, u32[]{:S(2)}) collective-permute-start(bf16[256,2560]{1,0:T(8,128)(2,1)} %get-tuple-element.764), channel_id=1, source_target_pairs={{0,4},{1,5},{2,6},{3,7},{4,0},{5,1},{6,2},{7,3},{8,12},{9,13},{10,... | collective-permute-start | bytes 3932168 | tf_op jit(solution)/shard_map/ppermute | solution.py:86
  633.7 30.7 %collective-permute-start.67 = (bf16[256,2560]{1,0:T(8,128)(2,1)S(1)}, bf16[256,2560]{1,0:T(8,128)(2,1)}, u32[]{:S(2)}, u32[]{:S(2)}) collective-permute-start(bf16[256,2560]{1,0:T(8,128)(2,1)S(1)} %get-tuple-element.765), channel_id=1, source_target_pairs={{0,2},{1,3},{2,0},{3,1},{4,6},{5,7},{6,4},{7,5},{8,10},{9,11},{10,... | collective-permute-start | bytes 3932168 | tf_op jit(solution)/shard_map/ppermute | solution.py:86
  637.6 115.8 %collective-permute-start.73 = (bf16[128,2560]{1,0:T(8,128)(2,1)}, bf16[128,2560]{1,0:T(8,128)(2,1)}, u32[]{:S(2)}, u32[]{:S(2)}) collective-permute-start(bf16[128,2560]{1,0:T(8,128)(2,1)} %get-tuple-element.1094), channel_id=1, source_target_pairs={{0,4},{1,5},{2,6},{3,7},{4,0},{5,1},{6,2},{7,3},{8,12},{9,13},{10,... | collective-permute-start | bytes 1966088 | tf_op jit(solution)/shard_map/ppermute | solution.py:86
  683.3 61.9 %collective-permute-start.71 = (bf16[128,2560]{1,0:T(8,128)(2,1)}, bf16[128,2560]{1,0:T(8,128)(2,1)}, u32[]{:S(2)}, u32[]{:S(2)}) collective-permute-start(bf16[128,2560]{1,0:T(8,128)(2,1)} %get-tuple-element.1098), channel_id=1, source_target_pairs={{0,4},{1,5},{2,6},{3,7},{4,0},{5,1},{6,2},{7,3},{8,12},{9,13},{10,... | collective-permute-start | bytes 1966088 | tf_op jit(solution)/shard_map/ppermute | solution.py:86
  687.4 58.8 %collective-permute-start.70 = (bf16[128,2560]{1,0:T(8,128)(2,1)}, bf16[128,2560]{1,0:T(8,128)(2,1)}, u32[]{:S(2)}, u32[]{:S(2)}) collective-permute-start(bf16[128,2560]{1,0:T(8,128)(2,1)} %get-tuple-element.1100), channel_id=1, source_target_pairs={{0,2},{1,3},{2,0},{3,1},{4,6},{5,7},{6,4},{7,5},{8,10},{9,11},{10,... | collective-permute-start | bytes 1966088 | tf_op jit(solution)/shard_map/ppermute | solution.py:86
  688.4 57.8 %collective-permute-start.68 = (bf16[400,2560]{1,0:T(8,128)(2,1)}, bf16[400,2560]{1,0:T(8,128)(2,1)}, u32[]{:S(2)}, u32[]{:S(2)}) collective-permute-start(bf16[400,2560]{1,0:T(8,128)(2,1)} %broadcast_select_fusion.9), channel_id=1, source_target_pairs={{0,8},{24,16},{8,0},{16,24},{1,9},{25,17},{9,1},{17,25},{2,10},{26... | collective-permute-start | bytes 6144008 | tf_op jit(solution)/shard_map/ppermute | solution.py:432
  691.3 54.9 %collective-permute-start.69 = (bf16[400,2560]{1,0:T(8,128)(2,1)}, bf16[400,2560]{1,0:T(8,128)(2,1)}, u32[]{:S(2)}, u32[]{:S(2)}) collective-permute-start(bf16[400,2560]{1,0:T(8,128)(2,1)} %add_convert_fusion.10), channel_id=1, source_target_pairs={{8,16},{16,8},{9,17},{17,9},{10,18},{18,10},{11,19},{19,11},{12,20... | collective-permute-start | bytes 6144008 | tf_op jit(solution)/shard_map/ppermute | solution.py:432
  784.3 43.7 %collective-permute-start.74 = (bf16[400,2560]{1,0:T(8,128)(2,1)}, bf16[400,2560]{1,0:T(8,128)(2,1)S(1)}, u32[]{:S(2)}, u32[]{:S(2)}) collective-permute-start(bf16[400,2560]{1,0:T(8,128)(2,1)} %broadcast_select_fusion.8), channel_id=1, source_target_pairs={{0,8},{24,16},{8,0},{16,24},{1,9},{25,17},{9,1},{17,25},{2,10},{26... | collective-permute-start | bytes 6144008 | tf_op jit(solution)/shard_map/ppermute | solution.py:432
  784.9 43.1 %collective-permute-start.75 = (bf16[400,2560]{1,0:T(8,128)(2,1)S(1)}, bf16[400,2560]{1,0:T(8,128)(2,1)S(1)}, u32[]{:S(2)}, u32[]{:S(2)}) collective-permute-start(bf16[400,2560]{1,0:T(8,128)(2,1)S(1)} %add_convert_fusion.7), channel_id=1, source_target_pairs={{8,16},{16,8},{9,17},{17,9},{10,18},{18,10},{11,19},{19,11},{12,20... | collective-permute-start | bytes 6144008 | tf_op jit(solution)/shard_map/ppermute | solution.py:432
  845.9 76.1 %collective-permute-start.78 = (bf16[4,1,160,2560]{3,2,0,1:T(8,128)(2,1)}, bf16[4,1,160,2560]{3,2,0,1:T(8,128)(2,1)}, u32[]{:S(2)}, u32[]{:S(2)}) collective-permute-start(bf16[4,1,160,2560]{3,2,0,1:T(8,128)(2,1)} %dynamic-slice_bitcast_fusion.1), channel_id=1, source_target_pairs={{0,1},{1,0},{2,3},{3,2},{4,5},{5,4},{6,7},{7,6},{8,9},{9,8},{10,11... | collective-permute-start | bytes 9830408 | tf_op jit(solution)/shard_map/ppermute | solution.py:86
  845.9 76.1 %collective-permute-start.79 = (bf16[4,1,160,2560]{3,2,0,1:T(8,128)(2,1)}, bf16[4,1,160,2560]{3,2,0,1:T(8,128)(2,1)}, u32[]{:S(2)}, u32[]{:S(2)}) collective-permute-start(bf16[4,1,160,2560]{3,2,0,1:T(8,128)(2,1)} %dynamic-slice_bitcast_fusion), channel_id=1, source_target_pairs={{0,1},{1,0},{2,3},{3,2},{4,5},{5,4},{6,7},{7,6},{8,9},{9,8},{10,11... | collective-permute-start | bytes 9830408 | tf_op jit(solution)/shard_map/ppermute | solution.py:86
  846.4 75.6 %collective-permute-start.76 = (bf16[400,2560]{1,0:T(8,128)(2,1)}, bf16[400,2560]{1,0:T(8,128)(2,1)}, u32[]{:S(2)}, u32[]{:S(2)}) collective-permute-start(bf16[400,2560]{1,0:T(8,128)(2,1)} %broadcast_select_fusion.7), channel_id=1, source_target_pairs={{0,8},{24,16},{8,0},{16,24},{1,9},{25,17},{9,1},{17,25},{2,10},{26... | collective-permute-start | bytes 6144008 | tf_op jit(solution)/shard_map/ppermute | solution.py:432
  849.1 72.9 %collective-permute-start.77 = (bf16[400,2560]{1,0:T(8,128)(2,1)}, bf16[400,2560]{1,0:T(8,128)(2,1)}, u32[]{:S(2)}, u32[]{:S(2)}) collective-permute-start(bf16[400,2560]{1,0:T(8,128)(2,1)} %add_convert_fusion.5), channel_id=1, source_target_pairs={{8,16},{16,8},{9,17},{17,9},{10,18},{18,10},{11,19},{19,11},{12,20... | collective-permute-start | bytes 6144008 | tf_op jit(solution)/shard_map/ppermute | solution.py:432
  851.1 134.0 %reduce-scatter.5.cloned.1.call-start = ((), (), s32[]{:S(2)}) async-start(), calls=%async_computation.4 | async-start | bytes 983040 | tf_op jit(solution)/shard_map/reduce_scatter | solution.py:918
  945.5 59.2 %collective-permute-start.80 = (bf16[400,2560]{1,0:T(8,128)(2,1)}, bf16[400,2560]{1,0:T(8,128)(2,1)}, u32[]{:S(2)}, u32[]{:S(2)}) collective-permute-start(bf16[400,2560]{1,0:T(8,128)(2,1)} %broadcast_select_fusion.6), channel_id=1, source_target_pairs={{0,8},{24,16},{8,0},{16,24},{1,9},{25,17},{9,1},{17,25},{2,10},{26... | collective-permute-start | bytes 6144008 | tf_op jit(solution)/shard_map/ppermute | solution.py:432
  946.3 58.3 %collective-permute-start.81 = (bf16[400,2560]{1,0:T(8,128)(2,1)}, bf16[400,2560]{1,0:T(8,128)(2,1)}, u32[]{:S(2)}, u32[]{:S(2)}) collective-permute-start(bf16[400,2560]{1,0:T(8,128)(2,1)} %add_convert_fusion.4), channel_id=1, source_target_pairs={{8,16},{16,8},{9,17},{17,9},{10,18},{18,10},{11,19},{19,11},{12,20... | collective-permute-start | bytes 6144008 | tf_op jit(solution)/shard_map/ppermute | solution.py:432
  948.5 37.6 %collective-permute-start.82 = (bf16[1,2,160,2560]{3,2,1,0:T(8,128)(2,1)}, bf16[1,2,160,2560]{3,2,1,0:T(8,128)(2,1)}, u32[]{:S(2)}, u32[]{:S(2)}) collective-permute-start(bf16[1,2,160,2560]{3,2,1,0:T(8,128)(2,1)} %dynamic-slice_bitcast_fusion.5), channel_id=1, source_target_pairs={{0,4},{1,5},{2,6},{3,7},{4,0},{5,1},{6,2},{7,3},{8,12},{9,13},{10,... | collective-permute-start | bytes 4915208 | tf_op jit(solution)/shard_map/ppermute | solution.py:86
  949.4 37.1 %collective-permute-start.83 = (bf16[2,1,160,2560]{3,2,0,1:T(8,128)(2,1)}, bf16[2,1,160,2560]{3,2,0,1:T(8,128)(2,1)}, u32[]{:S(2)}, u32[]{:S(2)}) collective-permute-start(bf16[2,1,160,2560]{3,2,0,1:T(8,128)(2,1)} %dynamic-slice_bitcast_fusion.4), channel_id=1, source_target_pairs={{0,2},{1,3},{2,0},{3,1},{4,6},{5,7},{6,4},{7,5},{8,10},{9,11},{10,... | collective-permute-start | bytes 4915208 | tf_op jit(solution)/shard_map/ppermute | solution.py:86
  1028.5 50.5 %collective-permute-start.88 = (bf16[4,1,96,3840]{3,2,0,1:T(8,128)(2,1)}, bf16[4,1,96,3840]{3,2,0,1:T(8,128)(2,1)}, u32[]{:S(2)}, u32[]{:S(2)}) collective-permute-start(bf16[4,1,96,3840]{3,2,0,1:T(8,128)(2,1)} %dynamic-slice_bitcast_fusion.2), channel_id=1, source_target_pairs={{0,1},{1,0},{2,3},{3,2},{4,5},{5,4},{6,7},{7,6},{8,9},{9,8},{10,11... | collective-permute-start | bytes 8847368 | tf_op jit(solution)/shard_map/ppermute | solution.py:86
  1028.5 50.5 %collective-permute-start.84 = (bf16[400,2560]{1,0:T(8,128)(2,1)}, bf16[400,2560]{1,0:T(8,128)(2,1)}, u32[]{:S(2)}, u32[]{:S(2)}) collective-permute-start(bf16[400,2560]{1,0:T(8,128)(2,1)} %add_convert_fusion.2), channel_id=1, source_target_pairs={{8,0},{16,24},{9,1},{17,25},{10,2},{18,26},{11,3},{19,27},{12,4},{... | collective-permute-start | bytes 6144008 | tf_op jit(solution)/shard_map/ppermute | solution.py:432
  1029.8 49.2 %collective-permute-start.85 = (bf16[400,2560]{1,0:T(8,128)(2,1)}, bf16[400,2560]{1,0:T(8,128)(2,1)}, u32[]{:S(2)}, u32[]{:S(2)}) collective-permute-start(bf16[400,2560]{1,0:T(8,128)(2,1)} %add_convert_fusion.1), channel_id=1, source_target_pairs={{8,16},{16,8},{9,17},{17,9},{10,18},{18,10},{11,19},{19,11},{12,20... | collective-permute-start | bytes 6144008 | tf_op jit(solution)/shard_map/ppermute | solution.py:432
  1098.3 48.7 %collective-permute-start.92 = (bf16[400,2560]{1,0:T(8,128)(2,1)S(1)}, bf16[400,2560]{1,0:T(8,128)(2,1)S(1)}, u32[]{:S(2)}, u32[]{:S(2)}) collective-permute-start(bf16[400,2560]{1,0:T(8,128)(2,1)S(1)} %add_convert_fusion), channel_id=1, source_target_pairs={{8,0},{16,24},{9,1},{17,25},{10,2},{18,26},{11,3},{19,27},{12,4},{... | collective-permute-start | bytes 6144008 | tf_op jit(solution)/shard_map/ppermute | solution.py:432
  1099.6 40.2 %collective-permute-start.91 = (bf16[320,2560]{1,0:T(8,128)(2,1)}, bf16[320,2560]{1,0:T(8,128)(2,1)S(1)}, u32[]{:S(2)}, u32[]{:S(2)}) collective-permute-start(bf16[320,2560]{1,0:T(8,128)(2,1)} %pad_maximum_fusion.7), channel_id=1, source_target_pairs={{0,8},{24,16},{1,9},{25,17},{2,10},{26,18},{3,11},{27,19},{4,12},{... | collective-permute-start | bytes 4915208 | tf_op jit(solution)/shard_map/ppermute | solution.py:432
  1105.0 34.0 %collective-permute-start.93 = (bf16[2,1,96,3840]{3,2,0,1:T(8,128)(2,1)}, bf16[2,1,96,3840]{3,2,0,1:T(8,128)(2,1)}, u32[]{:S(2)}, u32[]{:S(2)}) collective-permute-start(bf16[2,1,96,3840]{3,2,0,1:T(8,128)(2,1)} %dynamic-slice_bitcast_fusion.6), channel_id=1, source_target_pairs={{0,2},{1,3},{2,0},{3,1},{4,6},{5,7},{6,4},{7,5},{8,10},{9,11},{10,... | collective-permute-start | bytes 4423688 | tf_op jit(solution)/shard_map/ppermute | solution.py:86
  1152.5 37.1 %collective-permute-start.97 = (bf16[320,2560]{1,0:T(8,128)(2,1)S(1)}, bf16[320,2560]{1,0:T(8,128)(2,1)S(1)}, u32[]{:S(2)}, u32[]{:S(2)}) collective-permute-start(bf16[320,2560]{1,0:T(8,128)(2,1)S(1)} %add_convert_fusion.13), channel_id=1, source_target_pairs={{8,16},{16,8},{9,17},{17,9},{10,18},{18,10},{11,19},{19,11},{12,20... | collective-permute-start | bytes 4915208 | tf_op jit(solution)/shard_map/ppermute | solution.py:432
  1159.5 30.2 %collective-permute-start.98 = (bf16[1,1,96,3840]{3,2,0,1:T(8,128)(2,1)S(1)}, bf16[1,1,96,3840]{3,2,0,1:T(8,128)(2,1)S(1)}, u32[]{:S(2)}, u32[]{:S(2)}) collective-permute-start(bf16[1,1,96,3840]{3,2,0,1:T(8,128)(2,1)S(1)} %constant_dynamic-slice_fusion.3), channel_id=1, source_target_pairs={{0,4},{1,5},{2,6},{3,7},{4,0},{5,1},{6,2},{7,3},{8,12},{9,13},{10,... | collective-permute-start | bytes 2211848 | tf_op jit(solution)/shard_map/ppermute | solution.py:86
  1190.4 37.4 %collective-permute-start.103 = (bf16[320,2560]{1,0:T(8,128)(2,1)S(1)}, bf16[320,2560]{1,0:T(8,128)(2,1)S(1)}, u32[]{:S(2)}, u32[]{:S(2)}) collective-permute-start(bf16[320,2560]{1,0:T(8,128)(2,1)S(1)} %add_convert_fusion.12), channel_id=1, source_target_pairs={{8,0},{16,24},{9,1},{17,25},{10,2},{18,26},{11,3},{19,27},{12,4},{... | collective-permute-start | bytes 4915208 | tf_op jit(solution)/shard_map/ppermute | solution.py:432
  (279 other events, 2897.8 us)
Sparse Core Ops, SparseCore 0:
  109.5 33.3 all-gather.1
  851.2 33.3 reduce-scatter.2
  950.5 34.5 reduce-scatter.4
